TPU v7x, 32 devices: a whole 2x2x4 slice. The times are simulated.
32 devices in a mesh: freq: 4 (over z), row: 4 (over y, core), col: 2 (over x).
Axes of the slice: x: 2, y: 2, z: 4, core: 2. Of those that a mesh axis runs over, the one named last changes fastest.
Arguments:
- b_pairs: bfloat16 [6144, 2048], P(('row', 'col'), 'freq'), may hold values from -2 to 2
- occ_index: int32 [2048], P('freq'), may hold values from 0 to 255
- vir_index: int32 [2048], P('freq'), may hold values from 0 to 1791
- occ_depth: float32 [256], replicated, may hold values from 0.2 to 20
- vir_height: float32 [1792], replicated, may hold values from 0.05 to 30
- omega: float32 [4], P('freq'), may hold values from 0.05 to 50
Outputs:
- polar: float32 [4, 4, 2, 768, 6144], P('freq', None, 'col', None, 'row')
Inputs may be any that keep to these rules, and one draw needn't show every extreme that they name: `occ_index`: an occupied orbital number. `vir_index`: a virtual orbital number.
All inputs are finite; a program needn't handle non-finite values.
Results may differ from a plain program's by a relative error of at most 0.0027.
Values may be sent and summed in bfloat16 or wider, within the bound.
No kernel may reach another device: no remote copies, remote signals or barrier semaphores. Data moves between devices by JAX's collectives and lax.ppermute only.
A program may use at most 128 MiB of HBM per device.

v0:
```python
import jax
import jax.numpy as jnp
from jax import lax
from jax.sharding import PartitionSpec as P

STEPS = 4


def from_behind(value, axis, by):
    peers = lax.axis_size(axis)
    return lax.ppermute(value, axis, [(i, (i + by) % peers) for i in range(peers)])


def contract_pairs(left, right):
    return lax.dot_general(
        left, right, (((1,), (1,)), ((), ())), preferred_element_type=jnp.float32
    )


def per_device(b_pairs, occ_index, vir_index, occ_depth, vir_height, omega):
    square = omega[0] * omega[0]
    n_row = lax.axis_size("row")
    n_col = lax.axis_size("col")
    sub_width = b_pairs.shape[0]
    total = jnp.zeros((sub_width * n_row, sub_width * n_col), jnp.float32)
    left = lax.all_gather(b_pairs, "col", axis=0, tiled=True)
    right = lax.all_gather(b_pairs, "row", axis=0, tiled=True)
    occ_part = occ_index
    vir_part = vir_index
    for step in range(STEPS):
        gap = jnp.take(vir_height, vir_part) + jnp.take(occ_depth, occ_part)
        weight = 4.0 * gap / (gap * gap + square)
        total = total + contract_pairs(
            right, (left.astype(jnp.float32) * weight[None, :]).astype(jnp.bfloat16)
        )
        if step + 1 < STEPS:
            left, right, occ_part, vir_part = from_behind(
                (left, right, occ_part, vir_part), "freq", 1
            )
    return total.reshape(1, n_row, 1, sub_width, sub_width * n_col)


def solution(mesh):
    in_specs = (P(("row", "col"), "freq"), P("freq"), P("freq"), P(), P(), P("freq"))
    out_specs = P("freq", None, "col", None, "row")
    return jax.shard_map(
        per_device, mesh=mesh, in_specs=in_specs, out_specs=out_specs, check_vma=False
    )
```

profile of v0, /device:TPU:0, one launch (start us, length us, event | category | flops | bytes accessed | tf_op | source)
XLA Modules:
  0.0 413.8 jit_solution(15349299394847395587)
XLA Ops:
  8.2 32.9 %all-gather.5.cloned.1.call-done = bf16[3072,512]{1,0:T(8,128)(2,1)} async-done(((bf16[768,512]{1,0:T(8,128)(2,1)}), bf16[3072,512]{1,0:T(8,128)(2,1)}) %all-gather.5.cloned.1.call-update) | async-done | bytes 3145744 | tf_op jit(solution)/shard_map/all_gather | solution.py:27
  42.5 1.5 collective-permute-start.2
  44.1 1.5 collective-permute-start.1
  45.6 23.2 %all-gather.3.cloned.1.call-done = bf16[1536,512]{1,0:T(8,128)(2,1)} async-done(((bf16[768,512]{1,0:T(8,128)(2,1)}), bf16[1536,512]{1,0:T(8,128)(2,1)}) %all-gather.3.cloned.1.call-update) | async-done | bytes 1572880 | tf_op jit(solution)/shard_map/all_gather | solution.py:26
  68.8 1.5 collective-permute-start
  71.6 3.6 gather_fusion.1
  75.2 38.8 %collective-permute-done.3 = bf16[3072,512]{1,0:T(8,128)(2,1)} collective-permute-done((bf16[3072,512]{1,0:T(8,128)(2,1)}, bf16[3072,512]{1,0:T(8,128)(2,1)}, u32[]{:S(2)}, u32[]{:S(2)}) %collective-permute-start.3) | collective-permute-done | bytes 3145760 | tf_op jit(solution)/shard_map/ppermute | solution.py:11
  114.1 3.1 gather_fusion
  117.3 3.5 gather_fusion.3
  120.9 3.1 gather_fusion.2
  126.7 21.1 %collective-permute-done = bf16[1536,512]{1,0:T(8,128)(2,1)} collective-permute-done((bf16[1536,512]{1,0:T(8,128)(2,1)}, bf16[1536,512]{1,0:T(8,128)(2,1)}, u32[]{:S(2)}, u32[]{:S(2)}) %collective-permute-start) | collective-permute-done | bytes 1572896 | tf_op jit(solution)/shard_map/ppermute | solution.py:11
  147.9 67.4 %collective-permute-done.6 = s32[512]{0:T(512)S(1)} collective-permute-done((s32[512]{0:T(512)S(1)}, s32[512]{0:T(512)S(1)}, u32[]{:S(2)}, u32[]{:S(2)}) %collective-permute-start.6) | collective-permute-done | bytes 2080 | tf_op jit(solution)/shard_map/ppermute | solution.py:11
  215.3 3.5 gather_fusion.5
  218.8 3.1 gather_fusion.4
  223.2 25.2 %collective-permute-done.10 = s32[512]{0:T(512)S(1)} collective-permute-done((s32[512]{0:T(512)S(1)}, s32[512]{0:T(512)S(1)}, u32[]{:S(2)}, u32[]{:S(2)}) %collective-permute-start.10) | collective-permute-done | bytes 2080 | tf_op jit(solution)/shard_map/ppermute | solution.py:11
  248.5 3.5 gather_fusion.7
  252.0 3.1 gather_fusion.6
  256.4 11.0 %fusion = f32[1536,3072]{1,0:T(8,128)} fusion(bf16[3072,512]{1,0:T(8,128)(2,1)} %all-gather.5.cloned.1.call-done, bf16[1536,512]{1,0:T(8,128)(2,1)S(1)} %copy-done.5, f32[512]{0:T(512)S(1)} %add_divide_fusion.3), kind=kOutput, calls=%fused_computation.13 | convolution fusion | flops 4834197504 | bytes 23595008 | tf_op jit(solution)/shard_map/dot_general | solution.py:15
  267.4 11.0 %fusion.1 = f32[1536,3072]{1,0:T(8,128)} fusion(bf16[3072,512]{1,0:T(8,128)(2,1)} %collective-permute-done.3, bf16[1536,512]{1,0:T(8,128)(2,1)} %collective-permute-done, f32[512]{0:T(512)S(1)} %add_divide_fusion.2), kind=kOutput, calls=%fused_computation.14 | convolution fusion | flops 4834197504 | bytes 23595008 | tf_op jit(solution)/shard_map/dot_general | solution.py:15
  278.4 11.4 %fusion.2 = f32[1536,3072]{1,0:T(8,128)} fusion(bf16[3072,512]{1,0:T(8,128)(2,1)} %collective-permute-done.7, bf16[1536,512]{1,0:T(8,128)(2,1)} %collective-permute-done.4, f32[512]{0:T(512)S(1)} %add_divide_fusion.1), kind=kOutput, calls=%fused_computation.15 | convolution fusion | flops 4834197504 | bytes 23595008 | tf_op jit(solution)/shard_map/dot_general | solution.py:15
  289.8 4.7 %collective-permute-done.8 = bf16[1536,512]{1,0:T(8,128)(2,1)S(1)} collective-permute-done((bf16[1536,512]{1,0:T(8,128)(2,1)}, bf16[1536,512]{1,0:T(8,128)(2,1)S(1)}, u32[]{:S(2)}, u32[]{:S(2)}) %collective-permute-start.8) | collective-permute-done | bytes 1572896 | tf_op jit(solution)/shard_map/ppermute | solution.py:11
  294.6 65.9 %collective-permute-done.11 = bf16[3072,512]{1,0:T(8,128)(2,1)} collective-permute-done((bf16[3072,512]{1,0:T(8,128)(2,1)}, bf16[3072,512]{1,0:T(8,128)(2,1)}, u32[]{:S(2)}, u32[]{:S(2)}) %collective-permute-start.11) | collective-permute-done | bytes 3145760 | tf_op jit(solution)/shard_map/ppermute | solution.py:11
  360.5 27.3 %add_bitcast_fusion = f32[3072,1536]{0,1:T(8,128)} fusion(f32[1536,3072]{1,0:T(8,128)} %fusion.2, f32[1536,3072]{1,0:T(8,128)} %fusion, f32[1536,3072]{1,0:T(8,128)} %fusion.1, bf16[3072,512]{1,0:T(8,128)(2,1)} %collective-permute-done.11, bf16[1536,512]{1,0:T(8,128)(2,1)S(1)} %collective-permute-done.8, f32[512]{0:T(512)S(1)} %add_divide_fusion), kind=kOutput, calls=%fused_computation.8 | convolution fusion | flops 4848353280 | bytes 80218112 | tf_op jit(solution)/shard_map/dot_general | solution.py:15
  387.7 18.6 %copy.9 = f32[3072,1536]{1,0:T(8,128)} copy(f32[3072,1536]{0,1:T(8,128)} %add_bitcast_fusion) | data formatting | bytes 37748736 | tf_op jit(solution)/shard_map/reshape | solution.py:40
  (51 shorter events, 8.2 us)
Async XLA Ops:
  7.4 106.7 %copy-start = (f32[1792]{0:T(1024)S(1)}, f32[1792]{0:T(1024)}, u32[]{:S(2)}) copy-start(f32[1792]{0:T(1024)} %param.14) | copy-start | bytes 21508
  7.4 109.9 %copy-start.3 = (s32[512]{0:T(512)S(1)}, s32[512]{0:T(512)}, u32[]{:S(2)}) copy-start(s32[512]{0:T(512)} %param.11) | copy-start | bytes 6148
  7.4 106.7 %copy-start.4 = (s32[512]{0:T(512)S(1)}, s32[512]{0:T(512)}, u32[]{:S(2)}) copy-start(s32[512]{0:T(512)} %param.12) | copy-start | bytes 6148
  7.4 110.0 %copy-start.2 = (f32[256]{0:T(256)S(1)}, f32[256]{0:T(256)}, u32[]{:S(2)}) copy-start(f32[256]{0:T(256)} %param.13) | copy-start | bytes 3076
  7.4 33.7 %all-gather.5.cloned.1.call-start = ((), (), s32[]{:S(2)}) async-start(), calls=%async_computation.1 | async-start | bytes 3932160 | tf_op jit(solution)/shard_map/all_gather | solution.py:27
  8.1 60.7 %all-gather.3.cloned.1.call-start = ((), (), s32[]{:S(2)}) async-start(), calls=%async_computation | async-start | bytes 2359296 | tf_op jit(solution)/shard_map/all_gather | solution.py:26
  41.0 73.0 %collective-permute-start.3 = (bf16[3072,512]{1,0:T(8,128)(2,1)}, bf16[3072,512]{1,0:T(8,128)(2,1)}, u32[]{:S(2)}, u32[]{:S(2)}) collective-permute-start(bf16[3072,512]{1,0:T(8,128)(2,1)} %all-gather.5.cloned.1.call-done), channel_id=1, source_target_pairs={{0,8},{8,16},{16,24},{24,0},{1,9},{9,17},{17,25},{25,1},{2,10},{10... | collective-permute-start | bytes 9437192 | tf_op jit(solution)/shard_map/ppermute | solution.py:11
  42.5 74.8 %collective-permute-start.2 = (s32[512]{0:T(512)}, s32[512]{0:T(512)S(1)}, u32[]{:S(2)}, u32[]{:S(2)}) collective-permute-start(s32[512]{0:T(512)} %param.11), channel_id=1, source_target_pairs={{0,8},{8,16},{16,24},{24,0},{1,9},{9,17},{17,25},{25,1},{2,10},{10... | collective-permute-start | bytes 6152 | tf_op jit(solution)/shard_map/ppermute | solution.py:11
  44.1 76.8 %collective-permute-start.1 = (s32[512]{0:T(512)}, s32[512]{0:T(512)S(1)}, u32[]{:S(2)}, u32[]{:S(2)}) collective-permute-start(s32[512]{0:T(512)} %param.12), channel_id=1, source_target_pairs={{0,8},{8,16},{16,24},{24,0},{1,9},{9,17},{17,25},{25,1},{2,10},{10... | collective-permute-start | bytes 6152 | tf_op jit(solution)/shard_map/ppermute | solution.py:11
  68.8 79.1 %collective-permute-start = (bf16[1536,512]{1,0:T(8,128)(2,1)}, bf16[1536,512]{1,0:T(8,128)(2,1)}, u32[]{:S(2)}, u32[]{:S(2)}) collective-permute-start(bf16[1536,512]{1,0:T(8,128)(2,1)} %all-gather.3.cloned.1.call-done), channel_id=1, source_target_pairs={{0,8},{8,16},{16,24},{24,0},{1,9},{9,17},{17,25},{25,1},{2,10},{10... | collective-permute-start | bytes 4718600 | tf_op jit(solution)/shard_map/ppermute | solution.py:11
  114.1 141.2 %collective-permute-start.7 = (bf16[3072,512]{1,0:T(8,128)(2,1)}, bf16[3072,512]{1,0:T(8,128)(2,1)}, u32[]{:S(2)}, u32[]{:S(2)}) collective-permute-start(bf16[3072,512]{1,0:T(8,128)(2,1)} %collective-permute-done.3), channel_id=1, source_target_pairs={{0,8},{8,16},{16,24},{24,0},{1,9},{9,17},{17,25},{25,1},{2,10},{10... | collective-permute-start | bytes 9437192 | tf_op jit(solution)/shard_map/ppermute | solution.py:11
  124.0 91.3 %collective-permute-start.6 = (s32[512]{0:T(512)S(1)}, s32[512]{0:T(512)S(1)}, u32[]{:S(2)}, u32[]{:S(2)}) collective-permute-start(s32[512]{0:T(512)S(1)} %collective-permute-done.2), channel_id=1, source_target_pairs={{0,8},{8,16},{16,24},{24,0},{1,9},{9,17},{17,25},{25,1},{2,10},{10... | collective-permute-start | bytes 6152 | tf_op jit(solution)/shard_map/ppermute | solution.py:11
  125.2 93.6 %collective-permute-start.5 = (s32[512]{0:T(512)S(1)}, s32[512]{0:T(512)S(1)}, u32[]{:S(2)}, u32[]{:S(2)}) collective-permute-start(s32[512]{0:T(512)S(1)} %collective-permute-done.1), channel_id=1, source_target_pairs={{0,8},{8,16},{16,24},{24,0},{1,9},{9,17},{17,25},{25,1},{2,10},{10... | collective-permute-start | bytes 6152 | tf_op jit(solution)/shard_map/ppermute | solution.py:11
  147.9 107.3 %collective-permute-start.4 = (bf16[1536,512]{1,0:T(8,128)(2,1)}, bf16[1536,512]{1,0:T(8,128)(2,1)}, u32[]{:S(2)}, u32[]{:S(2)}) collective-permute-start(bf16[1536,512]{1,0:T(8,128)(2,1)} %collective-permute-done), channel_id=1, source_target_pairs={{0,8},{8,16},{16,24},{24,0},{1,9},{9,17},{17,25},{25,1},{2,10},{10... | collective-permute-start | bytes 4718600 | tf_op jit(solution)/shard_map/ppermute | solution.py:11
  218.8 37.6 %copy-start.5 = (bf16[1536,512]{1,0:T(8,128)(2,1)S(1)}, bf16[1536,512]{1,0:T(8,128)(2,1)}, u32[]{:S(2)}) copy-start(bf16[1536,512]{1,0:T(8,128)(2,1)} %all-gather.3.cloned.1.call-done) | copy-start | bytes 4718596
  222.0 26.4 %collective-permute-start.10 = (s32[512]{0:T(512)S(1)}, s32[512]{0:T(512)S(1)}, u32[]{:S(2)}, u32[]{:S(2)}) collective-permute-start(s32[512]{0:T(512)S(1)} %collective-permute-done.6), channel_id=1, source_target_pairs={{0,8},{8,16},{16,24},{24,0},{1,9},{9,17},{17,25},{25,1},{2,10},{10... | collective-permute-start | bytes 6152 | tf_op jit(solution)/shard_map/ppermute | solution.py:11
  222.1 29.9 %collective-permute-start.9 = (s32[512]{0:T(512)S(1)}, s32[512]{0:T(512)S(1)}, u32[]{:S(2)}, u32[]{:S(2)}) collective-permute-start(s32[512]{0:T(512)S(1)} %collective-permute-done.5), channel_id=1, source_target_pairs={{0,8},{8,16},{16,24},{24,0},{1,9},{9,17},{17,25},{25,1},{2,10},{10... | collective-permute-start | bytes 6152 | tf_op jit(solution)/shard_map/ppermute | solution.py:11
  255.2 39.4 %collective-permute-start.8 = (bf16[1536,512]{1,0:T(8,128)(2,1)}, bf16[1536,512]{1,0:T(8,128)(2,1)S(1)}, u32[]{:S(2)}, u32[]{:S(2)}) collective-permute-start(bf16[1536,512]{1,0:T(8,128)(2,1)} %collective-permute-done.4), channel_id=1, source_target_pairs={{0,8},{8,16},{16,24},{24,0},{1,9},{9,17},{17,25},{25,1},{2,10},{10... | collective-permute-start | bytes 4718600 | tf_op jit(solution)/shard_map/ppermute | solution.py:11
  255.2 105.2 %collective-permute-start.11 = (bf16[3072,512]{1,0:T(8,128)(2,1)}, bf16[3072,512]{1,0:T(8,128)(2,1)}, u32[]{:S(2)}, u32[]{:S(2)}) collective-permute-start(bf16[3072,512]{1,0:T(8,128)(2,1)} %collective-permute-done.7), channel_id=1, source_target_pairs={{0,8},{8,16},{16,24},{24,0},{1,9},{9,17},{17,25},{25,1},{2,10},{10... | collective-permute-start | bytes 9437192 | tf_op jit(solution)/shard_map/ppermute | solution.py:11
  387.7 18.7 %copy-start.1 = (f32[1792]{0:T(1024)S(1)}, f32[1792]{0:T(1024)}, u32[]{:S(2)}) copy-start(f32[1792]{0:T(1024)} %param.14) | copy-start | bytes 21508
Sparse Core Ops, SparseCore 0:
  9.8 31.2 all-gather.4
Sparse Core Ops, SparseCore 1:
  42.6 26.1 all-gather.2
where the time goes:
time: 414 us
  waiting for transfers between devices  280 us (68%)
  matrix products  60.7 us (15%)
  local copies, waits for them, and re-layouts  45.3 us (11%)
  between operations  15.8 us (4%)
  starting transfers between devices  11.2 us (3%)
    ppermute x12, waiting for transfers between devices, from_behind(): lax.ppermute(value, axis, [(i, (i + by) % peers) for i in range(peers)])  223 us
    dot_general x4, matrix products, contract_pairs(): lax.dot_general(left, right, (((1,), (1,)), ((), ())), preferred_element_...  60.7 us
    all_gather x1, waiting for transfers between devices, per_device(): right = lax.all_gather(b_pairs, 'row', axis=0, tiled=True)  32.9 us
    gather x8, local copies, waits for them, and re-layouts, per_device(): gap = jnp.take(vir_height, vir_part) + jnp.take(occ_depth, occ_part)  26.7 us
    all_gather x1, waiting for transfers between devices, per_device(): left = lax.all_gather(b_pairs, 'col', axis=0, tiled=True)  23.2 us
    reshape x1, local copies, waits for them, and re-layouts, per_device(): return total.reshape(1, n_row, 1, sub_width, sub_width * n_col)  18.6 us
    ppermute x12, starting transfers between devices, from_behind(): lax.ppermute(value, axis, [(i, (i + by) % peers) for i in range(peers)])  11.1 us
  transfers between devices with their start and end apart: 14, of which 8 were waited for; matrix products, arithmetic and copies ran while one was open for 15% of the time, Pallas kernels for 0%

commit v1 on v0

--- a/solution.py
+++ b/solution.py
@@ -1,9 +1,14 @@
+import functools
+
 import jax
 import jax.numpy as jnp
 from jax import lax
+from jax.experimental import pallas as pl
+from jax.experimental.pallas import tpu as pltpu
 from jax.sharding import PartitionSpec as P
 
 STEPS = 4
+PIECES = 6
 
 
 def from_behind(value, axis, by):
@@ -17,7 +22,7 @@
     )
 
 
-def per_device(b_pairs, occ_index, vir_index, occ_depth, vir_height, omega):
+def ring_device(b_pairs, occ_index, vir_index, occ_depth, vir_height, omega):
     square = omega[0] * omega[0]
     n_row = lax.axis_size("row")
     n_col = lax.axis_size("col")
@@ -40,9 +45,266 @@
     return total.reshape(1, n_row, 1, sub_width, sub_width * n_col)
 
 
+def across(even):
+    pairs = []
+    for row in range(4):
+        for col in range(2):
+            along_col = (row % 2 == 0) == even
+            to = (row, 1 - col) if along_col else ((row + 2) % 4, col)
+            pairs.append((row * 2 + col, to[0] * 2 + to[1]))
+    return lambda value: lax.ppermute(value, ("row", "col"), pairs)
+
+
+def along_line(core_0, core_1):
+    pairs = [
+        (a * 4 + y * 2 + core, b * 4 + y * 2 + core)
+        for core, hops in enumerate((core_0, core_1))
+        for y in range(2)
+        for a, b in hops
+    ]
+    return lambda value: lax.ppermute(value, ("freq", "row"), pairs)
+
+
+OUTER = ((0, 1), (1, 0), (2, 3), (3, 2))
+INNER = ((1, 2), (2, 1))
+TO_ENDS = ((1, 0), (2, 3))
+
+
+def other_core(value):
+    return lax.ppermute(value, "row", [(i, i ^ 1) for i in range(4)])
+
+
+def look_up(table, index):
+    hit = index[:, None] == lax.broadcasted_iota(jnp.int32, (1, table.shape[0]), 1)
+    return jnp.sum(jnp.where(hit, table[None, :], 0.0), axis=1)
+
+
+def tile_kernel(slots, fresh, tiles, sub, span, *refs):
+    n = len(slots)
+    place, weight = refs[:2]
+    pieces = [refs[2 + PIECES * k : 2 + PIECES * (k + 1)] for k in range(n)]
+    rest = list(refs[2 + PIECES * n :])
+    if not fresh:
+        rest.pop(0)
+    out, rbuf, lraw, lbuf, obuf, rsem, lsem, osem, isem = rest
+    core = place[0]
+
+    def cols(k):
+        return pl.ds(k * span, span)
+
+    def to_right(k, which, src):
+        return pltpu.make_async_copy(src, rbuf.at[which, :, cols(k)], rsem.at[which, k])
+
+    def to_left(k, src):
+        return pltpu.make_async_copy(src, lraw.at[:, cols(k)], lsem.at[k])
+
+    for k, slot in enumerate(slots):
+        op_a, op_b, xy_a, xy_b, cs_a, cs_b = pieces[k]
+        if slot == 0:
+            to_right(k, core, op_a).start()
+            to_right(k, 1 - core, op_b).start()
+            y_a, y_b = 3, 2
+        else:
+            to_right(k, 0, op_a).start()
+            to_right(k, 1, op_b).start()
+            y_a, y_b = 2, 3
+
+        @pl.when(core == 0)
+        def _():
+            to_left(k, xy_a).start()
+            to_right(k, y_a, cs_a).start()
+            to_right(k, y_b, xy_b).start()
+
+        @pl.when(core == 1)
+        def _():
+            to_left(k, xy_b).start()
+            to_right(k, y_a, xy_a).start()
+            to_right(k, y_b, cs_b).start()
+
+    def window(m):
+        i, j = tiles[m]
+        col = pl.multiple_of(((place[1] + j) % 2) * sub, sub)
+        return out.at[place[2 + i], :, pl.ds(col, sub)]
+
+    def put(m):
+        return pltpu.make_async_copy(obuf.at[m % 2], window(m), osem.at[m % 2])
+
+    def get(m):
+        return pltpu.make_async_copy(window(m), obuf.at[m % 2], isem.at[m % 2])
+
+    if not fresh:
+        get(0).start()
+    ready = set()
+
+    def await_right(i):
+        if i not in ready:
+            ready.add(i)
+            for k in range(n):
+                to_right(k, i, pieces[k][0]).wait()
+
+    def weigh(j):
+        if j == 0:
+            await_right(0)
+            await_right(1)
+        for k in range(n):
+            if j == 1:
+                to_left(k, pieces[k][2]).wait()
+
+            @pl.loop(0, sub // 128)
+            def _(r):
+                rows = pl.ds(pl.multiple_of(r * 128, 128), 128)
+                raw = rbuf[core, rows, cols(k)] if j == 0 else lraw[rows, cols(k)]
+                lbuf[j, rows, cols(k)] = (raw.astype(jnp.float32) * weight[k]).astype(
+                    jnp.bfloat16
+                )
+
+    weighed = set()
+    for m, (i, j) in enumerate(tiles):
+        if j not in weighed:
+            weighed.add(j)
+            weigh(j)
+        await_right(i)
+        if fresh:
+            if m >= 2:
+                put(m - 2).wait()
+        else:
+            get(m).wait()
+        part = contract_pairs(rbuf[i], lbuf[j])
+        obuf[m % 2] = part if fresh else obuf[m % 2] + part
+        put(m).start()
+        if not fresh and m + 1 < len(tiles):
+            if m >= 1:
+                put(m - 1).wait()
+            get(m + 1).start()
+    for m in range(max(len(tiles) - 2, 0), len(tiles)):
+        put(m).wait()
+
+
+def add_tiles(slots, tiles, place, weight, pieces, total):
+    fresh = total is None
+    n = len(slots)
+    sub, span = pieces[0][0].shape
+    anywhere = pl.BlockSpec(memory_space=pl.ANY)
+    operands = [place, weight] + [piece for slot in pieces for piece in slot]
+    aliases = {}
+    if not fresh:
+        aliases = {len(operands): 0}
+        operands.append(total)
+    moved = len(tiles) * sub * sub * 4 * (1 if fresh else 2)
+    return pl.pallas_call(
+        functools.partial(tile_kernel, slots, fresh, tiles, sub, span),
+        out_shape=jax.ShapeDtypeStruct((4, sub, 2 * sub), jnp.float32),
+        in_specs=[
+            pl.BlockSpec(memory_space=pltpu.SMEM),
+            pl.BlockSpec(memory_space=pltpu.VMEM),
+        ]
+        + [anywhere] * (len(operands) - 2),
+        out_specs=anywhere,
+        input_output_aliases=aliases,
+        scratch_shapes=[
+            pltpu.VMEM((4, sub, n * span), jnp.bfloat16),
+            pltpu.VMEM((sub, n * span), jnp.bfloat16),
+            pltpu.VMEM((2, sub, n * span), jnp.bfloat16),
+            pltpu.VMEM((2, sub, sub), jnp.float32),
+            pltpu.SemaphoreType.DMA((4, n)),
+            pltpu.SemaphoreType.DMA((n,)),
+            pltpu.SemaphoreType.DMA((2,)),
+            pltpu.SemaphoreType.DMA((2,)),
+        ],
+        cost_estimate=pl.CostEstimate(
+            flops=2 * len(tiles) * sub * sub * span * n,
+            bytes_accessed=moved + 5 * n * sub * span * 2,
+            transcendentals=0,
+        ),
+        compiler_params=pltpu.CompilerParams(vmem_limit_bytes=32 * 1024 * 1024),
+    )(*operands)
+
+
+def line_device(b_pairs, occ_index, vir_index, occ_depth, vir_height, omega):
+    group = lax.axis_index("freq")
+    row = lax.axis_index("row")
+    col = lax.axis_index("col")
+    core = row % 2
+    first = core == 0
+    end = (group == 0) | (group == 3)
+    sub, span = b_pairs.shape
+
+    xy = [across(True), across(False)]
+    own = b_pairs
+    cross = [None] * 8
+    cross[0] = xy[0](own)
+    hop_0 = along_line(OUTER, INNER)(own)
+    cross[1] = xy[1](own)
+    hop_1 = along_line(INNER, OUTER)(own)
+    own_swap = other_core(own)
+    hop_2 = along_line(INNER, TO_ENDS)(hop_0)
+    swap_0 = other_core(hop_0)
+    op_2 = jnp.where(first, hop_0, swap_0)
+    cross[2] = xy[0](op_2)
+    hop_3 = along_line(TO_ENDS, INNER)(hop_1)
+    swap_1 = other_core(hop_1)
+    op_3 = jnp.where(first, swap_1, hop_1)
+    cross[3] = xy[1](op_3)
+    hop_4 = along_line(TO_ENDS, ())(hop_2)
+    swap_2 = other_core(hop_2)
+    op_4 = jnp.where(
+        end, jnp.where(first, swap_2, hop_2), jnp.where(first, swap_0, hop_0)
+    )
+    cross[4] = xy[1](op_4)
+    hop_5 = along_line((), TO_ENDS)(hop_3)
+    swap_3 = other_core(hop_3)
+    op_5 = jnp.where(
+        end, jnp.where(first, hop_3, swap_3), jnp.where(first, hop_1, swap_1)
+    )
+    cross[5] = xy[0](op_5)
+    swap_4 = other_core(hop_4)
+    op_6 = jnp.where(
+        end, jnp.where(first, hop_4, swap_4), jnp.where(first, hop_2, swap_2)
+    )
+    cross[6] = xy[0](op_6)
+    swap_5 = other_core(hop_5)
+    op_7 = jnp.where(
+        end, jnp.where(first, swap_5, hop_5), jnp.where(first, swap_3, hop_3)
+    )
+    cross[7] = xy[1](op_7)
+    cross_swap = [other_core(value) for value in cross]
+
+    def slot(op_a, op_b, a, b):
+        return op_a, op_b, cross[a], cross[b], cross_swap[a], cross_swap[b]
+
+    slots = [
+        slot(own, own_swap, 0, 1),
+        slot(op_2, op_3, 2, 3),
+        slot(op_5, op_4, 5, 4),
+        slot(op_6, op_7, 6, 7),
+    ]
+
+    occ_index, vir_index, hop_0 = lax.optimization_barrier(
+        (occ_index, vir_index, hop_0)
+    )
+    gap = look_up(vir_height, vir_index) + look_up(occ_depth, occ_index)
+    gaps = jnp.stack([gap] + [from_behind(gap, "freq", by) for by in (1, 2, 3)])
+    near = jnp.where(group < 2, 2, 1)
+    far = jnp.where(group < 2, 3, 0)
+    source = jnp.stack([group, group ^ 1, near, far])
+    gaps = jnp.take(gaps, (group - source) % 4, axis=0)
+    weight = (4.0 * gaps / (gaps * gaps + omega[0] * omega[0]))[:, None, :]
+
+    y = row // 2
+    place = jnp.stack(
+        [core, col, y * 2, y * 2 + 1, (1 - y) * 2, (1 - y) * 2 + 1]
+    ).astype(jnp.int32)
+    tiles = tuple((i, j) for j in range(2) for i in range(4))
+    total = add_tiles((0, 1, 2), tiles, place, weight[:3], slots[:3], None)
+    total = add_tiles((3,), tiles, place, weight[3:], slots[3:], total)
+    return total.reshape(1, 4, 1, sub, 2 * sub)
+
+
 def solution(mesh):
     in_specs = (P(("row", "col"), "freq"), P("freq"), P("freq"), P(), P(), P("freq"))
     out_specs = P("freq", None, "col", None, "row")
+    shape = tuple(mesh.shape[axis] for axis in ("freq", "row", "col"))
+    per_device = line_device if shape == (4, 4, 2) else ring_device
     return jax.shard_map(
         per_device, mesh=mesh, in_specs=in_specs, out_specs=out_specs, check_vma=False
     )

time: 414 us -> 191 us (0.46)
  waiting for transfers between devices: 280 us -> 79.5 us
  matrix products: 60.7 us -> 0 us
  Pallas kernels: 0 us -> 55.6 us
  local copies, waits for them, and re-layouts: 45.3 us -> 9.04 us
  starting transfers between devices: 11.2 us -> 36.7 us
  between operations: 15.8 us -> 1.04 us
  other arithmetic: 0.81 us -> 8.29 us
    ppermute x12 -> x3, waiting for transfers between devices: 223 us -> 0.01 us  [from_behind(): lax.ppermute(value, axis, [(i, (i + by) % peers) for i in range(peers)])]
    ppermute x0 -> x29, waiting for transfers between devices: none -> 79.5 us  [the longest x8 46 us: across(): return lambda value: lax.ppermute(value, ('row', 'col'), pairs)]
    dot_general x4 -> x0, matrix products: 60.7 us -> none  [contract_pairs(): lax.dot_general(left, right, (((1,), (1,)), ((), ())), preferred_element_...]
    all_gather x2 -> x0, waiting for transfers between devices: 56.1 us -> none  [the longest x1 32.9 us: per_device(): right = lax.all_gather(b_pairs, 'row', axis=0, tiled=True)]
    pallas_call x0 -> x2, Pallas kernels: none -> 55.6 us  [add_tiles(): pl.pallas_call(functools.partial(tile_kernel, slots, fresh, tiles, sub, s...]
    ppermute x0 -> x29, starting transfers between devices: none -> 33.7 us  [the longest x6 14.2 us: along_line(): return lambda value: lax.ppermute(value, ('freq', 'row'), pairs)]
    gather x8 -> x1, local copies, waits for them, and re-layouts: 26.7 us -> 0.56 us  [line_device(): gaps = jnp.take(gaps, (group - source) % 4, axis=0)]
    reshape x1 -> x0, local copies, waits for them, and re-layouts: 18.6 us -> none  [per_device(): return total.reshape(1, n_row, 1, sub_width, sub_width * n_col)]
  transfers between devices with their start and end apart: 14 -> 32, of which waited for: 8 -> 10; matrix products, arithmetic and copies ran while one was open for 15% -> 5% of each run, Pallas kernels for 0% -> 13%
where the time goes in v1:
time: 191 us; the launch traced here: 190 us
  waiting for transfers between devices  79.5 us (42%)
  Pallas kernels  55.6 us (29%)
  starting transfers between devices  36.7 us (19%)
  local copies, waits for them, and re-layouts  9.04 us (5%)
  other arithmetic  8.29 us (4%)
    pallas_call x2, Pallas kernels, add_tiles(): pl.pallas_call(functools.partial(tile_kernel, slots, fresh, tiles, sub, s...  55.6 us
    ppermute x8, waiting for transfers between devices, across(): return lambda value: lax.ppermute(value, ('row', 'col'), pairs)  46 us
    ppermute x6, waiting for transfers between devices, along_line(): return lambda value: lax.ppermute(value, ('freq', 'row'), pairs)  31.6 us
    ppermute x6, starting transfers between devices, along_line(): return lambda value: lax.ppermute(value, ('freq', 'row'), pairs)  14.2 us
    ppermute x8, starting transfers between devices, across(): return lambda value: lax.ppermute(value, ('row', 'col'), pairs)  11.1 us
    ppermute x15, starting transfers between devices, other_core(): return lax.ppermute(value, 'row', [(i, i ^ 1) for i in range(4)])  8.47 us
    unnamed x24, local copies, waits for them, and re-layouts  8.39 us
  transfers between devices with their start and end apart: 32, of which 10 were waited for; matrix products, arithmetic and copies ran while one was open for 5% of the time, Pallas kernels for 13%

profile of v1, /device:TPU:0, one launch (start us, length us, event | category | flops | bytes accessed | tf_op | source)
XLA Modules:
  0.0 190.1 jit_solution(14821073274568785800)
XLA Ops:
  0.7 7.7 %collective-permute-start = (bf16[768,512]{1,0:T(8,128)(2,1)}, bf16[768,512]{1,0:T(8,128)(2,1)S(1)}, u32[]{:S(2)}, u32[]{:S(2)}) collective-permute-start(bf16[768,512]{1,0:T(8,128)(2,1)} %refs_2_.1), channel_id=1, source_target_pairs={{0,8},{8,0},{16,24},{24,16},{4,12},{12,4},{20,28},{28,20},{10,18},... | collective-permute-start | bytes 2359304 | tf_op jit(solution)/shard_map/ppermute | solution.py:65
  8.4 1.3 collective-permute-start.9
  9.7 1.6 collective-permute-start.18
  11.3 11.4 %collective-permute-done = bf16[768,512]{1,0:T(8,128)(2,1)S(1)} collective-permute-done((bf16[768,512]{1,0:T(8,128)(2,1)}, bf16[768,512]{1,0:T(8,128)(2,1)S(1)}, u32[]{:S(2)}, u32[]{:S(2)}) %collective-permute-start) | collective-permute-done | bytes 786464 | tf_op jit(solution)/shard_map/ppermute | solution.py:65
  22.7 1.6 collective-permute-start.4
  24.2 16.9 %collective-permute-done.9 = bf16[768,512]{1,0:T(8,128)(2,1)S(1)} collective-permute-done((bf16[768,512]{1,0:T(8,128)(2,1)S(1)}, bf16[768,512]{1,0:T(8,128)(2,1)S(1)}, u32[]{:S(2)}, u32[]{:S(2)}) %collective-permute-start.9) | collective-permute-done | bytes 786464 | tf_op jit(solution)/shard_map/ppermute | solution.py:65
  41.2 1.6 collective-permute-start.10
  42.8 2.4 %collective-permute-start.19 = (bf16[768,512]{1,0:T(8,128)(2,1)}, bf16[768,512]{1,0:T(8,128)(2,1)}, u32[]{:S(2)}, u32[]{:S(2)}) collective-permute-start(bf16[768,512]{1,0:T(8,128)(2,1)} %refs_2_.1), channel_id=1, source_target_pairs={{0,4},{1,5},{2,3},{3,2},{4,0},{5,1},{6,7},{7,6},{8,12},{9,13},{10,... | collective-permute-start | bytes 2359304 | tf_op jit(solution)/shard_map/ppermute | solution.py:55
  48.2 4.4 %collective-permute-start.11 = (bf16[768,512]{1,0:T(8,128)(2,1)}, bf16[768,512]{1,0:T(8,128)(2,1)}, u32[]{:S(2)}, u32[]{:S(2)}) collective-permute-start(bf16[768,512]{1,0:T(8,128)(2,1)} %collective-permute-done.10), channel_id=1, source_target_pairs={{0,2},{2,0},{4,6},{6,4},{1,3},{3,1},{5,7},{7,5},{8,10},{10,8},{12,... | collective-permute-start | bytes 2359304 | tf_op jit(solution)/shard_map/ppermute | solution.py:74
  52.5 2.9 %collective-permute-done.19.refs_5_ = bf16[768,512]{1,0:T(8,128)(2,1)} collective-permute-done((bf16[768,512]{1,0:T(8,128)(2,1)}, bf16[768,512]{1,0:T(8,128)(2,1)}, u32[]{:S(2)}, u32[]{:S(2)}) %collective-permute-start.19) | collective-permute-done | bytes 786464 | tf_op jit(solution)/shard_map/ppermute | solution.py:55
  56.9 3.3 %collective-permute-done.5 = bf16[768,512]{1,0:T(8,128)(2,1)} collective-permute-done((bf16[768,512]{1,0:T(8,128)(2,1)}, bf16[768,512]{1,0:T(8,128)(2,1)}, u32[]{:S(2)}, u32[]{:S(2)}) %collective-permute-start.5) | collective-permute-done | bytes 786464 | tf_op jit(solution)/shard_map/ppermute | solution.py:65
  61.1 1.3 select_reduce_fusion
  63.8 2.3 %select_select_fusion.1 = (bf16[768,512]{1,0:T(8,128)(2,1)S(1)}, bf16[768,512]{1,0:T(8,128)(2,1)S(1)}, bf16[768,512]{1,0:T(8,128)(2,1)S(1)}) fusion(bf16[768,512]{1,0:T(8,128)(2,1)} %copy-done.8, bf16[768,512]{1,0:T(8,128)(2,1)} %copy-done.10, bf16[768,512]{1,0:T(8,128)(2,1)} %copy-done.9, bf16[768,512]{1,0:T(8,128)(2,1)} %copy-done.11, pred[]{:T(512)S(6)} %eq.47, ...), kind=kLoop, calls=%fused_computation.4 | loop fusion | flops 2752512 | bytes 7077890 | tf_op jit(solution)/shard_map/jit(_where)/select_n | solution.py:256
  66.2 2.4 %collective-permute-start.3 = (f32[512]{0:T(512)S(1)}, f32[512]{0:T(512)S(1)}, u32[]{:S(2)}, u32[]{:S(2)}) collective-permute-start(f32[512]{0:T(512)S(1)} %add.67), channel_id=1, source_target_pairs={{0,24},{8,0},{16,8},{24,16},{1,25},{9,1},{17,9},{25,17},{2,26},{10... | collective-permute-start | bytes 6152 | tf_op jit(solution)/shard_map/ppermute | solution.py:16
  69.2 3.5 %select_select_fusion = (bf16[768,512]{1,0:T(8,128)(2,1)}, bf16[768,512]{1,0:T(8,128)(2,1)S(1)}, bf16[768,512]{1,0:T(8,128)(2,1)}) fusion(bf16[768,512]{1,0:T(8,128)(2,1)} %collective-permute-done.22, bf16[768,512]{1,0:T(8,128)(2,1)} %copy-done.7, bf16[768,512]{1,0:T(8,128)(2,1)} %collective-permute-done.7, bf16[768,512]{1,0:T(8,128)(2,1)} %collective-permute-done.4, ...), kind=kLoop, calls=%fused_computation.3 | loop fusion | flops 2752512 | bytes 7077890 | tf_op jit(solution)/shard_map/jit(_where)/select_n | solution.py:250
  72.6 1.5 collective-permute-start.28
  74.1 1.5 collective-permute-start.14
  77.1 1.5 collective-permute-start.29
  80.7 12.4 %collective-permute-done.28.refs_16_ = bf16[768,512]{1,0:T(8,128)(2,1)} collective-permute-done((bf16[768,512]{1,0:T(8,128)(2,1)S(1)}, bf16[768,512]{1,0:T(8,128)(2,1)}, u32[]{:S(2)}, u32[]{:S(2)}) %collective-permute-start.28) | collective-permute-done | bytes 786464 | tf_op jit(solution)/shard_map/ppermute | solution.py:55
  93.2 1.5 collective-permute-start.13
  94.7 16.8 %collective-permute-done.25.refs_11_ = bf16[768,512]{1,0:T(8,128)(2,1)} collective-permute-done((bf16[768,512]{1,0:T(8,128)(2,1)S(1)}, bf16[768,512]{1,0:T(8,128)(2,1)}, u32[]{:S(2)}, u32[]{:S(2)}) %collective-permute-start.25) | collective-permute-done | bytes 786464 | tf_op jit(solution)/shard_map/ppermute | solution.py:55
  111.6 13.8 %collective-permute-done.29.refs_17_ = bf16[768,512]{1,0:T(8,128)(2,1)} collective-permute-done((bf16[768,512]{1,0:T(8,128)(2,1)}, bf16[768,512]{1,0:T(8,128)(2,1)}, u32[]{:S(2)}, u32[]{:S(2)}) %collective-permute-start.29) | collective-permute-done | bytes 786464 | tf_op jit(solution)/shard_map/ppermute | solution.py:55
  134.3 25.6 %shard_map.64.refs_8_ = f32[4,768,1536]{2,1,0:T(8,128)} custom-call(s32[6]{0:T(128)S(1)} %stack.65.refs_0_, f32[3,1,512]{2,1,0:T(1,128)S(1)} %slice.15.refs_1_, bf16[768,512]{1,0:T(8,128)(2,1)S(1)} %copy-done, bf16[768,512]{1,0:T(8,128)(2,1)S(1)} %copy-done.2, bf16[768,512]{1,0:T(8,128)(2,1)} %collective-permute-done.18.refs_4_, ...), custom_call_target="tpu_custom_call" | custom-call | flops 14495514624 | bytes 30670848 | tf_op jit(solution)/shard_map/pallas_call | solution.py:194
  160.0 30.0 %shard_map.65 = f32[4,768,1536]{2,1,0:T(8,128)} custom-call(s32[6]{0:T(128)S(1)} %stack.65.refs_0_, f32[1,1,512]{2,1,0:T(1,128)S(1)} %slice_bitcast_fusion.refs_1_, bf16[768,512]{1,0:T(8,128)(2,1)S(1)} %get-tuple-element.10.refs_2_, bf16[768,512]{1,0:T(8,128)(2,1)S(1)} %get-tuple-element.13.refs_3_, ...), custom_call_target="tpu_custom_call", output_to_operand_aliasing={{}: (8, {})} | custom-call | flops 4831838208 | bytes 41680896 | tf_op jit(solution)/shard_map/pallas_call | solution.py:194
  (80 shorter events, 20.0 us)
Async XLA Ops:
  0.7 22.0 %collective-permute-start = (bf16[768,512]{1,0:T(8,128)(2,1)}, bf16[768,512]{1,0:T(8,128)(2,1)S(1)}, u32[]{:S(2)}, u32[]{:S(2)}) collective-permute-start(bf16[768,512]{1,0:T(8,128)(2,1)} %refs_2_.1), channel_id=1, source_target_pairs={{0,8},{8,0},{16,24},{24,16},{4,12},{12,4},{20,28},{28,20},{10,18},... | collective-permute-start | bytes 2359304 | tf_op jit(solution)/shard_map/ppermute | solution.py:65
  8.4 32.7 %collective-permute-start.9 = (bf16[768,512]{1,0:T(8,128)(2,1)S(1)}, bf16[768,512]{1,0:T(8,128)(2,1)S(1)}, u32[]{:S(2)}, u32[]{:S(2)}) collective-permute-start(bf16[768,512]{1,0:T(8,128)(2,1)S(1)} %collective-permute-done.8), channel_id=1, source_target_pairs={{8,0},{16,24},{12,4},{20,28},{10,18},{18,10},{14,22},{22,14},{9,1}... | collective-permute-start | bytes 2359304 | tf_op jit(solution)/shard_map/ppermute | solution.py:65
  9.7 35.5 %collective-permute-start.18 = (bf16[768,512]{1,0:T(8,128)(2,1)}, bf16[768,512]{1,0:T(8,128)(2,1)}, u32[]{:S(2)}, u32[]{:S(2)}) collective-permute-start(bf16[768,512]{1,0:T(8,128)(2,1)} %refs_2_.1), channel_id=1, source_target_pairs={{0,1},{1,0},{2,6},{3,7},{4,5},{5,4},{6,2},{7,3},{8,9},{9,8},{10,14... | collective-permute-start | bytes 2359304 | tf_op jit(solution)/shard_map/ppermute | solution.py:55
  22.7 22.5 %collective-permute-start.4 = (bf16[768,512]{1,0:T(8,128)(2,1)S(1)}, bf16[768,512]{1,0:T(8,128)(2,1)}, u32[]{:S(2)}, u32[]{:S(2)}) collective-permute-start(bf16[768,512]{1,0:T(8,128)(2,1)S(1)} %collective-permute-done), channel_id=1, source_target_pairs={{8,16},{16,8},{12,20},{20,12},{10,2},{18,26},{14,6},{22,30},{9,17}... | collective-permute-start | bytes 2359304 | tf_op jit(solution)/shard_map/ppermute | solution.py:65
  24.2 22.3 %collective-permute-start.17 = (bf16[768,512]{1,0:T(8,128)(2,1)}, bf16[768,512]{1,0:T(8,128)(2,1)S(1)}, u32[]{:S(2)}, u32[]{:S(2)}) collective-permute-start(bf16[768,512]{1,0:T(8,128)(2,1)} %refs_2_.1), channel_id=1, source_target_pairs={{0,2},{2,0},{4,6},{6,4},{1,3},{3,1},{5,7},{7,5},{8,10},{10,8},{12,... | collective-permute-start | bytes 2359304 | tf_op jit(solution)/shard_map/ppermute | solution.py:74
  42.8 12.7 %collective-permute-start.19 = (bf16[768,512]{1,0:T(8,128)(2,1)}, bf16[768,512]{1,0:T(8,128)(2,1)}, u32[]{:S(2)}, u32[]{:S(2)}) collective-permute-start(bf16[768,512]{1,0:T(8,128)(2,1)} %refs_2_.1), channel_id=1, source_target_pairs={{0,4},{1,5},{2,3},{3,2},{4,0},{5,1},{6,7},{7,6},{8,12},{9,13},{10,... | collective-permute-start | bytes 2359304 | tf_op jit(solution)/shard_map/ppermute | solution.py:55
  45.2 10.3 %collective-permute-start.23 = (bf16[768,512]{1,0:T(8,128)(2,1)S(1)}, bf16[768,512]{1,0:T(8,128)(2,1)S(1)}, u32[]{:S(2)}, u32[]{:S(2)}) collective-permute-start(bf16[768,512]{1,0:T(8,128)(2,1)S(1)} %collective-permute-done.8), channel_id=1, source_target_pairs={{0,2},{2,0},{4,6},{6,4},{1,3},{3,1},{5,7},{7,5},{8,10},{10,8},{12,... | collective-permute-start | bytes 2359304 | tf_op jit(solution)/shard_map/ppermute | solution.py:74
  45.2 15.0 %collective-permute-start.5 = (bf16[768,512]{1,0:T(8,128)(2,1)}, bf16[768,512]{1,0:T(8,128)(2,1)}, u32[]{:S(2)}, u32[]{:S(2)}) collective-permute-start(bf16[768,512]{1,0:T(8,128)(2,1)} %collective-permute-done.4), channel_id=1, source_target_pairs={{8,0},{16,24},{12,4},{20,28},{9,1},{17,25},{13,5},{21,29}} | collective-permute-start | bytes 2359304 | tf_op jit(solution)/shard_map/ppermute | solution.py:65
  47.4 15.0 %collective-permute-start.12 = (bf16[768,512]{1,0:T(8,128)(2,1)S(1)}, bf16[768,512]{1,0:T(8,128)(2,1)S(1)}, u32[]{:S(2)}, u32[]{:S(2)}) collective-permute-start(bf16[768,512]{1,0:T(8,128)(2,1)S(1)} %collective-permute-done.9), channel_id=1, source_target_pairs={{0,2},{2,0},{4,6},{6,4},{1,3},{3,1},{5,7},{7,5},{8,10},{10,8},{12,... | collective-permute-start | bytes 2359304 | tf_op jit(solution)/shard_map/ppermute | solution.py:74
  48.2 14.8 %collective-permute-start.11 = (bf16[768,512]{1,0:T(8,128)(2,1)}, bf16[768,512]{1,0:T(8,128)(2,1)}, u32[]{:S(2)}, u32[]{:S(2)}) collective-permute-start(bf16[768,512]{1,0:T(8,128)(2,1)} %collective-permute-done.10), channel_id=1, source_target_pairs={{0,2},{2,0},{4,6},{6,4},{1,3},{3,1},{5,7},{7,5},{8,10},{10,8},{12,... | collective-permute-start | bytes 2359304 | tf_op jit(solution)/shard_map/ppermute | solution.py:74
  55.5 10.7 %collective-permute-start.22 = (bf16[768,512]{1,0:T(8,128)(2,1)S(1)}, bf16[768,512]{1,0:T(8,128)(2,1)}, u32[]{:S(2)}, u32[]{:S(2)}) collective-permute-start(bf16[768,512]{1,0:T(8,128)(2,1)S(1)} %collective-permute-done), channel_id=1, source_target_pairs={{0,2},{2,0},{4,6},{6,4},{1,3},{3,1},{5,7},{7,5},{8,10},{10,8},{12,... | collective-permute-start | bytes 2359304 | tf_op jit(solution)/shard_map/ppermute | solution.py:74
  56.4 12.1 %collective-permute-start.7 = (bf16[768,512]{1,0:T(8,128)(2,1)}, bf16[768,512]{1,0:T(8,128)(2,1)}, u32[]{:S(2)}, u32[]{:S(2)}) collective-permute-start(bf16[768,512]{1,0:T(8,128)(2,1)} %collective-permute-done.4), channel_id=1, source_target_pairs={{0,2},{2,0},{4,6},{6,4},{1,3},{3,1},{5,7},{7,5},{8,10},{10,8},{12,... | collective-permute-start | bytes 2359304 | tf_op jit(solution)/shard_map/ppermute | solution.py:74
  62.4 13.7 %collective-permute-start.20 = (bf16[768,512]{1,0:T(8,128)(2,1)}, bf16[768,512]{1,0:T(8,128)(2,1)S(1)}, u32[]{:S(2)}, u32[]{:S(2)}) collective-permute-start(bf16[768,512]{1,0:T(8,128)(2,1)} %collective-permute-done.18.refs_4_), channel_id=1, source_target_pairs={{0,2},{2,0},{4,6},{6,4},{1,3},{3,1},{5,7},{7,5},{8,10},{10,8},{12,... | collective-permute-start | bytes 2359304 | tf_op jit(solution)/shard_map/ppermute | solution.py:74
  63.3 15.3 %collective-permute-start.21 = (bf16[768,512]{1,0:T(8,128)(2,1)}, bf16[768,512]{1,0:T(8,128)(2,1)S(1)}, u32[]{:S(2)}, u32[]{:S(2)}) collective-permute-start(bf16[768,512]{1,0:T(8,128)(2,1)} %collective-permute-done.19.refs_5_), channel_id=1, source_target_pairs={{0,2},{2,0},{4,6},{6,4},{1,3},{3,1},{5,7},{7,5},{8,10},{10,8},{12,... | collective-permute-start | bytes 2359304 | tf_op jit(solution)/shard_map/ppermute | solution.py:74
  72.6 20.5 %collective-permute-start.28 = (bf16[768,512]{1,0:T(8,128)(2,1)S(1)}, bf16[768,512]{1,0:T(8,128)(2,1)}, u32[]{:S(2)}, u32[]{:S(2)}) collective-permute-start(bf16[768,512]{1,0:T(8,128)(2,1)S(1)} %get-tuple-element.12.refs_14_), channel_id=1, source_target_pairs={{0,1},{1,0},{2,6},{3,7},{4,5},{5,4},{6,2},{7,3},{8,9},{9,8},{10,14... | collective-permute-start | bytes 2359304 | tf_op jit(solution)/shard_map/ppermute | solution.py:55
  74.1 20.6 %collective-permute-start.14 = (bf16[768,512]{1,0:T(8,128)(2,1)S(1)}, bf16[768,512]{1,0:T(8,128)(2,1)}, u32[]{:S(2)}, u32[]{:S(2)}) collective-permute-start(bf16[768,512]{1,0:T(8,128)(2,1)S(1)} %get-tuple-element.13.refs_3_), channel_id=1, source_target_pairs={{0,4},{1,5},{2,3},{3,2},{4,0},{5,1},{6,7},{7,6},{8,12},{9,13},{10,... | collective-permute-start | bytes 2359304 | tf_op jit(solution)/shard_map/ppermute | solution.py:55
  75.7 35.9 %collective-permute-start.25 = (bf16[768,512]{1,0:T(8,128)(2,1)S(1)}, bf16[768,512]{1,0:T(8,128)(2,1)}, u32[]{:S(2)}, u32[]{:S(2)}) collective-permute-start(bf16[768,512]{1,0:T(8,128)(2,1)S(1)} %get-tuple-element.14.refs_9_), channel_id=1, source_target_pairs={{0,4},{1,5},{2,3},{3,2},{4,0},{5,1},{6,7},{7,6},{8,12},{9,13},{10,... | collective-permute-start | bytes 2359304 | tf_op jit(solution)/shard_map/ppermute | solution.py:55
  77.1 48.3 %collective-permute-start.29 = (bf16[768,512]{1,0:T(8,128)(2,1)}, bf16[768,512]{1,0:T(8,128)(2,1)}, u32[]{:S(2)}, u32[]{:S(2)}) collective-permute-start(bf16[768,512]{1,0:T(8,128)(2,1)} %get-tuple-element.9.refs_15_), channel_id=1, source_target_pairs={{0,4},{1,5},{2,3},{3,2},{4,0},{5,1},{6,7},{7,6},{8,12},{9,13},{10,... | collective-permute-start | bytes 2359304 | tf_op jit(solution)/shard_map/ppermute | solution.py:55
  79.5 47.0 %collective-permute-start.24 = (bf16[768,512]{1,0:T(8,128)(2,1)}, bf16[768,512]{1,0:T(8,128)(2,1)}, u32[]{:S(2)}, u32[]{:S(2)}) collective-permute-start(bf16[768,512]{1,0:T(8,128)(2,1)} %get-tuple-element.11.refs_8_), channel_id=1, source_target_pairs={{0,1},{1,0},{2,6},{3,7},{4,5},{5,4},{6,2},{7,3},{8,9},{9,8},{10,14... | collective-permute-start | bytes 2359304 | tf_op jit(solution)/shard_map/ppermute | solution.py:55
  93.2 34.1 %collective-permute-start.13 = (bf16[768,512]{1,0:T(8,128)(2,1)S(1)}, bf16[768,512]{1,0:T(8,128)(2,1)}, u32[]{:S(2)}, u32[]{:S(2)}) collective-permute-start(bf16[768,512]{1,0:T(8,128)(2,1)S(1)} %get-tuple-element.10.refs_2_), channel_id=1, source_target_pairs={{0,1},{1,0},{2,6},{3,7},{4,5},{5,4},{6,2},{7,3},{8,9},{9,8},{10,14... | collective-permute-start | bytes 2359304 | tf_op jit(solution)/shard_map/ppermute | solution.py:55
  94.7 33.2 %collective-permute-start.30 = (bf16[768,512]{1,0:T(8,128)(2,1)}, bf16[768,512]{1,0:T(8,128)(2,1)}, u32[]{:S(2)}, u32[]{:S(2)}) collective-permute-start(bf16[768,512]{1,0:T(8,128)(2,1)} %collective-permute-done.28.refs_16_), channel_id=1, source_target_pairs={{0,2},{2,0},{4,6},{6,4},{1,3},{3,1},{5,7},{7,5},{8,10},{10,8},{12,... | collective-permute-start | bytes 2359304 | tf_op jit(solution)/shard_map/ppermute | solution.py:74
  111.6 16.4 %collective-permute-start.27 = (bf16[768,512]{1,0:T(8,128)(2,1)}, bf16[768,512]{1,0:T(8,128)(2,1)}, u32[]{:S(2)}, u32[]{:S(2)}) collective-permute-start(bf16[768,512]{1,0:T(8,128)(2,1)} %collective-permute-done.25.refs_11_), channel_id=1, source_target_pairs={{0,2},{2,0},{4,6},{6,4},{1,3},{3,1},{5,7},{7,5},{8,10},{10,8},{12,... | collective-permute-start | bytes 2359304 | tf_op jit(solution)/shard_map/ppermute | solution.py:74
  127.3 32.6 %collective-permute-start.16 = (bf16[768,512]{1,0:T(8,128)(2,1)}, bf16[768,512]{1,0:T(8,128)(2,1)S(1)}, u32[]{:S(2)}, u32[]{:S(2)}) collective-permute-start(bf16[768,512]{1,0:T(8,128)(2,1)} %collective-permute-done.14.refs_5_), channel_id=1, source_target_pairs={{0,2},{2,0},{4,6},{6,4},{1,3},{3,1},{5,7},{7,5},{8,10},{10,8},{12,... | collective-permute-start | bytes 2359304 | tf_op jit(solution)/shard_map/ppermute | solution.py:74
  127.9 32.1 %collective-permute-start.15 = (bf16[768,512]{1,0:T(8,128)(2,1)}, bf16[768,512]{1,0:T(8,128)(2,1)S(1)}, u32[]{:S(2)}, u32[]{:S(2)}) collective-permute-start(bf16[768,512]{1,0:T(8,128)(2,1)} %collective-permute-done.13.refs_4_), channel_id=1, source_target_pairs={{0,2},{2,0},{4,6},{6,4},{1,3},{3,1},{5,7},{7,5},{8,10},{10,8},{12,... | collective-permute-start | bytes 2359304 | tf_op jit(solution)/shard_map/ppermute | solution.py:74
  (20 other events, 181.0 us)

commit v2 on v0

--- a/solution.py
+++ b/solution.py
@@ -1,9 +1,14 @@
+import functools
+
 import jax
 import jax.numpy as jnp
 from jax import lax
+from jax.experimental import pallas as pl
+from jax.experimental.pallas import tpu as pltpu
 from jax.sharding import PartitionSpec as P
 
 STEPS = 4
+PAUSE = 4.0
 
 
 def from_behind(value, axis, by):
@@ -17,7 +22,7 @@
     )
 
 
-def per_device(b_pairs, occ_index, vir_index, occ_depth, vir_height, omega):
+def ring_device(b_pairs, occ_index, vir_index, occ_depth, vir_height, omega):
     square = omega[0] * omega[0]
     n_row = lax.axis_size("row")
     n_col = lax.axis_size("col")
@@ -40,9 +45,301 @@
     return total.reshape(1, n_row, 1, sub_width, sub_width * n_col)
 
 
+def across_col(value):
+    return lax.ppermute(value, "col", [(0, 1), (1, 0)])
+
+
+def across_row(value):
+    return lax.ppermute(value, "row", [(i, (i + 2) % 4) for i in range(4)])
+
+
+def along_line(core_0, core_1):
+    pairs = [
+        (a * 4 + y * 2 + core, b * 4 + y * 2 + core)
+        for core, hops in enumerate((core_0, core_1))
+        for y in range(2)
+        for a, b in hops
+    ]
+    return lambda value: lax.ppermute(value, ("freq", "row"), pairs)
+
+
+OUTER = ((0, 1), (1, 0), (2, 3), (3, 2))
+INNER = ((0, 0), (1, 2), (2, 1), (3, 3))
+TO_ENDS = ((0, 1), (1, 0), (2, 3), (3, 2))
+STAY = ((0, 0), (1, 1), (2, 2), (3, 3))
+
+
+def other_core(value):
+    return lax.ppermute(value, "row", [(i, i ^ 1) for i in range(4)])
+
+
+def split_rows(value):
+    rows = []
+    for _ in range(3):
+        part = lax.reduce_precision(value, exponent_bits=8, mantissa_bits=7)
+        value = value - part
+        rows.append(part)
+    rows = jnp.stack(rows).astype(jnp.bfloat16)
+    return jnp.concatenate([rows, jnp.zeros((13, rows.shape[1]), jnp.bfloat16)])
+
+
+def join_rows(rows):
+    rows = rows[:3].astype(jnp.float32)
+    return rows[0] + (rows[1] + rows[2])
+
+
+def after(value, *earlier):
+    return lax.optimization_barrier((value, earlier))[0]
+
+
+def look_up(table, index):
+    hit = index[:, None] == lax.broadcasted_iota(jnp.int32, (1, table.shape[0]), 1)
+    return jnp.sum(jnp.where(hit, table[None, :], 0.0), axis=1)
+
+
+def tile_kernel(fresh, tiles, rights, lefts, write, *refs):
+    place, weight = refs[:2]
+    blocks = dict(zip([("r", i) for i in rights] + [("l", j) for j in lefts], refs[2:]))
+    if write:
+        acc, out, weighted, sem = refs[-4:]
+    else:
+        acc, weighted = refs[-2:]
+    sub = acc.shape[2]
+
+    def put(m):
+        i, j = tiles[m]
+        col = pl.multiple_of(((place[0] + j) % 2) * sub, sub)
+        window = out.at[place[1 + i], :, pl.ds(col, sub)]
+        return pltpu.make_async_copy(acc.at[j, i], window, sem.at[m])
+
+    ready = set()
+    for m, (i, j) in enumerate(tiles):
+        if j not in ready:
+            ready.add(j)
+            left = blocks["l", j]
+
+            @pl.loop(0, sub // 128)
+            def _(r):
+                rows = pl.ds(pl.multiple_of(r * 128, 128), 128)
+                value = left[rows, :].astype(jnp.float32) * weight[...]
+                weighted[j, rows, :] = value.astype(jnp.bfloat16)
+
+        part = contract_pairs(blocks["r", i][:sub, :], weighted[j])
+        if fresh:
+            acc[j, i] = part
+        else:
+            acc[j, i] += part
+        if write:
+            put(m).start()
+    if write:
+        for m in range(len(tiles)):
+            put(m).wait()
+
+
+def add_tiles(tiles, place, weight, right, left, acc, write=False, out=None, tokens=()):
+    sub, span = left[0].shape
+    fresh = acc is None
+    rights = sorted({i for i, _ in tiles})
+    lefts = sorted({j for _, j in tiles})
+    near = pl.BlockSpec(memory_space=pltpu.VMEM)
+    far = pl.BlockSpec(memory_space=pl.ANY)
+    operands = [place, weight]
+    in_specs = [pl.BlockSpec(memory_space=pltpu.SMEM), near]
+    for block in [right[i] for i in rights] + [left[j] for j in lefts]:
+        operands.append(pltpu.with_memory_space_constraint(block, pltpu.VMEM))
+        in_specs.append(near)
+    aliases = {}
+    if not fresh:
+        aliases[len(operands)] = 0
+        operands.append(pltpu.with_memory_space_constraint(acc, pltpu.VMEM))
+        in_specs.append(near)
+    if out is not None:
+        aliases[len(operands)] = 1
+        operands.append(out)
+        in_specs.append(far)
+    for token in tokens:
+        operands.append(token)
+        in_specs.append(far)
+    out_shape = [pltpu.VMEM((2, 4, sub, sub), jnp.float32)]
+    out_specs = [near]
+    scratch = [pltpu.VMEM((2, sub, span), jnp.bfloat16)]
+    if write:
+        out_shape.append(jax.ShapeDtypeStruct((4, sub, 2 * sub), jnp.float32))
+        out_specs.append(far)
+        scratch.append(pltpu.SemaphoreType.DMA((len(tiles),)))
+    return pl.pallas_call(
+        functools.partial(tile_kernel, fresh, tiles, rights, lefts, write),
+        out_shape=out_shape,
+        in_specs=in_specs,
+        out_specs=out_specs,
+        input_output_aliases=aliases,
+        scratch_shapes=scratch,
+        cost_estimate=pl.CostEstimate(
+            flops=2 * len(tiles) * sub * sub * span,
+            bytes_accessed=len(tiles) * sub * sub * 4 if write else 0,
+            transcendentals=0,
+        ),
+        compiler_params=pltpu.CompilerParams(vmem_limit_bytes=12 * 1024 * 1024),
+    )(*operands)
+
+
+def mark_kernel(block, rows, marked, sem):
+    copy = pltpu.make_async_copy(block, marked.at[: block.shape[0], :], sem)
+    copy.start()
+    marked[block.shape[0] :, :] = rows[...]
+    copy.wait()
+
+
+def mark(block, rows):
+    shape = (block.shape[0] + rows.shape[0], block.shape[1])
+    return pl.pallas_call(
+        mark_kernel,
+        out_shape=pltpu.VMEM(shape, block.dtype),
+        in_specs=[
+            pl.BlockSpec(memory_space=pl.ANY),
+            pl.BlockSpec(memory_space=pltpu.VMEM),
+        ],
+        out_specs=pl.BlockSpec(memory_space=pltpu.VMEM),
+        scratch_shapes=[pltpu.SemaphoreType.DMA],
+        compiler_params=pltpu.CompilerParams(vmem_limit_bytes=1024 * 1024),
+    )(block, rows)
+
+
+def pause_kernel(*refs):
+    refs[-1][...] = jnp.zeros_like(refs[-1])
+
+
+def pause(value, micros, tokens):
+    parts = value if isinstance(value, tuple) else (value,)
+    token = pl.pallas_call(
+        pause_kernel,
+        out_shape=jax.ShapeDtypeStruct((8, 128), jnp.float32),
+        in_specs=[pl.BlockSpec(memory_space=pltpu.VMEM)] * len(parts),
+        out_specs=pl.BlockSpec(memory_space=pltpu.VMEM),
+        cost_estimate=pl.CostEstimate(
+            flops=int(micros * 1e9),
+            bytes_accessed=int(micros * 3e6),
+            transcendentals=0,
+        ),
+        compiler_params=pltpu.CompilerParams(vmem_limit_bytes=4 * 1024 * 1024),
+    )(*[pltpu.with_memory_space_constraint(v, pltpu.VMEM) for v in parts])
+    tokens.append(token)
+    return after(value, token)
+
+
+def line_device(b_pairs, occ_index, vir_index, occ_depth, vir_height, omega):
+    group = lax.axis_index("freq")
+    row = lax.axis_index("row")
+    col = lax.axis_index("col")
+    core = row % 2
+    first = core == 0
+    end = (group == 0) | (group == 3)
+    sub, span = b_pairs.shape
+
+    own = b_pairs
+    x, y = [None] * 4, [None] * 4
+    tokens = []
+    x[0] = across_col(own)
+    y[0] = across_row(own)
+    own_swap = other_core(own)
+    hop_0 = along_line(OUTER, INNER)(after(own, own_swap))
+
+    occ_index, vir_index = after((occ_index, vir_index), own_swap)
+    own_gap = look_up(vir_height, vir_index) + look_up(occ_depth, occ_index)
+    marked = mark(own, split_rows(own_gap))
+    hop_1 = along_line(INNER, OUTER)(marked)
+    x[0], y[0] = pause((x[0], y[0]), PAUSE, tokens)
+
+    def pick(at_end, inside):
+        def rows(low, high):
+            pairs = [
+                [v[low:high] if v.shape[0] > low else v[:high - low] for v in pair]
+                for pair in (at_end, inside)
+            ]
+            if at_end is inside:
+                return jnp.where(first, *pairs[0])
+            return jnp.where(
+                end, jnp.where(first, *pairs[0]), jnp.where(first, *pairs[1])
+            )
+
+        block = rows(0, sub)
+        return block, rows(sub, marked.shape[0])
+
+    hop_2 = along_line(INNER, TO_ENDS)(after(hop_0, marked))
+    hop_0 = pause(hop_0, PAUSE, tokens)
+    hop_3 = along_line(TO_ENDS, INNER)(after(hop_1, x[0], y[0]))
+    pair = (hop_0, hop_1)
+    mine_1, rows_1 = pick(pair, pair)
+    x[1] = across_col(mine_1)
+    y[1] = across_row(mine_1)
+    x[1], y[1] = pause((x[1], y[1]), PAUSE, tokens)
+    swap_1 = other_core(mine_1)
+
+    hop_4 = along_line(TO_ENDS, STAY)(hop_2)
+    hop_2 = pause(hop_2, PAUSE, tokens)
+    hop_5 = along_line(STAY, TO_ENDS)(after(hop_3, x[1], y[1]))
+    hop_0, hop_1 = after((hop_0, hop_1), mine_1)
+    mine_2, rows_2 = pick((hop_3, hop_2), (hop_1, hop_0))
+    x[2] = across_col(mine_2)
+    y[2] = across_row(mine_2)
+    x[2], y[2] = pause((x[2], y[2]), PAUSE, tokens)
+    swap_2 = other_core(mine_2)
+
+    hop_4 = pause(hop_4, PAUSE, tokens)
+    hop_2, hop_3 = after((hop_2, hop_3), mine_2)
+    mine_3, rows_3 = pick((hop_4, hop_5), (hop_2, hop_3))
+    x[3] = across_col(mine_3)
+    y[3] = across_row(mine_3)
+    swap_3 = other_core(mine_3)
+
+    def weigh(gap):
+        return (4.0 * gap / (gap * gap + omega[0] * omega[0]))[None, :]
+
+    def gap_of(rows, holder):
+        return join_rows(jnp.where(core == holder, rows, other_core(rows)))
+
+    rows_1 = after(rows_1, mine_1)
+    rows_2 = after(rows_2, mine_2)
+    rows_3 = after(rows_3, mine_3)
+    weight = [
+        weigh(own_gap),
+        weigh(gap_of(rows_1, 1)),
+        weigh(gap_of(rows_2, 0)),
+        weigh(gap_of(rows_3, 1)),
+    ]
+    mine = [own, mine_1, mine_2, mine_3]
+    swap = [own_swap, swap_1, swap_2, swap_3]
+
+    place = jnp.stack([col, row, row ^ 1, row ^ 2, row ^ 3]).astype(jnp.int32)
+    tiles = tuple((i, j) for j in range(2) for i in range(4))
+    acc = None
+    for k in range(3):
+        place = after(place, mine[min(k + 2, 3)])
+        right = (mine[k], swap[k], y[k], other_core(y[k]))
+        (acc,) = add_tiles(tiles, place, weight[k], right, (mine[k], x[k]), acc)
+    right = (mine[3], swap[3])
+    acc, out = add_tiles(
+        ((0, 0), (1, 0)), place, weight[3], right, (mine[3],), acc, write=True
+    )
+    x[3], y[3] = after((x[3], y[3]), acc)
+    right = (mine[3], swap[3], y[3], other_core(y[3]))
+    acc, out = add_tiles(
+        ((0, 1), (1, 1), (2, 1), (2, 0)),
+        place, weight[3], right, (mine[3], x[3]), acc, write=True, out=out,
+    )
+    _, out = add_tiles(
+        ((3, 1), (3, 0)),
+        place, weight[3], right, (mine[3], x[3]), acc, write=True, out=out,
+        tokens=tokens,
+    )
+    return out.reshape(1, 4, 1, sub, 2 * sub)
+
+
 def solution(mesh):
     in_specs = (P(("row", "col"), "freq"), P("freq"), P("freq"), P(), P(), P("freq"))
     out_specs = P("freq", None, "col", None, "row")
+    shape = tuple(mesh.shape[axis] for axis in ("freq", "row", "col"))
+    per_device = line_device if shape == (4, 4, 2) else ring_device
     return jax.shard_map(
         per_device, mesh=mesh, in_specs=in_specs, out_specs=out_specs, check_vma=False
     )

time: 414 us -> 122 us (0.29)
  waiting for transfers between devices: 280 us -> 40.3 us
  matrix products: 60.7 us -> 0 us
  local copies, waits for them, and re-layouts: 45.3 us -> 1.22 us
  Pallas kernels: 0 us -> 34.7 us
  starting transfers between devices: 11.2 us -> 37.4 us
  between operations: 15.8 us -> 1.11 us
  other arithmetic: 0.81 us -> 6.59 us
    ppermute x12 -> x25, waiting for transfers between devices: 223 us -> 40.3 us  [the longest x4 23.6 us: across_row(): return lax.ppermute(value, 'row', [(i, (i + 2) % 4) for i in range(4)])]
    dot_general x4 -> x0, matrix products: 60.7 us -> none  [contract_pairs(): lax.dot_general(left, right, (((1,), (1,)), ((), ())), preferred_element_...]
    all_gather x2 -> x0, waiting for transfers between devices: 56.1 us -> none  [the longest x1 32.9 us: per_device(): right = lax.all_gather(b_pairs, 'row', axis=0, tiled=True)]
    pallas_call x0 -> x13, Pallas kernels: none -> 34.7 us  [the longest x6 33.5 us: add_tiles(): pl.pallas_call(functools.partial(tile_kernel, fresh, tiles, rights, lefts...]
    gather x8 -> x0, local copies, waits for them, and re-layouts: 26.7 us -> none  [per_device(): gap = jnp.take(vir_height, vir_part) + jnp.take(occ_depth, occ_part)]
    ppermute x12 -> x25, starting transfers between devices: 11.1 us -> 37.4 us  [the longest x11 14.8 us: other_core(): return lax.ppermute(value, 'row', [(i, i ^ 1) for i in range(4)])]
    reshape x1 -> x0, local copies, waits for them, and re-layouts: 18.6 us -> none  [per_device(): return total.reshape(1, n_row, 1, sub_width, sub_width * n_col)]
  transfers between devices with their start and end apart: 14 -> 25, of which waited for: 8 -> 9; matrix products, arithmetic and copies ran while one was open for 15% -> 5% of each run, Pallas kernels for 0% -> 25%
where the time goes in v2:
time: 122 us; the launch traced here: 121 us
  waiting for transfers between devices  40.3 us (33%)
  starting transfers between devices  37.4 us (31%)
  Pallas kernels  34.7 us (28%)
  other arithmetic  6.59 us (5%)
  local copies, waits for them, and re-layouts  1.22 us (1%)
    pallas_call x6, Pallas kernels, add_tiles(): pl.pallas_call(functools.partial(tile_kernel, fresh, tiles, rights, lefts...  33.5 us
    ppermute x4, waiting for transfers between devices, across_row(): return lax.ppermute(value, 'row', [(i, (i + 2) % 4) for i in range(4)])  23.6 us
    ppermute x11, starting transfers between devices, other_core(): return lax.ppermute(value, 'row', [(i, i ^ 1) for i in range(4)])  14.8 us
    ppermute x6, starting transfers between devices, along_line(): return lambda value: lax.ppermute(value, ('freq', 'row'), pairs)  13.4 us
    ppermute x4, waiting for transfers between devices, across_col(): return lax.ppermute(value, 'col', [(0, 1), (1, 0)])  10.8 us
    ppermute x4, starting transfers between devices, across_col(): return lax.ppermute(value, 'col', [(0, 1), (1, 0)])  5.08 us
    ppermute x6, waiting for transfers between devices, along_line(): return lambda value: lax.ppermute(value, ('freq', 'row'), pairs)  4.45 us
    ppermute x4, starting transfers between devices, across_row(): return lax.ppermute(value, 'row', [(i, (i + 2) % 4) for i in range(4)])  4.17 us
  transfers between devices with their start and end apart: 25, of which 9 were waited for; matrix products, arithmetic and copies ran while one was open for 5% of the time, Pallas kernels for 25%

profile of v2, /device:TPU:0, one launch (start us, length us, event | category | flops | bytes accessed | tf_op | source)
XLA Modules:
  0.0 121.4 jit_solution(17437554666542370247)
XLA Ops:
  2.6 4.8 %collective-permute-start.5 = (bf16[768,512]{1,0:T(8,128)(2,1)}, bf16[768,512]{1,0:T(8,128)(2,1)S(1)}, u32[]{:S(2)}, u32[]{:S(2)}) collective-permute-start(bf16[768,512]{1,0:T(8,128)(2,1)} %refs_6_.1), channel_id=1, source_target_pairs={{0,8},{8,0},{16,24},{24,16},{4,12},{12,4},{20,28},{28,20},{2,2},{1... | collective-permute-start | bytes 2359304 | tf_op jit(solution)/shard_map/ppermute | solution.py:63
  10.9 1.6 %collective-permute-start.1 = (bf16[784,512]{1,0:T(8,128)(2,1)S(1)}, bf16[784,512]{1,0:T(8,128)(2,1)}, u32[]{:S(2)}, u32[]{:S(2)}) collective-permute-start(bf16[784,512]{1,0:T(8,128)(2,1)S(1)} %shard_map.64), channel_id=1, source_target_pairs={{0,0},{8,16},{16,8},{24,24},{4,4},{12,20},{20,12},{28,28},{2,10},{... | collective-permute-start | bytes 2408456 | tf_op jit(solution)/shard_map/ppermute | solution.py:63
  12.5 1.5 %collective-permute-start.3 = (bf16[768,512]{1,0:T(8,128)(2,1)}, bf16[768,512]{1,0:T(8,128)(2,1)S(1)}, u32[]{:S(2)}, u32[]{:S(2)}) collective-permute-start(bf16[768,512]{1,0:T(8,128)(2,1)} %refs_6_.1), channel_id=1, source_target_pairs={{0,4},{2,6},{4,0},{6,2},{1,5},{3,7},{5,1},{7,3},{8,12},{10,14},{12... | collective-permute-start | bytes 2359304 | tf_op jit(solution)/shard_map/ppermute | solution.py:53
  14.0 1.5 %collective-permute-start.2 = (bf16[768,512]{1,0:T(8,128)(2,1)}, bf16[768,512]{1,0:T(8,128)(2,1)}, u32[]{:S(2)}, u32[]{:S(2)}) collective-permute-start(bf16[768,512]{1,0:T(8,128)(2,1)} %refs_6_.1), channel_id=1, source_target_pairs={{0,1},{1,0},{2,3},{3,2},{4,5},{5,4},{6,7},{7,6},{8,9},{9,8},{10,11... | collective-permute-start | bytes 2359304 | tf_op jit(solution)/shard_map/ppermute | solution.py:49
  15.6 4.4 %collective-permute-done.5.refs_0_ = bf16[768,512]{1,0:T(8,128)(2,1)S(1)} collective-permute-done((bf16[768,512]{1,0:T(8,128)(2,1)}, bf16[768,512]{1,0:T(8,128)(2,1)S(1)}, u32[]{:S(2)}, u32[]{:S(2)}) %collective-permute-start.5) | collective-permute-done | bytes 786464 | tf_op jit(solution)/shard_map/ppermute | solution.py:63
  22.7 5.8 %collective-permute-start.20 = (bf16[16,512]{1,0:T(8,128)(2,1)S(1)}, bf16[16,512]{1,0:T(8,128)(2,1)S(1)}, u32[]{:S(2)}, u32[]{:S(2)}) collective-permute-start(bf16[16,512]{1,0:T(8,128)(2,1)S(1)} %slice_select_fusion.3), channel_id=1, source_target_pairs={{0,2},{2,0},{4,6},{6,4},{1,3},{3,1},{5,7},{7,5},{8,10},{10,8},{12,... | collective-permute-start | bytes 49160 | tf_op jit(solution)/shard_map/ppermute | solution.py:73
  28.4 4.1 %collective-permute-done.3.refs_1_.refs_4_ = bf16[768,512]{1,0:T(8,128)(2,1)S(1)} collective-permute-done((bf16[768,512]{1,0:T(8,128)(2,1)}, bf16[768,512]{1,0:T(8,128)(2,1)S(1)}, u32[]{:S(2)}, u32[]{:S(2)}) %collective-permute-start.3) | collective-permute-done | bytes 786464 | tf_op jit(solution)/shard_map/ppermute | solution.py:53
  32.5 1.9 %collective-permute-done.2.refs_0_.refs_7_ = bf16[768,512]{1,0:T(8,128)(2,1)} collective-permute-done((bf16[768,512]{1,0:T(8,128)(2,1)}, bf16[768,512]{1,0:T(8,128)(2,1)}, u32[]{:S(2)}, u32[]{:S(2)}) %collective-permute-start.2) | collective-permute-done | bytes 786464 | tf_op jit(solution)/shard_map/ppermute | solution.py:49
  36.2 1.5 %collective-permute-start.8 = (bf16[768,512]{1,0:T(8,128)(2,1)S(1)}, bf16[768,512]{1,0:T(8,128)(2,1)S(1)}, u32[]{:S(2)}, u32[]{:S(2)}) collective-permute-start(bf16[768,512]{1,0:T(8,128)(2,1)S(1)} %slice_select_fusion.1.refs_2_.refs_6_), channel_id=1, source_target_pairs={{0,1},{1,0},{2,3},{3,2},{4,5},{5,4},{6,7},{7,6},{8,9},{9,8},{10,11... | collective-permute-start | bytes 2359304 | tf_op jit(solution)/shard_map/ppermute | solution.py:49
  37.7 2.7 %collective-permute-start.4 = (bf16[784,512]{1,0:T(8,128)(2,1)}, bf16[784,512]{1,0:T(8,128)(2,1)S(1)}, u32[]{:S(2)}, u32[]{:S(2)}) collective-permute-start(bf16[784,512]{1,0:T(8,128)(2,1)} %collective-permute-done.1), channel_id=1, source_target_pairs={{0,8},{8,0},{16,24},{24,16},{4,12},{12,4},{20,28},{28,20},{2,2},{1... | collective-permute-start | bytes 2408456 | tf_op jit(solution)/shard_map/ppermute | solution.py:63
  40.5 15.0 %collective-permute-done.9.refs_1_.refs_4_ = bf16[768,512]{1,0:T(8,128)(2,1)S(1)} collective-permute-done((bf16[768,512]{1,0:T(8,128)(2,1)S(1)}, bf16[768,512]{1,0:T(8,128)(2,1)S(1)}, u32[]{:S(2)}, u32[]{:S(2)}) %collective-permute-start.9) | collective-permute-done | bytes 786464 | tf_op jit(solution)/shard_map/ppermute | solution.py:53
  55.5 2.9 %collective-permute-start.7 = (bf16[768,512]{1,0:T(8,128)(2,1)S(1)}, bf16[768,512]{1,0:T(8,128)(2,1)S(1)}, u32[]{:S(2)}, u32[]{:S(2)}) collective-permute-start(bf16[768,512]{1,0:T(8,128)(2,1)S(1)} %collective-permute-done.6.refs_0_), channel_id=1, source_target_pairs={{0,8},{8,0},{16,24},{24,16},{4,12},{12,4},{20,28},{28,20},{2,2},{1... | collective-permute-start | bytes 2359304 | tf_op jit(solution)/shard_map/ppermute | solution.py:63
  60.3 1.5 %collective-permute-start.17 = (bf16[768,512]{1,0:T(8,128)(2,1)S(1)}, bf16[768,512]{1,0:T(8,128)(2,1)S(1)}, u32[]{:S(2)}, u32[]{:S(2)}) collective-permute-start(bf16[768,512]{1,0:T(8,128)(2,1)S(1)} %fusion.1.refs_2_.refs_6_), channel_id=1, source_target_pairs={{0,1},{1,0},{2,3},{3,2},{4,5},{5,4},{6,7},{7,6},{8,9},{9,8},{10,11... | collective-permute-start | bytes 2359304 | tf_op jit(solution)/shard_map/ppermute | solution.py:49
  62.6 6.7 %shard_map.71.refs_8_ = f32[2,4,768,768]{3,2,1,0:T(8,128)S(1)} custom-call(s32[5]{0:T(128)S(1)} %stack.30.refs_0_, f32[1,512]{1,0:T(1,128)S(1)} %get-tuple-element.69.refs_1_, bf16[768,512]{1,0:T(8,128)(2,1)S(1)} %copy-done.1, bf16[768,512]{1,0:T(8,128)(2,1)S(1)} %collective-permute-done.refs_3_, ...), custom_call_target="tpu_custom_call" | custom-call | flops 4831838208 | tf_op jit(solution)/shard_map/pallas_call | solution.py:170
  70.2 2.5 %collective-permute-start.22 = (bf16[768,512]{1,0:T(8,128)(2,1)S(1)}, bf16[768,512]{1,0:T(8,128)(2,1)S(1)}, u32[]{:S(2)}, u32[]{:S(2)}) collective-permute-start(bf16[768,512]{1,0:T(8,128)(2,1)S(1)} %collective-permute-done.9.refs_1_.refs_4_), channel_id=1, source_target_pairs={{0,2},{2,0},{4,6},{6,4},{1,3},{3,1},{5,7},{7,5},{8,10},{10,8},{12,... | collective-permute-start | bytes 2359304 | tf_op jit(solution)/shard_map/ppermute | solution.py:73
  72.7 4.0 %collective-permute-done.18.refs_1_.refs_4_ = bf16[768,512]{1,0:T(8,128)(2,1)S(1)} collective-permute-done((bf16[768,512]{1,0:T(8,128)(2,1)S(1)}, bf16[768,512]{1,0:T(8,128)(2,1)S(1)}, u32[]{:S(2)}, u32[]{:S(2)}) %collective-permute-start.18) | collective-permute-done | bytes 786464 | tf_op jit(solution)/shard_map/ppermute | solution.py:53
  77.4 5.7 %collective-permute-start.14 = (bf16[768,512]{1,0:T(8,128)(2,1)S(1)}, bf16[768,512]{1,0:T(8,128)(2,1)S(1)}, u32[]{:S(2)}, u32[]{:S(2)}) collective-permute-start(bf16[768,512]{1,0:T(8,128)(2,1)S(1)} %fusion.refs_2_.refs_4_.refs_5_.refs_3_), channel_id=1, source_target_pairs={{0,2},{2,0},{4,6},{6,4},{1,3},{3,1},{5,7},{7,5},{8,10},{10,8},{12,... | collective-permute-start | bytes 2359304 | tf_op jit(solution)/shard_map/ppermute | solution.py:73
  83.1 1.6 %collective-permute-start.13 = (bf16[768,512]{1,0:T(8,128)(2,1)S(1)}, bf16[768,512]{1,0:T(8,128)(2,1)S(1)}, u32[]{:S(2)}, u32[]{:S(2)}) collective-permute-start(bf16[768,512]{1,0:T(8,128)(2,1)S(1)} %fusion.refs_2_.refs_4_.refs_5_.refs_3_), channel_id=1, source_target_pairs={{0,4},{2,6},{4,0},{6,2},{1,5},{3,7},{5,1},{7,3},{8,12},{10,14},{12... | collective-permute-start | bytes 2359304 | tf_op jit(solution)/shard_map/ppermute | solution.py:53
  84.7 6.5 %shard_map.72.refs_8_ = f32[2,4,768,768]{3,2,1,0:T(8,128)S(1)} custom-call(s32[5]{0:T(128)S(1)} %stack.30.refs_0_, f32[1,512]{1,0:T(1,128)S(1)} %add_divide_fusion.1.refs_1_, bf16[768,512]{1,0:T(8,128)(2,1)S(1)} %slice_select_fusion.1.refs_2_.refs_6_, bf16[768,512]{1,0:T(8,128)(2,1)S(1)} %collective-permute-done.21.refs_3_, ...), custom_call_target="tpu_custom_call", output_to_operand_aliasing={{}: (8, {})} | custom-call | flops 4831838208 | tf_op jit(solution)/shard_map/pallas_call | solution.py:170
  91.8 6.3 %shard_map.73.refs_5_ = f32[2,4,768,768]{3,2,1,0:T(8,128)S(1)} custom-call(s32[5]{0:T(128)S(1)} %stack.30.refs_0_, f32[1,512]{1,0:T(1,128)S(1)} %add_divide_fusion.2.refs_1_, bf16[768,512]{1,0:T(8,128)(2,1)S(1)} %fusion.1.refs_2_.refs_6_, bf16[768,512]{1,0:T(8,128)(2,1)S(1)} %collective-permute-done.16.refs_3_, ...), custom_call_target="tpu_custom_call", output_to_operand_aliasing={{}: (8, {})} | custom-call | flops 4831838208 | tf_op jit(solution)/shard_map/pallas_call | solution.py:170
  98.1 4.0 %shard_map.74 = (f32[2,4,768,768]{3,2,1,0:T(8,128)S(1)}, f32[4,768,1536]{2,1,0:T(8,128)}) custom-call(s32[5]{0:T(128)S(1)} %stack.30.refs_0_, f32[1,512]{1,0:T(1,128)S(1)} %add_divide_fusion.3.refs_1_, bf16[768,512]{1,0:T(8,128)(2,1)S(1)} %fusion.refs_2_.refs_4_.refs_5_.refs_3_, ...), custom_call_target="tpu_custom_call", output_to_operand_aliasing={{0}: (5, {})} | custom-call | flops 1207959552 | bytes 4718592 | tf_op jit(solution)/shard_map/pallas_call | solution.py:170
  102.6 8.5 %collective-permute-done.12.refs_6_.refs_4_ = bf16[768,512]{1,0:T(8,128)(2,1)S(1)} collective-permute-done((bf16[768,512]{1,0:T(8,128)(2,1)S(1)}, bf16[768,512]{1,0:T(8,128)(2,1)S(1)}, u32[]{:S(2)}, u32[]{:S(2)}) %collective-permute-start.12) | collective-permute-done | bytes 786464 | tf_op jit(solution)/shard_map/ppermute | solution.py:49
  111.2 5.7 %shard_map.75 = (f32[2,4,768,768]{3,2,1,0:T(8,128)S(1)}, f32[4,768,1536]{2,1,0:T(8,128)}) custom-call(s32[5]{0:T(128)S(1)} %stack.30.refs_0_, f32[1,512]{1,0:T(1,128)S(1)} %add_divide_fusion.3.refs_1_, bf16[768,512]{1,0:T(8,128)(2,1)S(1)} %fusion.refs_2_.refs_4_.refs_5_.refs_3_, ...), custom_call_target="tpu_custom_call", output_to_operand_aliasing={{0}: (7, {}), {1}: (8, {})} | custom-call | flops 2415919104 | bytes 9437184 | tf_op jit(solution)/shard_map/pallas_call | solution.py:170
  116.9 4.3 %shard_map.76 = (f32[2,4,768,768]{3,2,1,0:T(8,128)S(1)}, f32[4,768,1536]{2,1,0:T(8,128)}) custom-call(s32[5]{0:T(128)S(1)} %stack.30.refs_0_, f32[1,512]{1,0:T(1,128)S(1)} %add_divide_fusion.3.refs_1_, bf16[768,512]{1,0:T(8,128)(2,1)S(1)} %collective-permute-done.24.refs_2_, ...), custom_call_target="tpu_custom_call", output_to_operand_aliasing={{0}: (5, {}), {1}: (6, {})} | custom-call | flops 1207959552 | bytes 4718592 | tf_op jit(solution)/shard_map/pallas_call | solution.py:170
  (61 shorter events, 15.4 us)
Async XLA Ops:
  2.6 17.4 %collective-permute-start.5 = (bf16[768,512]{1,0:T(8,128)(2,1)}, bf16[768,512]{1,0:T(8,128)(2,1)S(1)}, u32[]{:S(2)}, u32[]{:S(2)}) collective-permute-start(bf16[768,512]{1,0:T(8,128)(2,1)} %refs_6_.1), channel_id=1, source_target_pairs={{0,8},{8,0},{16,24},{24,16},{4,12},{12,4},{20,28},{28,20},{2,2},{1... | collective-permute-start | bytes 2359304 | tf_op jit(solution)/shard_map/ppermute | solution.py:63
  10.9 9.8 %collective-permute-start.1 = (bf16[784,512]{1,0:T(8,128)(2,1)S(1)}, bf16[784,512]{1,0:T(8,128)(2,1)}, u32[]{:S(2)}, u32[]{:S(2)}) collective-permute-start(bf16[784,512]{1,0:T(8,128)(2,1)S(1)} %shard_map.64), channel_id=1, source_target_pairs={{0,0},{8,16},{16,8},{24,24},{4,4},{12,20},{20,12},{28,28},{2,10},{... | collective-permute-start | bytes 2408456 | tf_op jit(solution)/shard_map/ppermute | solution.py:63
  12.5 20.1 %collective-permute-start.3 = (bf16[768,512]{1,0:T(8,128)(2,1)}, bf16[768,512]{1,0:T(8,128)(2,1)S(1)}, u32[]{:S(2)}, u32[]{:S(2)}) collective-permute-start(bf16[768,512]{1,0:T(8,128)(2,1)} %refs_6_.1), channel_id=1, source_target_pairs={{0,4},{2,6},{4,0},{6,2},{1,5},{3,7},{5,1},{7,3},{8,12},{10,14},{12... | collective-permute-start | bytes 2359304 | tf_op jit(solution)/shard_map/ppermute | solution.py:53
  14.0 20.4 %collective-permute-start.2 = (bf16[768,512]{1,0:T(8,128)(2,1)}, bf16[768,512]{1,0:T(8,128)(2,1)}, u32[]{:S(2)}, u32[]{:S(2)}) collective-permute-start(bf16[768,512]{1,0:T(8,128)(2,1)} %refs_6_.1), channel_id=1, source_target_pairs={{0,1},{1,0},{2,3},{3,2},{4,5},{5,4},{6,7},{7,6},{8,9},{9,8},{10,11... | collective-permute-start | bytes 2359304 | tf_op jit(solution)/shard_map/ppermute | solution.py:49
  20.0 20.4 %collective-permute-start.6 = (bf16[768,512]{1,0:T(8,128)(2,1)S(1)}, bf16[768,512]{1,0:T(8,128)(2,1)S(1)}, u32[]{:S(2)}, u32[]{:S(2)}) collective-permute-start(bf16[768,512]{1,0:T(8,128)(2,1)S(1)} %collective-permute-done.5.refs_0_), channel_id=1, source_target_pairs={{0,0},{8,16},{16,8},{24,24},{4,4},{12,20},{20,12},{28,28},{2,10},{... | collective-permute-start | bytes 2359304 | tf_op jit(solution)/shard_map/ppermute | solution.py:63
  22.7 15.0 %collective-permute-start.20 = (bf16[16,512]{1,0:T(8,128)(2,1)S(1)}, bf16[16,512]{1,0:T(8,128)(2,1)S(1)}, u32[]{:S(2)}, u32[]{:S(2)}) collective-permute-start(bf16[16,512]{1,0:T(8,128)(2,1)S(1)} %slice_select_fusion.3), channel_id=1, source_target_pairs={{0,2},{2,0},{4,6},{6,4},{1,3},{3,1},{5,7},{7,5},{8,10},{10,8},{12,... | collective-permute-start | bytes 49160 | tf_op jit(solution)/shard_map/ppermute | solution.py:73
  35.5 27.0 %collective-permute-start.23 = (bf16[768,512]{1,0:T(8,128)(2,1)S(1)}, bf16[768,512]{1,0:T(8,128)(2,1)S(1)}, u32[]{:S(2)}, u32[]{:S(2)}) collective-permute-start(bf16[768,512]{1,0:T(8,128)(2,1)S(1)} %collective-permute-done.3.refs_1_.refs_4_), channel_id=1, source_target_pairs={{0,2},{2,0},{4,6},{6,4},{1,3},{3,1},{5,7},{7,5},{8,10},{10,8},{12,... | collective-permute-start | bytes 2359304 | tf_op jit(solution)/shard_map/ppermute | solution.py:73
  35.7 19.8 %collective-permute-start.9 = (bf16[768,512]{1,0:T(8,128)(2,1)S(1)}, bf16[768,512]{1,0:T(8,128)(2,1)S(1)}, u32[]{:S(2)}, u32[]{:S(2)}) collective-permute-start(bf16[768,512]{1,0:T(8,128)(2,1)S(1)} %slice_select_fusion.1.refs_2_.refs_6_), channel_id=1, source_target_pairs={{0,4},{2,6},{4,0},{6,2},{1,5},{3,7},{5,1},{7,3},{8,12},{10,14},{12... | collective-permute-start | bytes 2359304 | tf_op jit(solution)/shard_map/ppermute | solution.py:53
  36.2 22.2 %collective-permute-start.8 = (bf16[768,512]{1,0:T(8,128)(2,1)S(1)}, bf16[768,512]{1,0:T(8,128)(2,1)S(1)}, u32[]{:S(2)}, u32[]{:S(2)}) collective-permute-start(bf16[768,512]{1,0:T(8,128)(2,1)S(1)} %slice_select_fusion.1.refs_2_.refs_6_), channel_id=1, source_target_pairs={{0,1},{1,0},{2,3},{3,2},{4,5},{5,4},{6,7},{7,6},{8,9},{9,8},{10,11... | collective-permute-start | bytes 2359304 | tf_op jit(solution)/shard_map/ppermute | solution.py:49
  37.7 20.7 %collective-permute-start.4 = (bf16[784,512]{1,0:T(8,128)(2,1)}, bf16[784,512]{1,0:T(8,128)(2,1)S(1)}, u32[]{:S(2)}, u32[]{:S(2)}) collective-permute-start(bf16[784,512]{1,0:T(8,128)(2,1)} %collective-permute-done.1), channel_id=1, source_target_pairs={{0,8},{8,0},{16,24},{24,16},{4,12},{12,4},{20,28},{28,20},{2,2},{1... | collective-permute-start | bytes 2408456 | tf_op jit(solution)/shard_map/ppermute | solution.py:63
  40.4 42.6 %collective-permute-start.21 = (bf16[768,512]{1,0:T(8,128)(2,1)S(1)}, bf16[768,512]{1,0:T(8,128)(2,1)S(1)}, u32[]{:S(2)}, u32[]{:S(2)}) collective-permute-start(bf16[768,512]{1,0:T(8,128)(2,1)S(1)} %slice_select_fusion.1.refs_2_.refs_6_), channel_id=1, source_target_pairs={{0,2},{2,0},{4,6},{6,4},{1,3},{3,1},{5,7},{7,5},{8,10},{10,8},{12,... | collective-permute-start | bytes 2359304 | tf_op jit(solution)/shard_map/ppermute | solution.py:73
  55.5 14.7 %collective-permute-start.7 = (bf16[768,512]{1,0:T(8,128)(2,1)S(1)}, bf16[768,512]{1,0:T(8,128)(2,1)S(1)}, u32[]{:S(2)}, u32[]{:S(2)}) collective-permute-start(bf16[768,512]{1,0:T(8,128)(2,1)S(1)} %collective-permute-done.6.refs_0_), channel_id=1, source_target_pairs={{0,8},{8,0},{16,24},{24,16},{4,12},{12,4},{20,28},{28,20},{2,2},{1... | collective-permute-start | bytes 2359304 | tf_op jit(solution)/shard_map/ppermute | solution.py:63
  59.8 16.9 %collective-permute-start.18 = (bf16[768,512]{1,0:T(8,128)(2,1)S(1)}, bf16[768,512]{1,0:T(8,128)(2,1)S(1)}, u32[]{:S(2)}, u32[]{:S(2)}) collective-permute-start(bf16[768,512]{1,0:T(8,128)(2,1)S(1)} %fusion.1.refs_2_.refs_6_), channel_id=1, source_target_pairs={{0,4},{2,6},{4,0},{6,2},{1,5},{3,7},{5,1},{7,3},{8,12},{10,14},{12... | collective-permute-start | bytes 2359304 | tf_op jit(solution)/shard_map/ppermute | solution.py:53
  60.3 16.7 %collective-permute-start.17 = (bf16[768,512]{1,0:T(8,128)(2,1)S(1)}, bf16[768,512]{1,0:T(8,128)(2,1)S(1)}, u32[]{:S(2)}, u32[]{:S(2)}) collective-permute-start(bf16[768,512]{1,0:T(8,128)(2,1)S(1)} %fusion.1.refs_2_.refs_6_), channel_id=1, source_target_pairs={{0,1},{1,0},{2,3},{3,2},{4,5},{5,4},{6,7},{7,6},{8,9},{9,8},{10,11... | collective-permute-start | bytes 2359304 | tf_op jit(solution)/shard_map/ppermute | solution.py:49
  62.5 6.8 %collective-permute-start.15 = (bf16[16,512]{1,0:T(8,128)(2,1)S(1)}, bf16[16,512]{1,0:T(8,128)(2,1)S(1)}, u32[]{:S(2)}, u32[]{:S(2)}) collective-permute-start(bf16[16,512]{1,0:T(8,128)(2,1)S(1)} %fusion.7), channel_id=1, source_target_pairs={{0,2},{2,0},{4,6},{6,4},{1,3},{3,1},{5,7},{7,5},{8,10},{10,8},{12,... | collective-permute-start | bytes 49160 | tf_op jit(solution)/shard_map/ppermute | solution.py:73
  69.4 7.8 %collective-permute-start.10 = (bf16[784,512]{1,0:T(8,128)(2,1)S(1)}, bf16[784,512]{1,0:T(8,128)(2,1)S(1)}, u32[]{:S(2)}, u32[]{:S(2)}) collective-permute-start(bf16[784,512]{1,0:T(8,128)(2,1)S(1)} %collective-permute-done.4), channel_id=1, source_target_pairs={{0,0},{8,8},{16,16},{24,24},{4,4},{12,12},{20,20},{28,28},{2,10},{... | collective-permute-start | bytes 2408456 | tf_op jit(solution)/shard_map/ppermute | solution.py:63
  70.2 14.5 %collective-permute-start.22 = (bf16[768,512]{1,0:T(8,128)(2,1)S(1)}, bf16[768,512]{1,0:T(8,128)(2,1)S(1)}, u32[]{:S(2)}, u32[]{:S(2)}) collective-permute-start(bf16[768,512]{1,0:T(8,128)(2,1)S(1)} %collective-permute-done.9.refs_1_.refs_4_), channel_id=1, source_target_pairs={{0,2},{2,0},{4,6},{6,4},{1,3},{3,1},{5,7},{7,5},{8,10},{10,8},{12,... | collective-permute-start | bytes 2359304 | tf_op jit(solution)/shard_map/ppermute | solution.py:73
  76.7 15.1 %collective-permute-start.16 = (bf16[768,512]{1,0:T(8,128)(2,1)S(1)}, bf16[768,512]{1,0:T(8,128)(2,1)S(1)}, u32[]{:S(2)}, u32[]{:S(2)}) collective-permute-start(bf16[768,512]{1,0:T(8,128)(2,1)S(1)} %fusion.1.refs_2_.refs_6_), channel_id=1, source_target_pairs={{0,2},{2,0},{4,6},{6,4},{1,3},{3,1},{5,7},{7,5},{8,10},{10,8},{12,... | collective-permute-start | bytes 2359304 | tf_op jit(solution)/shard_map/ppermute | solution.py:73
  77.1 14.7 %collective-permute-start.19 = (bf16[768,512]{1,0:T(8,128)(2,1)S(1)}, bf16[768,512]{1,0:T(8,128)(2,1)S(1)}, u32[]{:S(2)}, u32[]{:S(2)}) collective-permute-start(bf16[768,512]{1,0:T(8,128)(2,1)S(1)} %collective-permute-done.18.refs_1_.refs_4_), channel_id=1, source_target_pairs={{0,2},{2,0},{4,6},{6,4},{1,3},{3,1},{5,7},{7,5},{8,10},{10,8},{12,... | collective-permute-start | bytes 2359304 | tf_op jit(solution)/shard_map/ppermute | solution.py:73
  77.4 20.7 %collective-permute-start.14 = (bf16[768,512]{1,0:T(8,128)(2,1)S(1)}, bf16[768,512]{1,0:T(8,128)(2,1)S(1)}, u32[]{:S(2)}, u32[]{:S(2)}) collective-permute-start(bf16[768,512]{1,0:T(8,128)(2,1)S(1)} %fusion.refs_2_.refs_4_.refs_5_.refs_3_), channel_id=1, source_target_pairs={{0,2},{2,0},{4,6},{6,4},{1,3},{3,1},{5,7},{7,5},{8,10},{10,8},{12,... | collective-permute-start | bytes 2359304 | tf_op jit(solution)/shard_map/ppermute | solution.py:73
  83.1 19.5 %collective-permute-start.13 = (bf16[768,512]{1,0:T(8,128)(2,1)S(1)}, bf16[768,512]{1,0:T(8,128)(2,1)S(1)}, u32[]{:S(2)}, u32[]{:S(2)}) collective-permute-start(bf16[768,512]{1,0:T(8,128)(2,1)S(1)} %fusion.refs_2_.refs_4_.refs_5_.refs_3_), channel_id=1, source_target_pairs={{0,4},{2,6},{4,0},{6,2},{1,5},{3,7},{5,1},{7,3},{8,12},{10,14},{12... | collective-permute-start | bytes 2359304 | tf_op jit(solution)/shard_map/ppermute | solution.py:53
  84.7 6.5 %collective-permute-start.11 = (bf16[16,512]{1,0:T(8,128)(2,1)S(1)}, bf16[16,512]{1,0:T(8,128)(2,1)S(1)}, u32[]{:S(2)}, u32[]{:S(2)}) collective-permute-start(bf16[16,512]{1,0:T(8,128)(2,1)S(1)} %fusion.8), channel_id=1, source_target_pairs={{0,2},{2,0},{4,6},{6,4},{1,3},{3,1},{5,7},{7,5},{8,10},{10,8},{12,... | collective-permute-start | bytes 49160 | tf_op jit(solution)/shard_map/ppermute | solution.py:73
  91.1 20.0 %collective-permute-start.12 = (bf16[768,512]{1,0:T(8,128)(2,1)S(1)}, bf16[768,512]{1,0:T(8,128)(2,1)S(1)}, u32[]{:S(2)}, u32[]{:S(2)}) collective-permute-start(bf16[768,512]{1,0:T(8,128)(2,1)S(1)} %fusion.refs_2_.refs_4_.refs_5_.refs_3_), channel_id=1, source_target_pairs={{0,1},{1,0},{2,3},{3,2},{4,5},{5,4},{6,7},{7,6},{8,9},{9,8},{10,11... | collective-permute-start | bytes 2359304 | tf_op jit(solution)/shard_map/ppermute | solution.py:49
  111.1 5.7 %collective-permute-start.24 = (bf16[768,512]{1,0:T(8,128)(2,1)S(1)}, bf16[768,512]{1,0:T(8,128)(2,1)S(1)}, u32[]{:S(2)}, u32[]{:S(2)}) collective-permute-start(bf16[768,512]{1,0:T(8,128)(2,1)S(1)} %collective-permute-done.13.refs_4_), channel_id=1, source_target_pairs={{0,2},{2,0},{4,6},{6,4},{1,3},{3,1},{5,7},{7,5},{8,10},{10,8},{12,... | collective-permute-start | bytes 2359304 | tf_op jit(solution)/shard_map/ppermute | solution.py:73
  (3 other events, 30.8 us)

commit v3 on v0

--- a/solution.py
+++ b/solution.py
@@ -1,9 +1,15 @@
+import functools
+
 import jax
 import jax.numpy as jnp
 from jax import lax
+from jax.experimental import pallas as pl
+from jax.experimental.pallas import tpu as pltpu
 from jax.sharding import PartitionSpec as P
 
 STEPS = 4
+COSTS = (12, 1, 1)
+LAGS = (8.0, 8.0, 4.0)
 
 
 def from_behind(value, axis, by):
@@ -17,7 +23,7 @@
     )
 
 
-def per_device(b_pairs, occ_index, vir_index, occ_depth, vir_height, omega):
+def ring_device(b_pairs, occ_index, vir_index, occ_depth, vir_height, omega):
     square = omega[0] * omega[0]
     n_row = lax.axis_size("row")
     n_col = lax.axis_size("col")
@@ -40,9 +46,337 @@
     return total.reshape(1, n_row, 1, sub_width, sub_width * n_col)
 
 
+def across_col(value):
+    return lax.ppermute(value, "col", [(0, 1), (1, 0)])
+
+
+def across_row(value):
+    return lax.ppermute(value, "row", [(i, (i + 2) % 4) for i in range(4)])
+
+
+def along_line(hops):
+    return lambda value: lax.ppermute(value, "freq", hops)
+
+
+OUTER = ((0, 1), (1, 0), (2, 3), (3, 2))
+INNER = ((0, 0), (1, 2), (2, 1), (3, 3))
+TO_ENDS = ((0, 1), (1, 0), (2, 3), (3, 2))
+
+
+def other_core(value):
+    return lax.ppermute(value, "row", [(i, i ^ 1) for i in range(4)])
+
+
+def join_rows(rows):
+    rows = rows[:3].astype(jnp.float32)
+    return rows[0] + (rows[1] + rows[2])
+
+
+def after(value, *earlier):
+    return lax.optimization_barrier((value, earlier))[0]
+
+
+def look_up(long_table, long_index, table, index):
+    size = long_table.shape[0]
+    table = jnp.pad(table, (0, size - table.shape[0]))
+    at = lax.broadcasted_iota(jnp.int32, (1, size), 1)
+    first = jnp.where(long_index[:, None] == at, long_table[None, :], 0.0)
+    second = jnp.where(index[:, None] == at, table[None, :], 0.0)
+    return jnp.sum(first + second, axis=1)
+
+
+def split_rows(value):
+    rows = []
+    for _ in range(3):
+        part = lax.reduce_precision(value, exponent_bits=8, mantissa_bits=7)
+        value = value - part
+        rows.append(part)
+    rows = jnp.stack(rows).astype(jnp.bfloat16)
+    return jnp.concatenate([rows, jnp.zeros((13, rows.shape[1]), jnp.bfloat16)])
+
+
+def in_vmem(value):
+    return pltpu.with_memory_space_constraint(value, pltpu.VMEM)
+
+
+def weigh_rows(weighted, left, weight):
+    step = 128
+
+    @pl.loop(0, weighted.shape[0] // step)
+    def _(n):
+        rows = pl.ds(pl.multiple_of(n * step, step), step)
+        value = left[rows, :].astype(jnp.float32) * weight[...]
+        weighted[rows, :] = value.astype(jnp.bfloat16)
+
+
+def slot_kernel(fresh, token, weight, *refs):
+    del token
+    right, left = refs[:4], (refs[0], refs[4])
+    acc, weighted = refs[-2:]
+    sub = acc.shape[2]
+    for j in range(2):
+        weigh_rows(weighted.at[j], left[j], weight)
+        for i in range(4):
+            part = contract_pairs(right[i][:sub, :], weighted[j])
+            if fresh:
+                acc[j, i] = part
+            else:
+                acc[j, i] += part
+
+
+def add_slot(sub, token, weight, right, left, acc, cost):
+    span = left.shape[1]
+    near = pl.BlockSpec(memory_space=pltpu.VMEM)
+    operands = [token, weight] + [in_vmem(block) for block in (*right, left)]
+    aliases = {}
+    if acc is not None:
+        aliases[len(operands)] = 0
+        operands.append(in_vmem(acc))
+    return pl.pallas_call(
+        functools.partial(slot_kernel, acc is None),
+        out_shape=pltpu.VMEM((2, 4, sub, sub), jnp.float32),
+        in_specs=[near] * len(operands),
+        out_specs=near,
+        input_output_aliases=aliases,
+        scratch_shapes=[pltpu.VMEM((2, sub, span), jnp.bfloat16)],
+        cost_estimate=pl.CostEstimate(
+            flops=16 * sub * sub * span * cost, bytes_accessed=0, transcendentals=0
+        ),
+        compiler_params=pltpu.CompilerParams(vmem_limit_bytes=12 * 1024 * 1024),
+    )(*operands)
+
+
+def finish_kernel(rights, lefts, jobs, n_in, *refs):
+    place, weight = refs[:2]
+    blocks = refs[2:n_in]
+    acc, out, weighted, sem = refs[-4:]
+    sub = acc.shape[2]
+
+    def put(n):
+        _, i, row, rows = rights[jobs[n][0]]
+        _, j, first, cols = lefts[jobs[n][1]]
+        column = pl.multiple_of(((place[0] + j) % 2) * sub + first, 128)
+        window = out.at[place[1 + i], pl.ds(row, rows), pl.ds(column, cols)]
+        part = acc.at[j, i, pl.ds(row, rows), pl.ds(first, cols)]
+        return pltpu.make_async_copy(part, window, sem.at[n])
+
+    ready = set()
+    for n, (right, left) in enumerate(jobs):
+        at, i, row, rows = rights[right]
+        left_at, j, first, cols = lefts[left]
+        if left not in ready:
+            ready.add(left)
+            part = weighted.at[j, pl.ds(first, cols), :]
+            weigh_rows(part, blocks[left_at], weight)
+        part = contract_pairs(blocks[at][:rows, :], weighted[j, first : first + cols, :])
+        acc[j, i, row : row + rows, first : first + cols] += part
+        put(n).start()
+    for n in range(len(jobs)):
+        put(n).wait()
+
+
+def finish(place, weight, rights, lefts, jobs, acc, out, tokens=()):
+    near = pl.BlockSpec(memory_space=pltpu.VMEM)
+    far = pl.BlockSpec(memory_space=pltpu.HBM)
+    sub, span = acc.shape[2], weight.shape[1]
+    blocks, where = [], []
+    for parts, used in ((rights, {r for r, _ in jobs}), (lefts, {l for _, l in jobs})):
+        where.append({})
+        for name in sorted(used):
+            block, *at = parts[name]
+            if not any(block is other for other in blocks):
+                blocks.append(block)
+            index = [block is other for other in blocks].index(True)
+            where[-1][name] = (index, *at)
+    operands = [place, weight] + [in_vmem(block) for block in blocks]
+    n_in = len(operands)
+    aliases = {n_in: 0}
+    operands.append(in_vmem(acc))
+    in_specs = [pl.BlockSpec(memory_space=pltpu.SMEM)] + [near] * n_in
+    if out is not None:
+        aliases[len(operands)] = 1
+        operands.append(out)
+        in_specs.append(far)
+    operands += tokens
+    in_specs += [near] * len(tokens)
+    area = sum(where[0][r][-1] * where[1][l][-1] for r, l in jobs)
+    return pl.pallas_call(
+        functools.partial(finish_kernel, *where, jobs, n_in),
+        out_shape=[
+            pltpu.VMEM(acc.shape, acc.dtype),
+            jax.ShapeDtypeStruct((4, sub, 2 * sub), jnp.float32),
+        ],
+        in_specs=in_specs,
+        out_specs=[near, far],
+        input_output_aliases=aliases,
+        scratch_shapes=[
+            pltpu.VMEM((2, sub, span), jnp.bfloat16),
+            pltpu.SemaphoreType.DMA((len(jobs),)),
+        ],
+        cost_estimate=pl.CostEstimate(
+            flops=2 * area * span, bytes_accessed=4 * area, transcendentals=0
+        ),
+        compiler_params=pltpu.CompilerParams(vmem_limit_bytes=12 * 1024 * 1024),
+    )(*operands)
+
+
+def mark_kernel(block, rows, marked, sem):
+    part = block.shape[0] // 4
+    copies = []
+    for n in range(4):
+        at = pl.ds(n * part, part)
+        copies.append(pltpu.make_async_copy(block.at[at, :], marked.at[at, :], sem.at[n]))
+    for copy in copies:
+        copy.start()
+    marked[block.shape[0] :, :] = rows[...]
+    for copy in copies:
+        copy.wait()
+
+
+def mark(block, rows):
+    shape = (block.shape[0] + rows.shape[0], block.shape[1])
+    near = pl.BlockSpec(memory_space=pltpu.VMEM)
+    return pl.pallas_call(
+        mark_kernel,
+        out_shape=pltpu.VMEM(shape, block.dtype),
+        in_specs=[pl.BlockSpec(memory_space=pltpu.HBM), near],
+        out_specs=near,
+        scratch_shapes=[pltpu.SemaphoreType.DMA((4,))],
+        compiler_params=pltpu.CompilerParams(vmem_limit_bytes=4 * 1024 * 1024),
+    )(block, rows)
+
+
+def pause_kernel(*refs):
+    refs[-1][...] = jnp.zeros_like(refs[-1])
+
+
+def lag(parts, micros, tokens):
+    token = pl.pallas_call(
+        pause_kernel,
+        out_shape=jax.ShapeDtypeStruct((8, 128), jnp.float32),
+        in_specs=[pl.BlockSpec(memory_space=pltpu.VMEM)] * len(parts),
+        out_specs=pl.BlockSpec(memory_space=pltpu.VMEM),
+        cost_estimate=pl.CostEstimate(
+            flops=int(micros * 1e9),
+            bytes_accessed=int(micros * 3e6),
+            transcendentals=0,
+        ),
+        compiler_params=pltpu.CompilerParams(vmem_limit_bytes=4 * 1024 * 1024),
+    )(*[pltpu.with_memory_space_constraint(v, pltpu.VMEM) for v in parts])
+    tokens.append(token)
+    return token
+
+
+def gate_kernel(value, token, out):
+    del value, token, out
+
+
+def gate(value, token):
+    near = pl.BlockSpec(memory_space=pltpu.VMEM)
+    return pl.pallas_call(
+        gate_kernel,
+        out_shape=pltpu.VMEM(value.shape, value.dtype),
+        in_specs=[near, near],
+        out_specs=near,
+        input_output_aliases={0: 0},
+        cost_estimate=pl.CostEstimate(flops=1, bytes_accessed=1, transcendentals=0),
+        compiler_params=pltpu.CompilerParams(vmem_limit_bytes=4 * 1024 * 1024),
+    )(pltpu.with_memory_space_constraint(value, pltpu.VMEM), token)
+
+
+def line_device(b_pairs, occ_index, vir_index, occ_depth, vir_height, omega):
+    group = lax.axis_index("freq")
+    row = lax.axis_index("row")
+    col = lax.axis_index("col")
+    end = (group == 0) | (group == 3)
+    sub, span = b_pairs.shape
+
+    tokens = []
+    x, y = [None] * 4, [None] * 4
+    own = b_pairs
+    x[0] = across_col(own)
+    y[0] = across_row(own)
+    own_swap = other_core(own)
+
+    gap = look_up(vir_height, vir_index, occ_depth, occ_index)
+    marked = mark(own, split_rows(gap))
+    near_1 = along_line(OUTER)(marked)
+    near_2 = along_line(INNER)(marked)
+    got = lag((near_2,), 0.1, tokens)
+    place = jnp.stack([col, row, row ^ 1, row ^ 2, row ^ 3]).astype(jnp.int32)
+
+    def add(mine, swap, x, y, acc, token, cost):
+        right = (mine, swap, y, other_core(y))
+        acc = add_slot(sub, token, weigh(mine), right, x, acc, cost)
+        return acc, lag((acc, swap), 0.1, tokens)
+
+    def weigh(block):
+        gap = join_rows(block[sub:])
+        return (4.0 * gap / (gap * gap + omega[0] * omega[0]))[None, :]
+
+    here = lag((near_1, near_2), LAGS[2], tokens)
+    mine_1 = jnp.where(after(group, here) >= 0, near_1, near_2)
+    crossed = lag((mine_1,), 0.1, tokens)
+    far_1 = along_line(TO_ENDS)(near_2)
+    far_2 = along_line(INNER)(near_1)
+    x[1] = across_col(mine_1)
+    y[1] = across_row(mine_1)
+    swap_1 = other_core(mine_1)
+    acc, added = add(
+        marked, own_swap, x[0], y[0], None, crossed, COSTS[0]
+    )
+
+    got_2 = lag((far_1, far_2, swap_1), LAGS[0], tokens)
+    mine_2 = jnp.where(after(end, got, got_2, added), far_1, near_2)
+    last = along_line(TO_ENDS)(far_2)
+    x[2] = across_col(mine_2)
+    y[2] = across_row(mine_2)
+    swap_2 = other_core(mine_2)
+    y[1] = gate(y[1], added)
+    acc, added = add(
+        mine_1, swap_1, x[1], y[1], acc, lag((mine_2,), 0.1, tokens), COSTS[1]
+    )
+
+    got = lag((last, swap_2), LAGS[1], tokens)
+    mine_3 = jnp.where(after(end, got, added), last, far_2)
+    cut = sub // 2
+    halves = [(mine_3[:cut], 0), (mine_3[cut:sub], cut)]
+    x[3] = [across_col(half) for half, _ in halves]
+    y[3] = [across_row(half) for half, _ in halves]
+    swap_3 = other_core(mine_3)
+    acc, _ = add(
+        mine_2, swap_2, x[2], y[2], acc, lag((mine_3,), 0.1, tokens), COSTS[2]
+    )
+
+    weight = weigh(mine_3)
+    rights = {"own": (mine_3, 0, 0, sub), "swap": (swap_3, 1, 0, sub)}
+    lefts = {"own": (mine_3, 0, 0, sub)}
+    jobs = (("own", "own"), ("swap", "own"))
+    acc, out = finish(place, weight, rights, lefts, jobs, acc, None)
+    for n, (_, first) in enumerate(halves):
+        token = lag((acc,), 0.1, tokens)
+        left, right = gate(x[3][n], token), gate(y[3][n], token)
+        here = after(place, lag((left, right), 16.0 if n == 0 else 4.0, tokens))
+        rights |= {f"y{n}": (right, 2, first, cut), f"s{n}": (other_core(right), 3, first, cut)}
+        lefts[f"x{n}"] = (left, 1, first, cut)
+        if n == 0:
+            jobs = (("own", "x0"), ("swap", "x0"), ("y0", "own"), ("y0", "x0"))
+            jobs += (("s0", "own"), ("s0", "x0"))
+            acc, out = finish(here, weight, rights, lefts, jobs, acc, out)
+        else:
+            jobs = (("own", "x1"), ("swap", "x1"), ("y1", "own"), ("y1", "x0"))
+            jobs += (("y1", "x1"), ("y0", "x1"), ("s0", "x1"))
+            acc, out = finish(here, weight, rights, lefts, jobs, acc, out)
+            jobs = (("s1", "own"), ("s1", "x0"), ("s1", "x1"))
+            acc, out = finish(place, weight, rights, lefts, jobs, acc, out, tokens)
+    return out.reshape(1, 4, 1, sub, 2 * sub)
+
+
 def solution(mesh):
     in_specs = (P(("row", "col"), "freq"), P("freq"), P("freq"), P(), P(), P("freq"))
     out_specs = P("freq", None, "col", None, "row")
+    shape = tuple(mesh.shape[axis] for axis in ("freq", "row", "col"))
+    per_device = line_device if shape == (4, 4, 2) else ring_device
     return jax.shard_map(
         per_device, mesh=mesh, in_specs=in_specs, out_specs=out_specs, check_vma=False
     )

time: 414 us -> 107 us (0.26)
  waiting for transfers between devices: 280 us -> 42.1 us
  matrix products: 60.7 us -> 0 us
  local copies, waits for them, and re-layouts: 45.3 us -> 0.82 us
  Pallas kernels: 0 us -> 36.5 us
  between operations: 15.8 us -> 1.16 us
  starting transfers between devices: 11.2 us -> 23.9 us
    ppermute x12 -> x24, waiting for transfers between devices: 223 us -> 42.1 us  [the longest x5 26.9 us: across_row(): return lax.ppermute(value, 'row', [(i, (i + 2) % 4) for i in range(4)])]
    dot_general x4 -> x0, matrix products: 60.7 us -> none  [contract_pairs(): lax.dot_general(left, right, (((1,), (1,)), ((), ())), preferred_element_...]
    all_gather x2 -> x0, waiting for transfers between devices: 56.1 us -> none  [the longest x1 32.9 us: per_device(): right = lax.all_gather(b_pairs, 'row', axis=0, tiled=True)]
    pallas_call x0 -> x27, Pallas kernels: none -> 36.5 us  [the longest x3 19 us: add_slot(): pl.pallas_call(functools.partial(slot_kernel, acc is None), out_shape=plt...]
    gather x8 -> x0, local copies, waits for them, and re-layouts: 26.7 us -> none  [per_device(): gap = jnp.take(vir_height, vir_part) + jnp.take(occ_depth, occ_part)]
    reshape x1 -> x0, local copies, waits for them, and re-layouts: 18.6 us -> none  [per_device(): return total.reshape(1, n_row, 1, sub_width, sub_width * n_col)]
    ppermute x12 -> x24, starting transfers between devices: 11.1 us -> 23.9 us  [the longest x5 11.6 us: along_line(): return lambda value: lax.ppermute(value, 'freq', hops)]
  transfers between devices with their start and end apart: 14 -> 24, of which waited for: 8 -> 6; matrix products, arithmetic and copies ran while one was open for 15% -> 0% of each run, Pallas kernels for 0% -> 30%
where the time goes in v3:
time: 107 us
  waiting for transfers between devices  42.1 us (39%)
  Pallas kernels  36.5 us (34%)
  starting transfers between devices  23.9 us (22%)
  other arithmetic  2.29 us (2%)
  between operations  1.16 us (1%)
    ppermute x5, waiting for transfers between devices, across_row(): return lax.ppermute(value, 'row', [(i, (i + 2) % 4) for i in range(4)])  26.9 us
    pallas_call x3, Pallas kernels, add_slot(): pl.pallas_call(functools.partial(slot_kernel, acc is None), out_shape=plt...  19 us
    pallas_call x4, Pallas kernels, finish(): pl.pallas_call(functools.partial(finish_kernel, *where, jobs, n_in), out_...  16.2 us
    ppermute x5, waiting for transfers between devices, along_line(): return lambda value: lax.ppermute(value, 'freq', hops)  13.5 us
    ppermute x5, starting transfers between devices, along_line(): return lambda value: lax.ppermute(value, 'freq', hops)  11.6 us
    ppermute x5, starting transfers between devices, across_row(): return lax.ppermute(value, 'row', [(i, (i + 2) % 4) for i in range(4)])  5.7 us
    ppermute x5, starting transfers between devices, across_col(): return lax.ppermute(value, 'col', [(0, 1), (1, 0)])  5.66 us
  transfers between devices with their start and end apart: 24, of which 6 were waited for; matrix products, arithmetic and copies ran while one was open for 0% of the time, Pallas kernels for 30%

profile of v3, /device:TPU:0, one launch (start us, length us, event | category | flops | bytes accessed | tf_op | source)
XLA Modules:
  0.0 106.8 jit_solution(14416460869175236352)
XLA Ops:
  0.7 1.9 %add_reduce_fusion = f32[512]{0:T(512)S(1)} fusion(f32[1792]{0:T(1024)S(1)} %pad.5, s32[512]{0:T(512)} %param.7, f32[1792]{0:T(1024)} %param.10, s32[512]{0:T(512)} %param.8), kind=kLoop, calls=%fused_computation | loop fusion | flops 5504512 | bytes 20480 | tf_op jit(solution)/shard_map/reduce_sum | solution.py:85
  2.6 1.3 %shard_map.64.refs_0_ = bf16[784,512]{1,0:T(8,128)(2,1)S(1)} custom-call(bf16[768,512]{1,0:T(8,128)(2,1)} %block.1, bf16[16,512]{1,0:T(8,128)(2,1)S(1)} %fusion.4.rows), custom_call_target="tpu_custom_call" | custom-call | tf_op jit(solution)/shard_map/pallas_call | solution.py:239
  4.6 5.9 %collective-permute-start = (bf16[784,512]{1,0:T(8,128)(2,1)S(1)}, bf16[784,512]{1,0:T(8,128)(2,1)S(1)}, u32[]{:S(2)}, u32[]{:S(2)}) collective-permute-start(bf16[784,512]{1,0:T(8,128)(2,1)S(1)} %shard_map.64.refs_0_), channel_id=1, source_target_pairs={{0,8},{8,0},{16,24},{24,16},{1,9},{9,1},{17,25},{25,17},{2,10},{10... | collective-permute-start | bytes 2408456 | tf_op jit(solution)/shard_map/ppermute | solution.py:58
  10.5 1.5 %collective-permute-start.7 = (bf16[768,512]{1,0:T(8,128)(2,1)}, bf16[768,512]{1,0:T(8,128)(2,1)}, u32[]{:S(2)}, u32[]{:S(2)}) collective-permute-start(bf16[768,512]{1,0:T(8,128)(2,1)} %block.1), channel_id=1, source_target_pairs={{0,4},{2,6},{4,0},{6,2},{1,5},{3,7},{5,1},{7,3},{8,12},{10,14},{12... | collective-permute-start | bytes 2359304 | tf_op jit(solution)/shard_map/ppermute | solution.py:54
  12.0 1.5 %collective-permute-start.9 = (bf16[768,512]{1,0:T(8,128)(2,1)}, bf16[768,512]{1,0:T(8,128)(2,1)}, u32[]{:S(2)}, u32[]{:S(2)}) collective-permute-start(bf16[768,512]{1,0:T(8,128)(2,1)} %block.1), channel_id=1, source_target_pairs={{0,1},{1,0},{2,3},{3,2},{4,5},{5,4},{6,7},{7,6},{8,9},{9,8},{10,11... | collective-permute-start | bytes 2359304 | tf_op jit(solution)/shard_map/ppermute | solution.py:50
  14.3 15.3 %collective-permute-done.7.refs_2_ = bf16[768,512]{1,0:T(8,128)(2,1)} collective-permute-done((bf16[768,512]{1,0:T(8,128)(2,1)}, bf16[768,512]{1,0:T(8,128)(2,1)}, u32[]{:S(2)}, u32[]{:S(2)}) %collective-permute-start.7) | collective-permute-done | bytes 786464 | tf_op jit(solution)/shard_map/ppermute | solution.py:54
  29.6 1.6 %collective-permute-start.13 = (bf16[784,512]{1,0:T(8,128)(2,1)S(1)}, bf16[784,512]{1,0:T(8,128)(2,1)S(1)}, u32[]{:S(2)}, u32[]{:S(2)}) collective-permute-start(bf16[784,512]{1,0:T(8,128)(2,1)S(1)} %broadcast_select_fusion.2.refs_0_), channel_id=1, source_target_pairs={{0,1},{1,0},{2,3},{3,2},{4,5},{5,4},{6,7},{7,6},{8,9},{9,8},{10,11... | collective-permute-start | bytes 2408456 | tf_op jit(solution)/shard_map/ppermute | solution.py:50
  31.2 1.5 %collective-permute-start.11 = (bf16[784,512]{1,0:T(8,128)(2,1)S(1)}, bf16[784,512]{1,0:T(8,128)(2,1)S(1)}, u32[]{:S(2)}, u32[]{:S(2)}) collective-permute-start(bf16[784,512]{1,0:T(8,128)(2,1)S(1)} %broadcast_select_fusion.2.refs_0_), channel_id=1, source_target_pairs={{0,4},{2,6},{4,0},{6,2},{1,5},{3,7},{5,1},{7,3},{8,12},{10,14},{12... | collective-permute-start | bytes 2408456 | tf_op jit(solution)/shard_map/ppermute | solution.py:54
  33.3 0.9 collective-permute-start.1
  34.1 7.2 %shard_map.69.refs_0_.refs_5_ = f32[2,4,768,768]{3,2,1,0:T(8,128)S(1)} custom-call(f32[8,128]{1,0:T(8,128)S(1)} %shard_map.68.token.refs_10_, f32[1,512]{1,0:T(1,128)S(1)} %add_divide_fusion.3.weight, bf16[784,512]{1,0:T(8,128)(2,1)S(1)} %shard_map.64.refs_0_, bf16[768,512]{1,0:T(8,128)(2,1)S(1)} %collective-permute-done.6.refs_1_, ...), custom_call_target="tpu_custom_call" | custom-call | flops 57982058496 | tf_op jit(solution)/shard_map/pallas_call | solution.py:135
  41.4 9.8 %collective-permute-done.11.value = bf16[784,512]{1,0:T(8,128)(2,1)S(1)} collective-permute-done((bf16[784,512]{1,0:T(8,128)(2,1)S(1)}, bf16[784,512]{1,0:T(8,128)(2,1)S(1)}, u32[]{:S(2)}, u32[]{:S(2)}) %collective-permute-start.11) | collective-permute-done | bytes 802848 | tf_op jit(solution)/shard_map/ppermute | solution.py:54
  51.2 1.9 %collective-permute-done.4.refs_0_ = bf16[784,512]{1,0:T(8,128)(2,1)S(1)} collective-permute-done((bf16[784,512]{1,0:T(8,128)(2,1)S(1)}, bf16[784,512]{1,0:T(8,128)(2,1)S(1)}, u32[]{:S(2)}, u32[]{:S(2)}) %collective-permute-start.4) | collective-permute-done | bytes 802848 | tf_op jit(solution)/shard_map/ppermute | solution.py:58
  53.3 3.7 %collective-permute-start.2 = (bf16[784,512]{1,0:T(8,128)(2,1)S(1)}, bf16[784,512]{1,0:T(8,128)(2,1)S(1)}, u32[]{:S(2)}, u32[]{:S(2)}) collective-permute-start(bf16[784,512]{1,0:T(8,128)(2,1)S(1)} %collective-permute-done.1.refs_1_), channel_id=1, source_target_pairs={{0,8},{8,0},{16,24},{24,16},{1,9},{9,1},{17,25},{25,17},{2,10},{10... | collective-permute-start | bytes 2408456 | tf_op jit(solution)/shard_map/ppermute | solution.py:58
  58.2 5.8 %shard_map.74.refs_0_.refs_5_ = f32[2,4,768,768]{3,2,1,0:T(8,128)S(1)} custom-call(f32[8,128]{1,0:T(8,128)S(1)} %shard_map.72.token.refs_13_, f32[1,512]{1,0:T(1,128)S(1)} %add_divide_fusion.2.weight, bf16[784,512]{1,0:T(8,128)(2,1)S(1)} %broadcast_select_fusion.2.refs_0_, ...), custom_call_target="tpu_custom_call", output_to_operand_aliasing={{}: (7, {})} | custom-call | flops 4831838208 | tf_op jit(solution)/shard_map/pallas_call | solution.py:135
  64.0 11.5 %collective-permute-done.2.refs_0_ = bf16[784,512]{1,0:T(8,128)(2,1)S(1)} collective-permute-done((bf16[784,512]{1,0:T(8,128)(2,1)S(1)}, bf16[784,512]{1,0:T(8,128)(2,1)S(1)}, u32[]{:S(2)}, u32[]{:S(2)}) %collective-permute-start.2) | collective-permute-done | bytes 802848 | tf_op jit(solution)/shard_map/ppermute | solution.py:58
  75.5 1.8 %collective-permute-done.17.refs_2_ = bf16[784,512]{1,0:T(8,128)(2,1)S(1)} collective-permute-done((bf16[784,512]{1,0:T(8,128)(2,1)S(1)}, bf16[784,512]{1,0:T(8,128)(2,1)S(1)}, u32[]{:S(2)}, u32[]{:S(2)}) %collective-permute-start.17) | collective-permute-done | bytes 802848 | tf_op jit(solution)/shard_map/ppermute | solution.py:54
  78.6 1.5 %collective-permute-start.15 = (bf16[384,512]{1,0:T(8,128)(2,1)S(1)}, bf16[384,512]{1,0:T(8,128)(2,1)S(1)}, u32[]{:S(2)}, u32[]{:S(2)}) collective-permute-start(bf16[384,512]{1,0:T(8,128)(2,1)S(1)} %get-tuple-element.29), channel_id=1, source_target_pairs={{0,1},{1,0},{2,3},{3,2},{4,5},{5,4},{6,7},{7,6},{8,9},{9,8},{10,11... | collective-permute-start | bytes 1179656 | tf_op jit(solution)/shard_map/ppermute | solution.py:50
  80.8 1.5 %collective-permute-start.14 = (bf16[384,512]{1,0:T(8,128)(2,1)S(1)}, bf16[384,512]{1,0:T(8,128)(2,1)S(1)}, u32[]{:S(2)}, u32[]{:S(2)}) collective-permute-start(bf16[384,512]{1,0:T(8,128)(2,1)S(1)} %get-tuple-element.30), channel_id=1, source_target_pairs={{0,4},{2,6},{4,0},{6,2},{1,5},{3,7},{5,1},{7,3},{8,12},{10,14},{12... | collective-permute-start | bytes 1179656 | tf_op jit(solution)/shard_map/ppermute | solution.py:54
  82.3 6.0 %shard_map.77.refs_4_.refs_0_ = f32[2,4,768,768]{3,2,1,0:T(8,128)S(1)} custom-call(f32[8,128]{1,0:T(8,128)S(1)} %shard_map.76.token.refs_16_, f32[1,512]{1,0:T(1,128)S(1)} %add_divide_fusion.weight, bf16[784,512]{1,0:T(8,128)(2,1)S(1)} %broadcast_select_fusion.1.refs_0_, ...), custom_call_target="tpu_custom_call", output_to_operand_aliasing={{}: (7, {})} | custom-call | flops 4831838208 | tf_op jit(solution)/shard_map/pallas_call | solution.py:135
  88.3 4.0 %shard_map.78 = (f32[2,4,768,768]{3,2,1,0:T(8,128)S(1)}, f32[4,768,1536]{2,1,0:T(8,128)}) custom-call(s32[5]{0:T(128)S(1)} %stack.30.refs_0_, f32[1,512]{1,0:T(1,128)S(1)} %add_divide_fusion.1.refs_1_, bf16[784,512]{1,0:T(8,128)(2,1)S(1)} %broadcast_select_fusion.refs_0_.refs_2_.refs_3_, ...), custom_call_target="tpu_custom_call", output_to_operand_aliasing={{0}: (4, {})} | custom-call | flops 1207959552 | bytes 4718592 | tf_op jit(solution)/shard_map/pallas_call | solution.py:203
  92.5 1.7 %collective-permute-done.21.refs_3_ = bf16[384,512]{1,0:T(8,128)(2,1)S(1)} collective-permute-done((bf16[384,512]{1,0:T(8,128)(2,1)S(1)}, bf16[384,512]{1,0:T(8,128)(2,1)S(1)}, u32[]{:S(2)}, u32[]{:S(2)}) %collective-permute-start.21) | collective-permute-done | bytes 393248 | tf_op jit(solution)/shard_map/ppermute | solution.py:67
  94.2 4.3 %shard_map.83 = (f32[2,4,768,768]{3,2,1,0:T(8,128)S(1)}, f32[4,768,1536]{2,1,0:T(8,128)}) custom-call(s32[5]{0:T(128)S(1)} %stack.30.refs_0_, f32[1,512]{1,0:T(1,128)S(1)} %add_divide_fusion.1.refs_1_, bf16[784,512]{1,0:T(8,128)(2,1)S(1)} %broadcast_select_fusion.refs_0_.refs_2_.refs_3_, ...), custom_call_target="tpu_custom_call", output_to_operand_aliasing={{0}: (7, {}), {1}: (8, {})} | custom-call | flops 1509949440 | bytes 5898240 | tf_op jit(solution)/shard_map/pallas_call | solution.py:203
  98.7 4.7 %shard_map.88 = (f32[2,4,768,768]{3,2,1,0:T(8,128)S(1)}, f32[4,768,1536]{2,1,0:T(8,128)}) custom-call(s32[5]{0:T(128)S(1)} %stack.30.refs_0_, f32[1,512]{1,0:T(1,128)S(1)} %add_divide_fusion.1.refs_1_, bf16[784,512]{1,0:T(8,128)(2,1)S(1)} %broadcast_select_fusion.refs_0_.refs_2_.refs_3_, ...), custom_call_target="tpu_custom_call", output_to_operand_aliasing={{0}: (9, {}), {1}: (10, {})} | custom-call | flops 1509949440 | bytes 5898240 | tf_op jit(solution)/shard_map/pallas_call | solution.py:203
  103.4 3.2 %shard_map.90 = (f32[2,4,768,768]{3,2,1,0:T(8,128)S(1)}, f32[4,768,1536]{2,1,0:T(8,128)}) custom-call(s32[5]{0:T(128)S(1)} %stack.30.refs_0_, f32[1,512]{1,0:T(1,128)S(1)} %add_divide_fusion.1.refs_1_, bf16[384,512]{1,0:T(8,128)(2,1)S(1)} %collective-permute-done.22.refs_2_, ...), custom_call_target="tpu_custom_call", output_to_operand_aliasing={{0}: (6, {}), {1}: (7, {})} | custom-call | flops 603979776 | bytes 2359296 | tf_op jit(solution)/shard_map/pallas_call | solution.py:203
  (68 shorter events, 5.7 us)
Async XLA Ops:
  3.9 25.6 %collective-permute-start.3 = (bf16[784,512]{1,0:T(8,128)(2,1)S(1)}, bf16[784,512]{1,0:T(8,128)(2,1)S(1)}, u32[]{:S(2)}, u32[]{:S(2)}) collective-permute-start(bf16[784,512]{1,0:T(8,128)(2,1)S(1)} %shard_map.64.refs_0_), channel_id=1, source_target_pairs={{0,0},{8,16},{16,8},{24,24},{1,1},{9,17},{17,9},{25,25},{2,2},{10,... | collective-permute-start | bytes 2408456 | tf_op jit(solution)/shard_map/ppermute | solution.py:58
  4.6 24.9 %collective-permute-start = (bf16[784,512]{1,0:T(8,128)(2,1)S(1)}, bf16[784,512]{1,0:T(8,128)(2,1)S(1)}, u32[]{:S(2)}, u32[]{:S(2)}) collective-permute-start(bf16[784,512]{1,0:T(8,128)(2,1)S(1)} %shard_map.64.refs_0_), channel_id=1, source_target_pairs={{0,8},{8,0},{16,24},{24,16},{1,9},{9,1},{17,25},{25,17},{2,10},{10... | collective-permute-start | bytes 2408456 | tf_op jit(solution)/shard_map/ppermute | solution.py:58
  10.5 19.0 %collective-permute-start.7 = (bf16[768,512]{1,0:T(8,128)(2,1)}, bf16[768,512]{1,0:T(8,128)(2,1)}, u32[]{:S(2)}, u32[]{:S(2)}) collective-permute-start(bf16[768,512]{1,0:T(8,128)(2,1)} %block.1), channel_id=1, source_target_pairs={{0,4},{2,6},{4,0},{6,2},{1,5},{3,7},{5,1},{7,3},{8,12},{10,14},{12... | collective-permute-start | bytes 2359304 | tf_op jit(solution)/shard_map/ppermute | solution.py:54
  12.0 20.7 %collective-permute-start.6 = (bf16[768,512]{1,0:T(8,128)(2,1)}, bf16[768,512]{1,0:T(8,128)(2,1)S(1)}, u32[]{:S(2)}, u32[]{:S(2)}) collective-permute-start(bf16[768,512]{1,0:T(8,128)(2,1)} %block.1), channel_id=1, source_target_pairs={{0,2},{2,0},{4,6},{6,4},{1,3},{3,1},{5,7},{7,5},{8,10},{10,8},{12,... | collective-permute-start | bytes 2359304 | tf_op jit(solution)/shard_map/ppermute | solution.py:67
  12.0 20.8 %collective-permute-start.9 = (bf16[768,512]{1,0:T(8,128)(2,1)}, bf16[768,512]{1,0:T(8,128)(2,1)}, u32[]{:S(2)}, u32[]{:S(2)}) collective-permute-start(bf16[768,512]{1,0:T(8,128)(2,1)} %block.1), channel_id=1, source_target_pairs={{0,1},{1,0},{2,3},{3,2},{4,5},{5,4},{6,7},{7,6},{8,9},{9,8},{10,11... | collective-permute-start | bytes 2359304 | tf_op jit(solution)/shard_map/ppermute | solution.py:50
  29.5 3.7 %collective-permute-start.8 = (bf16[768,512]{1,0:T(8,128)(2,1)}, bf16[768,512]{1,0:T(8,128)(2,1)}, u32[]{:S(2)}, u32[]{:S(2)}) collective-permute-start(bf16[768,512]{1,0:T(8,128)(2,1)} %collective-permute-done.7.refs_2_), channel_id=1, source_target_pairs={{0,2},{2,0},{4,6},{6,4},{1,3},{3,1},{5,7},{7,5},{8,10},{10,8},{12,... | collective-permute-start | bytes 2359304 | tf_op jit(solution)/shard_map/ppermute | solution.py:67
  29.6 27.9 %collective-permute-start.13 = (bf16[784,512]{1,0:T(8,128)(2,1)S(1)}, bf16[784,512]{1,0:T(8,128)(2,1)S(1)}, u32[]{:S(2)}, u32[]{:S(2)}) collective-permute-start(bf16[784,512]{1,0:T(8,128)(2,1)S(1)} %broadcast_select_fusion.2.refs_0_), channel_id=1, source_target_pairs={{0,1},{1,0},{2,3},{3,2},{4,5},{5,4},{6,7},{7,6},{8,9},{9,8},{10,11... | collective-permute-start | bytes 2408456 | tf_op jit(solution)/shard_map/ppermute | solution.py:50
  31.2 20.0 %collective-permute-start.11 = (bf16[784,512]{1,0:T(8,128)(2,1)S(1)}, bf16[784,512]{1,0:T(8,128)(2,1)S(1)}, u32[]{:S(2)}, u32[]{:S(2)}) collective-permute-start(bf16[784,512]{1,0:T(8,128)(2,1)S(1)} %broadcast_select_fusion.2.refs_0_), channel_id=1, source_target_pairs={{0,4},{2,6},{4,0},{6,2},{1,5},{3,7},{5,1},{7,3},{8,12},{10,14},{12... | collective-permute-start | bytes 2408456 | tf_op jit(solution)/shard_map/ppermute | solution.py:54
  32.7 20.4 %collective-permute-start.5 = (bf16[784,512]{1,0:T(8,128)(2,1)S(1)}, bf16[784,512]{1,0:T(8,128)(2,1)S(1)}, u32[]{:S(2)}, u32[]{:S(2)}) collective-permute-start(bf16[784,512]{1,0:T(8,128)(2,1)S(1)} %broadcast_select_fusion.2.refs_0_), channel_id=1, source_target_pairs={{0,2},{2,0},{4,6},{6,4},{1,3},{3,1},{5,7},{7,5},{8,10},{10,8},{12,... | collective-permute-start | bytes 2408456 | tf_op jit(solution)/shard_map/ppermute | solution.py:67
  32.8 20.3 %collective-permute-start.4 = (bf16[784,512]{1,0:T(8,128)(2,1)S(1)}, bf16[784,512]{1,0:T(8,128)(2,1)S(1)}, u32[]{:S(2)}, u32[]{:S(2)}) collective-permute-start(bf16[784,512]{1,0:T(8,128)(2,1)S(1)} %collective-permute-done.3.refs_0_.refs_1_), channel_id=1, source_target_pairs={{0,8},{8,0},{16,24},{24,16},{1,9},{9,1},{17,25},{25,17},{2,10},{10... | collective-permute-start | bytes 2408456 | tf_op jit(solution)/shard_map/ppermute | solution.py:58
  33.3 19.9 %collective-permute-start.1 = (bf16[784,512]{1,0:T(8,128)(2,1)S(1)}, bf16[784,512]{1,0:T(8,128)(2,1)S(1)}, u32[]{:S(2)}, u32[]{:S(2)}) collective-permute-start(bf16[784,512]{1,0:T(8,128)(2,1)S(1)} %collective-permute-done.refs_0_), channel_id=1, source_target_pairs={{0,0},{8,16},{16,8},{24,24},{1,1},{9,17},{17,9},{25,25},{2,2},{10,... | collective-permute-start | bytes 2408456 | tf_op jit(solution)/shard_map/ppermute | solution.py:58
  51.2 7.0 %collective-permute-start.12 = (bf16[784,512]{1,0:T(8,128)(2,1)S(1)}, bf16[784,512]{1,0:T(8,128)(2,1)S(1)}, u32[]{:S(2)}, u32[]{:S(2)}) collective-permute-start(bf16[784,512]{1,0:T(8,128)(2,1)S(1)} %shard_map.73.refs_2_), channel_id=1, source_target_pairs={{0,2},{2,0},{4,6},{6,4},{1,3},{3,1},{5,7},{7,5},{8,10},{10,8},{12,... | collective-permute-start | bytes 2408456 | tf_op jit(solution)/shard_map/ppermute | solution.py:67
  53.3 22.3 %collective-permute-start.10 = (bf16[784,512]{1,0:T(8,128)(2,1)S(1)}, bf16[784,512]{1,0:T(8,128)(2,1)S(1)}, u32[]{:S(2)}, u32[]{:S(2)}) collective-permute-start(bf16[784,512]{1,0:T(8,128)(2,1)S(1)} %broadcast_select_fusion.1.refs_0_), channel_id=1, source_target_pairs={{0,2},{2,0},{4,6},{6,4},{1,3},{3,1},{5,7},{7,5},{8,10},{10,8},{12,... | collective-permute-start | bytes 2408456 | tf_op jit(solution)/shard_map/ppermute | solution.py:67
  53.3 22.2 %collective-permute-start.2 = (bf16[784,512]{1,0:T(8,128)(2,1)S(1)}, bf16[784,512]{1,0:T(8,128)(2,1)S(1)}, u32[]{:S(2)}, u32[]{:S(2)}) collective-permute-start(bf16[784,512]{1,0:T(8,128)(2,1)S(1)} %collective-permute-done.1.refs_1_), channel_id=1, source_target_pairs={{0,8},{8,0},{16,24},{24,16},{1,9},{9,1},{17,25},{25,17},{2,10},{10... | collective-permute-start | bytes 2408456 | tf_op jit(solution)/shard_map/ppermute | solution.py:58
  57.0 23.1 %collective-permute-start.19 = (bf16[784,512]{1,0:T(8,128)(2,1)S(1)}, bf16[784,512]{1,0:T(8,128)(2,1)S(1)}, u32[]{:S(2)}, u32[]{:S(2)}) collective-permute-start(bf16[784,512]{1,0:T(8,128)(2,1)S(1)} %broadcast_select_fusion.1.refs_0_), channel_id=1, source_target_pairs={{0,1},{1,0},{2,3},{3,2},{4,5},{5,4},{6,7},{7,6},{8,9},{9,8},{10,11... | collective-permute-start | bytes 2408456 | tf_op jit(solution)/shard_map/ppermute | solution.py:50
  57.6 19.7 %collective-permute-start.17 = (bf16[784,512]{1,0:T(8,128)(2,1)S(1)}, bf16[784,512]{1,0:T(8,128)(2,1)S(1)}, u32[]{:S(2)}, u32[]{:S(2)}) collective-permute-start(bf16[784,512]{1,0:T(8,128)(2,1)S(1)} %broadcast_select_fusion.1.refs_0_), channel_id=1, source_target_pairs={{0,4},{2,6},{4,0},{6,2},{1,5},{3,7},{5,1},{7,3},{8,12},{10,14},{12... | collective-permute-start | bytes 2408456 | tf_op jit(solution)/shard_map/ppermute | solution.py:54
  77.3 3.4 %collective-permute-start.18 = (bf16[784,512]{1,0:T(8,128)(2,1)S(1)}, bf16[784,512]{1,0:T(8,128)(2,1)S(1)}, u32[]{:S(2)}, u32[]{:S(2)}) collective-permute-start(bf16[784,512]{1,0:T(8,128)(2,1)S(1)} %collective-permute-done.17.refs_2_), channel_id=1, source_target_pairs={{0,2},{2,0},{4,6},{6,4},{1,3},{3,1},{5,7},{7,5},{8,10},{10,8},{12,... | collective-permute-start | bytes 2408456 | tf_op jit(solution)/shard_map/ppermute | solution.py:67
  77.4 10.9 %collective-permute-start.16 = (bf16[784,512]{1,0:T(8,128)(2,1)S(1)}, bf16[784,512]{1,0:T(8,128)(2,1)S(1)}, u32[]{:S(2)}, u32[]{:S(2)}) collective-permute-start(bf16[784,512]{1,0:T(8,128)(2,1)S(1)} %broadcast_select_fusion.refs_0_.refs_2_.refs_3_), channel_id=1, source_target_pairs={{0,2},{2,0},{4,6},{6,4},{1,3},{3,1},{5,7},{7,5},{8,10},{10,8},{12,... | collective-permute-start | bytes 2408456 | tf_op jit(solution)/shard_map/ppermute | solution.py:67
  78.1 14.3 %collective-permute-start.20 = (bf16[384,512]{1,0:T(8,128)(2,1)S(1)}, bf16[384,512]{1,0:T(8,128)(2,1)S(1)}, u32[]{:S(2)}, u32[]{:S(2)}) collective-permute-start(bf16[384,512]{1,0:T(8,128)(2,1)S(1)} %get-tuple-element.29), channel_id=1, source_target_pairs={{0,4},{2,6},{4,0},{6,2},{1,5},{3,7},{5,1},{7,3},{8,12},{10,14},{12... | collective-permute-start | bytes 1179656 | tf_op jit(solution)/shard_map/ppermute | solution.py:54
  78.6 13.8 %collective-permute-start.15 = (bf16[384,512]{1,0:T(8,128)(2,1)S(1)}, bf16[384,512]{1,0:T(8,128)(2,1)S(1)}, u32[]{:S(2)}, u32[]{:S(2)}) collective-permute-start(bf16[384,512]{1,0:T(8,128)(2,1)S(1)} %get-tuple-element.29), channel_id=1, source_target_pairs={{0,1},{1,0},{2,3},{3,2},{4,5},{5,4},{6,7},{7,6},{8,9},{9,8},{10,11... | collective-permute-start | bytes 1179656 | tf_op jit(solution)/shard_map/ppermute | solution.py:50
  80.2 18.5 %collective-permute-start.23 = (bf16[384,512]{1,0:T(8,128)(2,1)S(1)}, bf16[384,512]{1,0:T(8,128)(2,1)S(1)}, u32[]{:S(2)}, u32[]{:S(2)}) collective-permute-start(bf16[384,512]{1,0:T(8,128)(2,1)S(1)} %get-tuple-element.30), channel_id=1, source_target_pairs={{0,1},{1,0},{2,3},{3,2},{4,5},{5,4},{6,7},{7,6},{8,9},{9,8},{10,11... | collective-permute-start | bytes 1179656 | tf_op jit(solution)/shard_map/ppermute | solution.py:50
  80.8 17.7 %collective-permute-start.14 = (bf16[384,512]{1,0:T(8,128)(2,1)S(1)}, bf16[384,512]{1,0:T(8,128)(2,1)S(1)}, u32[]{:S(2)}, u32[]{:S(2)}) collective-permute-start(bf16[384,512]{1,0:T(8,128)(2,1)S(1)} %get-tuple-element.30), channel_id=1, source_target_pairs={{0,4},{2,6},{4,0},{6,2},{1,5},{3,7},{5,1},{7,3},{8,12},{10,14},{12... | collective-permute-start | bytes 1179656 | tf_op jit(solution)/shard_map/ppermute | solution.py:54
  92.4 1.8 %collective-permute-start.21 = (bf16[384,512]{1,0:T(8,128)(2,1)S(1)}, bf16[384,512]{1,0:T(8,128)(2,1)S(1)}, u32[]{:S(2)}, u32[]{:S(2)}) collective-permute-start(bf16[384,512]{1,0:T(8,128)(2,1)S(1)} %shard_map.81.refs_1_.refs_5_), channel_id=1, source_target_pairs={{0,2},{2,0},{4,6},{6,4},{1,3},{3,1},{5,7},{7,5},{8,10},{10,8},{12,... | collective-permute-start | bytes 1179656 | tf_op jit(solution)/shard_map/ppermute | solution.py:67
  98.5 4.9 %collective-permute-start.22 = (bf16[384,512]{1,0:T(8,128)(2,1)S(1)}, bf16[384,512]{1,0:T(8,128)(2,1)S(1)}, u32[]{:S(2)}, u32[]{:S(2)}) collective-permute-start(bf16[384,512]{1,0:T(8,128)(2,1)S(1)} %shard_map.85.refs_1_.refs_6_), channel_id=1, source_target_pairs={{0,2},{2,0},{4,6},{6,4},{1,3},{3,1},{5,7},{7,5},{8,10},{10,8},{12,... | collective-permute-start | bytes 1179656 | tf_op jit(solution)/shard_map/ppermute | solution.py:67

commit v4 on v3

--- a/solution.py
+++ b/solution.py
@@ -76,13 +76,9 @@
     return lax.optimization_barrier((value, earlier))[0]
 
 
-def look_up(long_table, long_index, table, index):
-    size = long_table.shape[0]
-    table = jnp.pad(table, (0, size - table.shape[0]))
-    at = lax.broadcasted_iota(jnp.int32, (1, size), 1)
-    first = jnp.where(long_index[:, None] == at, long_table[None, :], 0.0)
-    second = jnp.where(index[:, None] == at, table[None, :], 0.0)
-    return jnp.sum(first + second, axis=1)
+def look_up(table, index):
+    hit = index[:, None] == lax.broadcasted_iota(jnp.int32, (1, table.shape[0]), 1)
+    return jnp.sum(jnp.where(hit, table[None, :], 0.0), axis=1)
 
 
 def split_rows(value):
@@ -146,7 +142,7 @@
     )(*operands)
 
 
-def finish_kernel(rights, lefts, jobs, n_in, *refs):
+def finish_kernel(rights, lefts, fresh, jobs, n_in, *refs):
     place, weight = refs[:2]
     blocks = refs[2:n_in]
     acc, out, weighted, sem = refs[-4:]
@@ -164,7 +160,7 @@
     for n, (right, left) in enumerate(jobs):
         at, i, row, rows = rights[right]
         left_at, j, first, cols = lefts[left]
-        if left not in ready:
+        if left in fresh and left not in ready:
             ready.add(left)
             part = weighted.at[j, pl.ds(first, cols), :]
             weigh_rows(part, blocks[left_at], weight)
@@ -175,15 +171,19 @@
         put(n).wait()
 
 
-def finish(place, weight, rights, lefts, jobs, acc, out, tokens=()):
+def finish(place, weight, rights, lefts, fresh, jobs, state, tokens=()):
     near = pl.BlockSpec(memory_space=pltpu.VMEM)
     far = pl.BlockSpec(memory_space=pltpu.HBM)
+    acc, weighted, out = state
     sub, span = acc.shape[2], weight.shape[1]
     blocks, where = [], []
     for parts, used in ((rights, {r for r, _ in jobs}), (lefts, {l for _, l in jobs})):
         where.append({})
         for name in sorted(used):
             block, *at = parts[name]
+            if parts is lefts and name not in fresh:
+                where[-1][name] = (None, *at)
+                continue
             if not any(block is other for other in blocks):
                 blocks.append(block)
             index = [block is other for other in blocks].index(True)
@@ -194,25 +194,23 @@
     operands.append(in_vmem(acc))
     in_specs = [pl.BlockSpec(memory_space=pltpu.SMEM)] + [near] * n_in
     if out is not None:
-        aliases[len(operands)] = 1
-        operands.append(out)
-        in_specs.append(far)
+        aliases |= {len(operands): 1, len(operands) + 1: 2}
+        operands += [out, in_vmem(weighted)]
+        in_specs += [far, near]
     operands += tokens
     in_specs += [near] * len(tokens)
     area = sum(where[0][r][-1] * where[1][l][-1] for r, l in jobs)
     return pl.pallas_call(
-        functools.partial(finish_kernel, *where, jobs, n_in),
+        functools.partial(finish_kernel, *where, fresh, jobs, n_in),
         out_shape=[
             pltpu.VMEM(acc.shape, acc.dtype),
             jax.ShapeDtypeStruct((4, sub, 2 * sub), jnp.float32),
+            pltpu.VMEM((2, sub, span), jnp.bfloat16),
         ],
         in_specs=in_specs,
-        out_specs=[near, far],
+        out_specs=[near, far, near],
         input_output_aliases=aliases,
-        scratch_shapes=[
-            pltpu.VMEM((2, sub, span), jnp.bfloat16),
-            pltpu.SemaphoreType.DMA((len(jobs),)),
-        ],
+        scratch_shapes=[pltpu.SemaphoreType.DMA((len(jobs),))],
         cost_estimate=pl.CostEstimate(
             flops=2 * area * span, bytes_accessed=4 * area, transcendentals=0
         ),
@@ -298,7 +296,7 @@
     y[0] = across_row(own)
     own_swap = other_core(own)
 
-    gap = look_up(vir_height, vir_index, occ_depth, occ_index)
+    gap = look_up(vir_height, vir_index) + look_up(occ_depth, occ_index)
     marked = mark(own, split_rows(gap))
     near_1 = along_line(OUTER)(marked)
     near_2 = along_line(INNER)(marked)
@@ -340,9 +338,9 @@
     got = lag((last, swap_2), LAGS[1], tokens)
     mine_3 = jnp.where(after(end, got, added), last, far_2)
     cut = sub // 2
-    halves = [(mine_3[:cut], 0), (mine_3[cut:sub], cut)]
-    x[3] = [across_col(half) for half, _ in halves]
-    y[3] = [across_row(half) for half, _ in halves]
+    parts = [(mine_3[:cut], 0, cut), (mine_3[cut:sub], cut, sub - cut)]
+    x[3] = [across_col(part) for part, _, _ in parts]
+    y[3] = [across_row(part) for part, _, _ in parts]
     swap_3 = other_core(mine_3)
     acc, _ = add(
         mine_2, swap_2, x[2], y[2], acc, lag((mine_3,), 0.1, tokens), COSTS[2]
@@ -352,23 +350,31 @@
     rights = {"own": (mine_3, 0, 0, sub), "swap": (swap_3, 1, 0, sub)}
     lefts = {"own": (mine_3, 0, 0, sub)}
     jobs = (("own", "own"), ("swap", "own"))
-    acc, out = finish(place, weight, rights, lefts, jobs, acc, None)
-    for n, (_, first) in enumerate(halves):
+    state = finish(
+        place, weight, rights, lefts, ("own",), jobs, (acc, None, None)
+    )
+    for n, (_, first, size) in enumerate(parts):
+        acc, out, weighted = state
         token = lag((acc,), 0.1, tokens)
         left, right = gate(x[3][n], token), gate(y[3][n], token)
-        here = after(place, lag((left, right), 16.0 if n == 0 else 4.0, tokens))
-        rights |= {f"y{n}": (right, 2, first, cut), f"s{n}": (other_core(right), 3, first, cut)}
-        lefts[f"x{n}"] = (left, 1, first, cut)
+        here = after(place, lag((left, right), 16.0, tokens))
+        rights[f"y{n}"] = (right, 2, first, size)
+        rights[f"s{n}"] = (other_core(right), 3, first, size)
+        lefts[f"x{n}"] = (left, 1, first, size)
+        state = acc, weighted, out
         if n == 0:
             jobs = (("own", "x0"), ("swap", "x0"), ("y0", "own"), ("y0", "x0"))
             jobs += (("s0", "own"), ("s0", "x0"))
-            acc, out = finish(here, weight, rights, lefts, jobs, acc, out)
+            state = finish(here, weight, rights, lefts, ("x0",), jobs, state)
         else:
             jobs = (("own", "x1"), ("swap", "x1"), ("y1", "own"), ("y1", "x0"))
             jobs += (("y1", "x1"), ("y0", "x1"), ("s0", "x1"))
-            acc, out = finish(here, weight, rights, lefts, jobs, acc, out)
+            acc, out, weighted = finish(
+                here, weight, rights, lefts, ("x1",), jobs, state
+            )
             jobs = (("s1", "own"), ("s1", "x0"), ("s1", "x1"))
-            acc, out = finish(place, weight, rights, lefts, jobs, acc, out, tokens)
+            state = acc, weighted, out
+            _, out, _ = finish(place, weight, rights, lefts, (), jobs, state, tokens)
     return out.reshape(1, 4, 1, sub, 2 * sub)
 
 

time: 107 us -> 103 us (0.963)
  waiting for transfers between devices: 42.1 us -> 40.2 us
  Pallas kernels: 36.5 us -> 34.7 us
    ppermute x5, waiting for transfers between devices: 26.9 us -> 23.7 us  [across_row(): return lax.ppermute(value, 'row', [(i, (i + 2) % 4) for i in range(4)])]
    pallas_call x4, Pallas kernels: 16.2 us -> 14.5 us  [finish(): pl.pallas_call(functools.partial(finish_kernel, *where, fresh, jobs, n_in...]
    reduce_sum x1 -> x2, other arithmetic: 1.91 us -> 2.23 us  [look_up(): return jnp.sum(jnp.where(hit, table[None, :], 0.0), axis=1)]
where the time goes in v4:
time: 103 us
  waiting for transfers between devices  40.2 us (39%)
  Pallas kernels  34.7 us (34%)
  starting transfers between devices  24.3 us (24%)
  other arithmetic  2.62 us (3%)
  between operations  1.15 us (1%)
    ppermute x5, waiting for transfers between devices, across_row(): return lax.ppermute(value, 'row', [(i, (i + 2) % 4) for i in range(4)])  23.7 us
    pallas_call x3, Pallas kernels, add_slot(): pl.pallas_call(functools.partial(slot_kernel, acc is None), out_shape=plt...  18.9 us
    pallas_call x4, Pallas kernels, finish(): pl.pallas_call(functools.partial(finish_kernel, *where, fresh, jobs, n_in...  14.5 us
    ppermute x5, waiting for transfers between devices, along_line(): return lambda value: lax.ppermute(value, 'freq', hops)  14.2 us
    ppermute x5, starting transfers between devices, along_line(): return lambda value: lax.ppermute(value, 'freq', hops)  11.3 us
    ppermute x5, starting transfers between devices, across_col(): return lax.ppermute(value, 'col', [(0, 1), (1, 0)])  5.86 us
    ppermute x5, starting transfers between devices, across_row(): return lax.ppermute(value, 'row', [(i, (i + 2) % 4) for i in range(4)])  5.7 us
    reduce_sum x2, other arithmetic, look_up(): return jnp.sum(jnp.where(hit, table[None, :], 0.0), axis=1)  2.23 us
  transfers between devices with their start and end apart: 24, of which 6 were waited for; matrix products, arithmetic and copies ran while one was open for 0% of the time, Pallas kernels for 30%

profile of v4, /device:TPU:0, one launch (start us, length us, event | category | flops | bytes accessed | tf_op | source)
XLA Modules:
  0.0 103.1 jit_solution(2723439905536673082)
XLA Ops:
  0.0 1.3 %select_reduce_fusion = f32[512]{0:T(512)S(1)} fusion(f32[1792]{0:T(1024)} %param.10, s32[512]{0:T(512)} %param.8), kind=kLoop, calls=%fused_computation | loop fusion | flops 2752000 | bytes 11264 | tf_op jit(solution)/shard_map/reduce_sum | solution.py:81
  1.3 0.9 select_reduce_fusion.1
  2.3 1.3 %shard_map.64.refs_0_ = bf16[784,512]{1,0:T(8,128)(2,1)S(1)} custom-call(bf16[768,512]{1,0:T(8,128)(2,1)} %block.1, bf16[16,512]{1,0:T(8,128)(2,1)S(1)} %fusion.4.rows), custom_call_target="tpu_custom_call" | custom-call | tf_op jit(solution)/shard_map/pallas_call | solution.py:237
  4.3 5.9 %collective-permute-start = (bf16[784,512]{1,0:T(8,128)(2,1)S(1)}, bf16[784,512]{1,0:T(8,128)(2,1)S(1)}, u32[]{:S(2)}, u32[]{:S(2)}) collective-permute-start(bf16[784,512]{1,0:T(8,128)(2,1)S(1)} %shard_map.64.refs_0_), channel_id=1, source_target_pairs={{0,8},{8,0},{16,24},{24,16},{1,9},{9,1},{17,25},{25,17},{2,10},{10... | collective-permute-start | bytes 2408456 | tf_op jit(solution)/shard_map/ppermute | solution.py:58
  10.1 1.5 %collective-permute-start.7 = (bf16[768,512]{1,0:T(8,128)(2,1)}, bf16[768,512]{1,0:T(8,128)(2,1)}, u32[]{:S(2)}, u32[]{:S(2)}) collective-permute-start(bf16[768,512]{1,0:T(8,128)(2,1)} %block.1), channel_id=1, source_target_pairs={{0,4},{2,6},{4,0},{6,2},{1,5},{3,7},{5,1},{7,3},{8,12},{10,14},{12... | collective-permute-start | bytes 2359304 | tf_op jit(solution)/shard_map/ppermute | solution.py:54
  11.6 1.5 %collective-permute-start.9 = (bf16[768,512]{1,0:T(8,128)(2,1)}, bf16[768,512]{1,0:T(8,128)(2,1)}, u32[]{:S(2)}, u32[]{:S(2)}) collective-permute-start(bf16[768,512]{1,0:T(8,128)(2,1)} %block.1), channel_id=1, source_target_pairs={{0,1},{1,0},{2,3},{3,2},{4,5},{5,4},{6,7},{7,6},{8,9},{9,8},{10,11... | collective-permute-start | bytes 2359304 | tf_op jit(solution)/shard_map/ppermute | solution.py:50
  13.9 15.3 %collective-permute-done.7.refs_2_ = bf16[768,512]{1,0:T(8,128)(2,1)} collective-permute-done((bf16[768,512]{1,0:T(8,128)(2,1)}, bf16[768,512]{1,0:T(8,128)(2,1)}, u32[]{:S(2)}, u32[]{:S(2)}) %collective-permute-start.7) | collective-permute-done | bytes 786464 | tf_op jit(solution)/shard_map/ppermute | solution.py:54
  29.8 1.5 %collective-permute-start.11 = (bf16[784,512]{1,0:T(8,128)(2,1)S(1)}, bf16[784,512]{1,0:T(8,128)(2,1)S(1)}, u32[]{:S(2)}, u32[]{:S(2)}) collective-permute-start(bf16[784,512]{1,0:T(8,128)(2,1)S(1)} %broadcast_select_fusion.2.refs_0_), channel_id=1, source_target_pairs={{0,4},{2,6},{4,0},{6,2},{1,5},{3,7},{5,1},{7,3},{8,12},{10,14},{12... | collective-permute-start | bytes 2408456 | tf_op jit(solution)/shard_map/ppermute | solution.py:54
  31.4 1.6 %collective-permute-start.13 = (bf16[784,512]{1,0:T(8,128)(2,1)S(1)}, bf16[784,512]{1,0:T(8,128)(2,1)S(1)}, u32[]{:S(2)}, u32[]{:S(2)}) collective-permute-start(bf16[784,512]{1,0:T(8,128)(2,1)S(1)} %broadcast_select_fusion.2.refs_0_), channel_id=1, source_target_pairs={{0,1},{1,0},{2,3},{3,2},{4,5},{5,4},{6,7},{7,6},{8,9},{9,8},{10,11... | collective-permute-start | bytes 2408456 | tf_op jit(solution)/shard_map/ppermute | solution.py:50
  34.0 7.2 %shard_map.69.refs_0_.refs_5_ = f32[2,4,768,768]{3,2,1,0:T(8,128)S(1)} custom-call(f32[8,128]{1,0:T(8,128)S(1)} %shard_map.68.token.refs_8_, f32[1,512]{1,0:T(1,128)S(1)} %add_divide_fusion.3.weight, bf16[784,512]{1,0:T(8,128)(2,1)S(1)} %shard_map.64.refs_0_, bf16[768,512]{1,0:T(8,128)(2,1)S(1)} %collective-permute-done.6.refs_1_, ...), custom_call_target="tpu_custom_call" | custom-call | flops 57982058496 | tf_op jit(solution)/shard_map/pallas_call | solution.py:131
  41.2 8.5 %collective-permute-done.11.value = bf16[784,512]{1,0:T(8,128)(2,1)S(1)} collective-permute-done((bf16[784,512]{1,0:T(8,128)(2,1)S(1)}, bf16[784,512]{1,0:T(8,128)(2,1)S(1)}, u32[]{:S(2)}, u32[]{:S(2)}) %collective-permute-start.11) | collective-permute-done | bytes 802848 | tf_op jit(solution)/shard_map/ppermute | solution.py:54
  49.7 2.6 %collective-permute-done.4.refs_0_ = bf16[784,512]{1,0:T(8,128)(2,1)S(1)} collective-permute-done((bf16[784,512]{1,0:T(8,128)(2,1)S(1)}, bf16[784,512]{1,0:T(8,128)(2,1)S(1)}, u32[]{:S(2)}, u32[]{:S(2)}) %collective-permute-start.4) | collective-permute-done | bytes 802848 | tf_op jit(solution)/shard_map/ppermute | solution.py:58
  53.0 3.6 %collective-permute-start.2 = (bf16[784,512]{1,0:T(8,128)(2,1)S(1)}, bf16[784,512]{1,0:T(8,128)(2,1)S(1)}, u32[]{:S(2)}, u32[]{:S(2)}) collective-permute-start(bf16[784,512]{1,0:T(8,128)(2,1)S(1)} %collective-permute-done.1.refs_1_), channel_id=1, source_target_pairs={{0,8},{8,0},{16,24},{24,16},{1,9},{9,1},{17,25},{25,17},{2,10},{10... | collective-permute-start | bytes 2408456 | tf_op jit(solution)/shard_map/ppermute | solution.py:58
  56.7 0.7 collective-permute-start.19
  57.4 5.8 %shard_map.74.refs_0_.refs_5_ = f32[2,4,768,768]{3,2,1,0:T(8,128)S(1)} custom-call(f32[8,128]{1,0:T(8,128)S(1)} %shard_map.72.token.refs_11_, f32[1,512]{1,0:T(1,128)S(1)} %add_divide_fusion.2.weight, bf16[784,512]{1,0:T(8,128)(2,1)S(1)} %broadcast_select_fusion.2.refs_0_, ...), custom_call_target="tpu_custom_call", output_to_operand_aliasing={{}: (7, {})} | custom-call | flops 4831838208 | tf_op jit(solution)/shard_map/pallas_call | solution.py:131
  63.3 11.6 %collective-permute-done.2.refs_0_ = bf16[784,512]{1,0:T(8,128)(2,1)S(1)} collective-permute-done((bf16[784,512]{1,0:T(8,128)(2,1)S(1)}, bf16[784,512]{1,0:T(8,128)(2,1)S(1)}, u32[]{:S(2)}, u32[]{:S(2)}) %collective-permute-start.2) | collective-permute-done | bytes 802848 | tf_op jit(solution)/shard_map/ppermute | solution.py:58
  75.6 1.6 %collective-permute-start.20 = (bf16[384,512]{1,0:T(8,128)(2,1)S(1)}, bf16[384,512]{1,0:T(8,128)(2,1)S(1)}, u32[]{:S(2)}, u32[]{:S(2)}) collective-permute-start(bf16[384,512]{1,0:T(8,128)(2,1)S(1)} %get-tuple-element.35), channel_id=1, source_target_pairs={{0,4},{2,6},{4,0},{6,2},{1,5},{3,7},{5,1},{7,3},{8,12},{10,14},{12... | collective-permute-start | bytes 1179656 | tf_op jit(solution)/shard_map/ppermute | solution.py:54
  77.9 1.4 %collective-permute-start.23 = (bf16[384,512]{1,0:T(8,128)(2,1)S(1)}, bf16[384,512]{1,0:T(8,128)(2,1)S(1)}, u32[]{:S(2)}, u32[]{:S(2)}) collective-permute-start(bf16[384,512]{1,0:T(8,128)(2,1)S(1)} %get-tuple-element.36), channel_id=1, source_target_pairs={{0,1},{1,0},{2,3},{3,2},{4,5},{5,4},{6,7},{7,6},{8,9},{9,8},{10,11... | collective-permute-start | bytes 1179656 | tf_op jit(solution)/shard_map/ppermute | solution.py:50
  79.8 6.0 %shard_map.77.refs_4_.refs_0_ = f32[2,4,768,768]{3,2,1,0:T(8,128)S(1)} custom-call(f32[8,128]{1,0:T(8,128)S(1)} %shard_map.76.token.refs_14_, f32[1,512]{1,0:T(1,128)S(1)} %add_divide_fusion.weight, bf16[784,512]{1,0:T(8,128)(2,1)S(1)} %broadcast_select_fusion.1.refs_0_, ...), custom_call_target="tpu_custom_call", output_to_operand_aliasing={{}: (7, {})} | custom-call | flops 4831838208 | tf_op jit(solution)/shard_map/pallas_call | solution.py:131
  85.8 4.0 %shard_map.78 = (f32[2,4,768,768]{3,2,1,0:T(8,128)S(1)}, f32[4,768,1536]{2,1,0:T(8,128)}, bf16[2,768,512]{2,1,0:T(8,128)(2,1)S(1)}) custom-call(s32[5]{0:T(128)S(1)} %stack.30.refs_0_, f32[1,512]{1,0:T(1,128)S(1)} %add_divide_fusion.1.refs_1_, bf16[784,512]{1,0:T(8,128)(2,1)S(1)} %broadcast_select_fusion.refs_0_.refs_2_, ...), custom_call_target="tpu_custom_call", output_to_operand_aliasing={{0}: (4, {})} | custom-call | flops 1207959552 | bytes 4718592 | tf_op jit(solution)/shard_map/pallas_call | solution.py:203
  90.0 1.7 %collective-permute-done.21.refs_3_ = bf16[384,512]{1,0:T(8,128)(2,1)S(1)} collective-permute-done((bf16[384,512]{1,0:T(8,128)(2,1)S(1)}, bf16[384,512]{1,0:T(8,128)(2,1)S(1)}, u32[]{:S(2)}, u32[]{:S(2)}) %collective-permute-start.21) | collective-permute-done | bytes 393248 | tf_op jit(solution)/shard_map/ppermute | solution.py:67
  91.7 4.0 %shard_map.83 = (f32[2,4,768,768]{3,2,1,0:T(8,128)S(1)}, f32[4,768,1536]{2,1,0:T(8,128)}, bf16[2,768,512]{2,1,0:T(8,128)(2,1)S(1)}) custom-call(s32[5]{0:T(128)S(1)} %stack.30.refs_0_, f32[1,512]{1,0:T(1,128)S(1)} %add_divide_fusion.1.refs_1_, ...), custom_call_target="tpu_custom_call", output_to_operand_aliasing={{0}: (7, {}), {1}: (8, {}), {2}: (9, {})} | custom-call | flops 1509949440 | bytes 5898240 | tf_op jit(solution)/shard_map/pallas_call | solution.py:203
  96.4 3.9 %shard_map.88 = (f32[2,4,768,768]{3,2,1,0:T(8,128)S(1)}, f32[4,768,1536]{2,1,0:T(8,128)}, bf16[2,768,512]{2,1,0:T(8,128)(2,1)S(1)}) custom-call(s32[5]{0:T(128)S(1)} %stack.30.refs_0_, f32[1,512]{1,0:T(1,128)S(1)} %add_divide_fusion.1.refs_1_, ...), custom_call_target="tpu_custom_call", output_to_operand_aliasing={{0}: (8, {}), {1}: (9, {}), {2}: (10, {})} | custom-call | flops 1509949440 | bytes 5898240 | tf_op jit(solution)/shard_map/pallas_call | solution.py:203
  100.3 2.6 %shard_map.90 = (f32[2,4,768,768]{3,2,1,0:T(8,128)S(1)}, f32[4,768,1536]{2,1,0:T(8,128)}, bf16[2,768,512]{2,1,0:T(8,128)(2,1)S(1)}) custom-call(s32[5]{0:T(128)S(1)} %stack.30.refs_0_, f32[1,512]{1,0:T(1,128)S(1)} %add_divide_fusion.1.refs_1_, ...), custom_call_target="tpu_custom_call", output_to_operand_aliasing={{0}: (3, {}), {1}: (4, {}), {2}: (5, {})} | custom-call | flops 603979776 | bytes 2359296 | tf_op jit(solution)/shard_map/pallas_call | solution.py:203
  (69 shorter events, 6.1 us)
Async XLA Ops:
  3.5 25.6 %collective-permute-start.3 = (bf16[784,512]{1,0:T(8,128)(2,1)S(1)}, bf16[784,512]{1,0:T(8,128)(2,1)S(1)}, u32[]{:S(2)}, u32[]{:S(2)}) collective-permute-start(bf16[784,512]{1,0:T(8,128)(2,1)S(1)} %shard_map.64.refs_0_), channel_id=1, source_target_pairs={{0,0},{8,16},{16,8},{24,24},{1,1},{9,17},{17,9},{25,25},{2,2},{10,... | collective-permute-start | bytes 2408456 | tf_op jit(solution)/shard_map/ppermute | solution.py:58
  4.3 24.9 %collective-permute-start = (bf16[784,512]{1,0:T(8,128)(2,1)S(1)}, bf16[784,512]{1,0:T(8,128)(2,1)S(1)}, u32[]{:S(2)}, u32[]{:S(2)}) collective-permute-start(bf16[784,512]{1,0:T(8,128)(2,1)S(1)} %shard_map.64.refs_0_), channel_id=1, source_target_pairs={{0,8},{8,0},{16,24},{24,16},{1,9},{9,1},{17,25},{25,17},{2,10},{10... | collective-permute-start | bytes 2408456 | tf_op jit(solution)/shard_map/ppermute | solution.py:58
  10.1 19.0 %collective-permute-start.7 = (bf16[768,512]{1,0:T(8,128)(2,1)}, bf16[768,512]{1,0:T(8,128)(2,1)}, u32[]{:S(2)}, u32[]{:S(2)}) collective-permute-start(bf16[768,512]{1,0:T(8,128)(2,1)} %block.1), channel_id=1, source_target_pairs={{0,4},{2,6},{4,0},{6,2},{1,5},{3,7},{5,1},{7,3},{8,12},{10,14},{12... | collective-permute-start | bytes 2359304 | tf_op jit(solution)/shard_map/ppermute | solution.py:54
  11.6 19.7 %collective-permute-start.6 = (bf16[768,512]{1,0:T(8,128)(2,1)}, bf16[768,512]{1,0:T(8,128)(2,1)S(1)}, u32[]{:S(2)}, u32[]{:S(2)}) collective-permute-start(bf16[768,512]{1,0:T(8,128)(2,1)} %block.1), channel_id=1, source_target_pairs={{0,2},{2,0},{4,6},{6,4},{1,3},{3,1},{5,7},{7,5},{8,10},{10,8},{12,... | collective-permute-start | bytes 2359304 | tf_op jit(solution)/shard_map/ppermute | solution.py:67
  11.6 21.3 %collective-permute-start.9 = (bf16[768,512]{1,0:T(8,128)(2,1)}, bf16[768,512]{1,0:T(8,128)(2,1)}, u32[]{:S(2)}, u32[]{:S(2)}) collective-permute-start(bf16[768,512]{1,0:T(8,128)(2,1)} %block.1), channel_id=1, source_target_pairs={{0,1},{1,0},{2,3},{3,2},{4,5},{5,4},{6,7},{7,6},{8,9},{9,8},{10,11... | collective-permute-start | bytes 2359304 | tf_op jit(solution)/shard_map/ppermute | solution.py:50
  29.2 4.2 %collective-permute-start.8 = (bf16[768,512]{1,0:T(8,128)(2,1)}, bf16[768,512]{1,0:T(8,128)(2,1)}, u32[]{:S(2)}, u32[]{:S(2)}) collective-permute-start(bf16[768,512]{1,0:T(8,128)(2,1)} %collective-permute-done.7.refs_2_), channel_id=1, source_target_pairs={{0,2},{2,0},{4,6},{6,4},{1,3},{3,1},{5,7},{7,5},{8,10},{10,8},{12,... | collective-permute-start | bytes 2359304 | tf_op jit(solution)/shard_map/ppermute | solution.py:67
  29.3 20.4 %collective-permute-start.5 = (bf16[784,512]{1,0:T(8,128)(2,1)S(1)}, bf16[784,512]{1,0:T(8,128)(2,1)S(1)}, u32[]{:S(2)}, u32[]{:S(2)}) collective-permute-start(bf16[784,512]{1,0:T(8,128)(2,1)S(1)} %broadcast_select_fusion.2.refs_0_), channel_id=1, source_target_pairs={{0,2},{2,0},{4,6},{6,4},{1,3},{3,1},{5,7},{7,5},{8,10},{10,8},{12,... | collective-permute-start | bytes 2408456 | tf_op jit(solution)/shard_map/ppermute | solution.py:67
  29.8 19.9 %collective-permute-start.11 = (bf16[784,512]{1,0:T(8,128)(2,1)S(1)}, bf16[784,512]{1,0:T(8,128)(2,1)S(1)}, u32[]{:S(2)}, u32[]{:S(2)}) collective-permute-start(bf16[784,512]{1,0:T(8,128)(2,1)S(1)} %broadcast_select_fusion.2.refs_0_), channel_id=1, source_target_pairs={{0,4},{2,6},{4,0},{6,2},{1,5},{3,7},{5,1},{7,3},{8,12},{10,14},{12... | collective-permute-start | bytes 2408456 | tf_op jit(solution)/shard_map/ppermute | solution.py:54
  31.4 25.3 %collective-permute-start.13 = (bf16[784,512]{1,0:T(8,128)(2,1)S(1)}, bf16[784,512]{1,0:T(8,128)(2,1)S(1)}, u32[]{:S(2)}, u32[]{:S(2)}) collective-permute-start(bf16[784,512]{1,0:T(8,128)(2,1)S(1)} %broadcast_select_fusion.2.refs_0_), channel_id=1, source_target_pairs={{0,1},{1,0},{2,3},{3,2},{4,5},{5,4},{6,7},{7,6},{8,9},{9,8},{10,11... | collective-permute-start | bytes 2408456 | tf_op jit(solution)/shard_map/ppermute | solution.py:50
  33.0 19.3 %collective-permute-start.4 = (bf16[784,512]{1,0:T(8,128)(2,1)S(1)}, bf16[784,512]{1,0:T(8,128)(2,1)S(1)}, u32[]{:S(2)}, u32[]{:S(2)}) collective-permute-start(bf16[784,512]{1,0:T(8,128)(2,1)S(1)} %collective-permute-done.3.refs_0_.refs_1_), channel_id=1, source_target_pairs={{0,8},{8,0},{16,24},{24,16},{1,9},{9,1},{17,25},{25,17},{2,10},{10... | collective-permute-start | bytes 2408456 | tf_op jit(solution)/shard_map/ppermute | solution.py:58
  33.3 19.0 %collective-permute-start.1 = (bf16[784,512]{1,0:T(8,128)(2,1)S(1)}, bf16[784,512]{1,0:T(8,128)(2,1)S(1)}, u32[]{:S(2)}, u32[]{:S(2)}) collective-permute-start(bf16[784,512]{1,0:T(8,128)(2,1)S(1)} %collective-permute-done.refs_0_), channel_id=1, source_target_pairs={{0,0},{8,16},{16,8},{24,24},{1,1},{9,17},{17,9},{25,25},{2,2},{10,... | collective-permute-start | bytes 2408456 | tf_op jit(solution)/shard_map/ppermute | solution.py:58
  49.7 7.7 %collective-permute-start.12 = (bf16[784,512]{1,0:T(8,128)(2,1)S(1)}, bf16[784,512]{1,0:T(8,128)(2,1)S(1)}, u32[]{:S(2)}, u32[]{:S(2)}) collective-permute-start(bf16[784,512]{1,0:T(8,128)(2,1)S(1)} %shard_map.73.refs_2_), channel_id=1, source_target_pairs={{0,2},{2,0},{4,6},{6,4},{1,3},{3,1},{5,7},{7,5},{8,10},{10,8},{12,... | collective-permute-start | bytes 2408456 | tf_op jit(solution)/shard_map/ppermute | solution.py:67
  52.4 10.8 %collective-permute-start.10 = (bf16[784,512]{1,0:T(8,128)(2,1)S(1)}, bf16[784,512]{1,0:T(8,128)(2,1)S(1)}, u32[]{:S(2)}, u32[]{:S(2)}) collective-permute-start(bf16[784,512]{1,0:T(8,128)(2,1)S(1)} %broadcast_select_fusion.1.refs_0_), channel_id=1, source_target_pairs={{0,2},{2,0},{4,6},{6,4},{1,3},{3,1},{5,7},{7,5},{8,10},{10,8},{12,... | collective-permute-start | bytes 2408456 | tf_op jit(solution)/shard_map/ppermute | solution.py:67
  52.5 22.4 %collective-permute-start.17 = (bf16[784,512]{1,0:T(8,128)(2,1)S(1)}, bf16[784,512]{1,0:T(8,128)(2,1)S(1)}, u32[]{:S(2)}, u32[]{:S(2)}) collective-permute-start(bf16[784,512]{1,0:T(8,128)(2,1)S(1)} %broadcast_select_fusion.1.refs_0_), channel_id=1, source_target_pairs={{0,4},{2,6},{4,0},{6,2},{1,5},{3,7},{5,1},{7,3},{8,12},{10,14},{12... | collective-permute-start | bytes 2408456 | tf_op jit(solution)/shard_map/ppermute | solution.py:54
  53.0 21.8 %collective-permute-start.2 = (bf16[784,512]{1,0:T(8,128)(2,1)S(1)}, bf16[784,512]{1,0:T(8,128)(2,1)S(1)}, u32[]{:S(2)}, u32[]{:S(2)}) collective-permute-start(bf16[784,512]{1,0:T(8,128)(2,1)S(1)} %collective-permute-done.1.refs_1_), channel_id=1, source_target_pairs={{0,8},{8,0},{16,24},{24,16},{1,9},{9,1},{17,25},{25,17},{2,10},{10... | collective-permute-start | bytes 2408456 | tf_op jit(solution)/shard_map/ppermute | solution.py:58
  56.7 21.2 %collective-permute-start.19 = (bf16[784,512]{1,0:T(8,128)(2,1)S(1)}, bf16[784,512]{1,0:T(8,128)(2,1)S(1)}, u32[]{:S(2)}, u32[]{:S(2)}) collective-permute-start(bf16[784,512]{1,0:T(8,128)(2,1)S(1)} %broadcast_select_fusion.1.refs_0_), channel_id=1, source_target_pairs={{0,1},{1,0},{2,3},{3,2},{4,5},{5,4},{6,7},{7,6},{8,9},{9,8},{10,11... | collective-permute-start | bytes 2408456 | tf_op jit(solution)/shard_map/ppermute | solution.py:50
  74.9 4.4 %collective-permute-start.18 = (bf16[784,512]{1,0:T(8,128)(2,1)S(1)}, bf16[784,512]{1,0:T(8,128)(2,1)S(1)}, u32[]{:S(2)}, u32[]{:S(2)}) collective-permute-start(bf16[784,512]{1,0:T(8,128)(2,1)S(1)} %collective-permute-done.17.refs_2_), channel_id=1, source_target_pairs={{0,2},{2,0},{4,6},{6,4},{1,3},{3,1},{5,7},{7,5},{8,10},{10,8},{12,... | collective-permute-start | bytes 2408456 | tf_op jit(solution)/shard_map/ppermute | solution.py:67
  75.0 10.8 %collective-permute-start.16 = (bf16[784,512]{1,0:T(8,128)(2,1)S(1)}, bf16[784,512]{1,0:T(8,128)(2,1)S(1)}, u32[]{:S(2)}, u32[]{:S(2)}) collective-permute-start(bf16[784,512]{1,0:T(8,128)(2,1)S(1)} %broadcast_select_fusion.refs_0_.refs_2_), channel_id=1, source_target_pairs={{0,2},{2,0},{4,6},{6,4},{1,3},{3,1},{5,7},{7,5},{8,10},{10,8},{12,... | collective-permute-start | bytes 2408456 | tf_op jit(solution)/shard_map/ppermute | solution.py:67
  75.6 14.2 %collective-permute-start.20 = (bf16[384,512]{1,0:T(8,128)(2,1)S(1)}, bf16[384,512]{1,0:T(8,128)(2,1)S(1)}, u32[]{:S(2)}, u32[]{:S(2)}) collective-permute-start(bf16[384,512]{1,0:T(8,128)(2,1)S(1)} %get-tuple-element.35), channel_id=1, source_target_pairs={{0,4},{2,6},{4,0},{6,2},{1,5},{3,7},{5,1},{7,3},{8,12},{10,14},{12... | collective-permute-start | bytes 1179656 | tf_op jit(solution)/shard_map/ppermute | solution.py:54
  77.2 12.8 %collective-permute-start.15 = (bf16[384,512]{1,0:T(8,128)(2,1)S(1)}, bf16[384,512]{1,0:T(8,128)(2,1)S(1)}, u32[]{:S(2)}, u32[]{:S(2)}) collective-permute-start(bf16[384,512]{1,0:T(8,128)(2,1)S(1)} %get-tuple-element.35), channel_id=1, source_target_pairs={{0,1},{1,0},{2,3},{3,2},{4,5},{5,4},{6,7},{7,6},{8,9},{9,8},{10,11... | collective-permute-start | bytes 1179656 | tf_op jit(solution)/shard_map/ppermute | solution.py:50
  77.9 18.5 %collective-permute-start.23 = (bf16[384,512]{1,0:T(8,128)(2,1)S(1)}, bf16[384,512]{1,0:T(8,128)(2,1)S(1)}, u32[]{:S(2)}, u32[]{:S(2)}) collective-permute-start(bf16[384,512]{1,0:T(8,128)(2,1)S(1)} %get-tuple-element.36), channel_id=1, source_target_pairs={{0,1},{1,0},{2,3},{3,2},{4,5},{5,4},{6,7},{7,6},{8,9},{9,8},{10,11... | collective-permute-start | bytes 1179656 | tf_op jit(solution)/shard_map/ppermute | solution.py:50
  79.3 16.3 %collective-permute-start.14 = (bf16[384,512]{1,0:T(8,128)(2,1)S(1)}, bf16[384,512]{1,0:T(8,128)(2,1)S(1)}, u32[]{:S(2)}, u32[]{:S(2)}) collective-permute-start(bf16[384,512]{1,0:T(8,128)(2,1)S(1)} %get-tuple-element.36), channel_id=1, source_target_pairs={{0,4},{2,6},{4,0},{6,2},{1,5},{3,7},{5,1},{7,3},{8,12},{10,14},{12... | collective-permute-start | bytes 1179656 | tf_op jit(solution)/shard_map/ppermute | solution.py:54
  89.9 1.8 %collective-permute-start.21 = (bf16[384,512]{1,0:T(8,128)(2,1)S(1)}, bf16[384,512]{1,0:T(8,128)(2,1)S(1)}, u32[]{:S(2)}, u32[]{:S(2)}) collective-permute-start(bf16[384,512]{1,0:T(8,128)(2,1)S(1)} %shard_map.81.refs_1_.refs_5_), channel_id=1, source_target_pairs={{0,2},{2,0},{4,6},{6,4},{1,3},{3,1},{5,7},{7,5},{8,10},{10,8},{12,... | collective-permute-start | bytes 1179656 | tf_op jit(solution)/shard_map/ppermute | solution.py:67
  95.7 4.6 %collective-permute-start.22 = (bf16[384,512]{1,0:T(8,128)(2,1)S(1)}, bf16[384,512]{1,0:T(8,128)(2,1)S(1)}, u32[]{:S(2)}, u32[]{:S(2)}) collective-permute-start(bf16[384,512]{1,0:T(8,128)(2,1)S(1)} %shard_map.85.refs_1_.refs_6_), channel_id=1, source_target_pairs={{0,2},{2,0},{4,6},{6,4},{1,3},{3,1},{5,7},{7,5},{8,10},{10,8},{12,... | collective-permute-start | bytes 1179656 | tf_op jit(solution)/shard_map/ppermute | solution.py:67

commit v5 on v4

--- a/solution.py
+++ b/solution.py
@@ -252,7 +252,7 @@
     token = pl.pallas_call(
         pause_kernel,
         out_shape=jax.ShapeDtypeStruct((8, 128), jnp.float32),
-        in_specs=[pl.BlockSpec(memory_space=pltpu.VMEM)] * len(parts),
+        in_specs=[pl.BlockSpec(memory_space=pl.ANY)] * len(parts),
         out_specs=pl.BlockSpec(memory_space=pltpu.VMEM),
         cost_estimate=pl.CostEstimate(
             flops=int(micros * 1e9),
@@ -260,7 +260,7 @@
             transcendentals=0,
         ),
         compiler_params=pltpu.CompilerParams(vmem_limit_bytes=4 * 1024 * 1024),
-    )(*[pltpu.with_memory_space_constraint(v, pltpu.VMEM) for v in parts])
+    )(*parts)
     tokens.append(token)
     return token
 
@@ -300,6 +300,7 @@
     marked = mark(own, split_rows(gap))
     near_1 = along_line(OUTER)(marked)
     near_2 = along_line(INNER)(marked)
+    near_2 = gate(near_2, lag((x[0], y[0]), 0.1, tokens))
     got = lag((near_2,), 0.1, tokens)
     place = jnp.stack([col, row, row ^ 1, row ^ 2, row ^ 3]).astype(jnp.int32)
 
@@ -312,19 +313,19 @@
         gap = join_rows(block[sub:])
         return (4.0 * gap / (gap * gap + omega[0] * omega[0]))[None, :]
 
-    here = lag((near_1, near_2), LAGS[2], tokens)
+    swap_1 = other_core(near_1)
+    here = lag((near_1, near_2, swap_1), LAGS[2], tokens)
     mine_1 = jnp.where(after(group, here) >= 0, near_1, near_2)
     crossed = lag((mine_1,), 0.1, tokens)
     far_1 = along_line(TO_ENDS)(near_2)
     far_2 = along_line(INNER)(near_1)
     x[1] = across_col(mine_1)
     y[1] = across_row(mine_1)
-    swap_1 = other_core(mine_1)
     acc, added = add(
         marked, own_swap, x[0], y[0], None, crossed, COSTS[0]
     )
 
-    got_2 = lag((far_1, far_2, swap_1), LAGS[0], tokens)
+    got_2 = lag((far_2,), LAGS[0], tokens)
     mine_2 = jnp.where(after(end, got, got_2, added), far_1, near_2)
     last = along_line(TO_ENDS)(far_2)
     x[2] = across_col(mine_2)
@@ -335,13 +336,14 @@
         mine_1, swap_1, x[1], y[1], acc, lag((mine_2,), 0.1, tokens), COSTS[1]
     )
 
-    got = lag((last, swap_2), LAGS[1], tokens)
-    mine_3 = jnp.where(after(end, got, added), last, far_2)
+    got = lag((last, swap_2, added), LAGS[1], tokens)
+    mine_3 = jnp.where(after(end, got), last, far_2)
     cut = sub // 2
     parts = [(mine_3[:cut], 0, cut), (mine_3[cut:sub], cut, sub - cut)]
     x[3] = [across_col(part) for part, _, _ in parts]
     y[3] = [across_row(part) for part, _, _ in parts]
     swap_3 = other_core(mine_3)
+    y[2] = gate(y[2], added)
     acc, _ = add(
         mine_2, swap_2, x[2], y[2], acc, lag((mine_3,), 0.1, tokens), COSTS[2]
     )

time: 103 us -> 100 us (0.971)
  waiting for transfers between devices: 40.2 us -> 35.1 us
  other arithmetic: 2.62 us -> 3.75 us
    ppermute x5, waiting for transfers between devices: 23.7 us -> 7.99 us  [across_row(): return lax.ppermute(value, 'row', [(i, (i + 2) % 4) for i in range(4)])]
    ppermute x5, waiting for transfers between devices: 14.2 us -> 22.2 us  [along_line(): return lambda value: lax.ppermute(value, 'freq', hops)]
    ppermute x5, waiting for transfers between devices: 0.52 us -> 2.58 us  [across_col(): return lax.ppermute(value, 'col', [(0, 1), (1, 0)])]
    select_n x1, other arithmetic: 0.11 us -> 1.22 us  [line_device(): mine_2 = jnp.where(after(end, got, got_2, added), far_1, near_2)]
  transfers between devices with their start and end apart: 24 -> 24, of which waited for: 6 -> 10; matrix products, arithmetic and copies ran while one was open for 0% -> 2% of each run, Pallas kernels for 30% -> 31%
where the time goes in v5:
time: 100 us; the launch traced here: 99.7 us
  waiting for transfers between devices  35.1 us (35%)
  Pallas kernels  35 us (35%)
  starting transfers between devices  24.5 us (24%)
  other arithmetic  3.75 us (4%)
  between operations  1.18 us (1%)
    ppermute x5, waiting for transfers between devices, along_line(): return lambda value: lax.ppermute(value, 'freq', hops)  22.2 us
    pallas_call x3, Pallas kernels, add_slot(): pl.pallas_call(functools.partial(slot_kernel, acc is None), out_shape=plt...  19.2 us
    pallas_call x4, Pallas kernels, finish(): pl.pallas_call(functools.partial(finish_kernel, *where, fresh, jobs, n_in...  14.5 us
    ppermute x5, starting transfers between devices, along_line(): return lambda value: lax.ppermute(value, 'freq', hops)  12.2 us
    ppermute x5, waiting for transfers between devices, across_row(): return lax.ppermute(value, 'row', [(i, (i + 2) % 4) for i in range(4)])  7.99 us
    ppermute x5, starting transfers between devices, across_col(): return lax.ppermute(value, 'col', [(0, 1), (1, 0)])  6.7 us
    ppermute x5, starting transfers between devices, across_row(): return lax.ppermute(value, 'row', [(i, (i + 2) % 4) for i in range(4)])  4.78 us
    ppermute x5, waiting for transfers between devices, across_col(): return lax.ppermute(value, 'col', [(0, 1), (1, 0)])  2.58 us
  transfers between devices with their start and end apart: 24, of which 10 were waited for; matrix products, arithmetic and copies ran while one was open for 2% of the time, Pallas kernels for 31%

profile of v5, /device:TPU:0, one launch (start us, length us, event | category | flops | bytes accessed | tf_op | source)
XLA Modules:
  0.0 99.7 jit_solution(5583472423540216571)
XLA Ops:
  0.0 1.3 %select_reduce_fusion = f32[512]{0:T(512)S(1)} fusion(f32[1792]{0:T(1024)} %param.10, s32[512]{0:T(512)} %param.8), kind=kLoop, calls=%fused_computation | loop fusion | flops 2752000 | bytes 11264 | tf_op jit(solution)/shard_map/reduce_sum | solution.py:81
  3.5 3.1 %collective-permute-start = (bf16[784,512]{1,0:T(8,128)(2,1)S(1)}, bf16[784,512]{1,0:T(8,128)(2,1)S(1)}, u32[]{:S(2)}, u32[]{:S(2)}) collective-permute-start(bf16[784,512]{1,0:T(8,128)(2,1)S(1)} %shard_map.64.refs_0_), channel_id=1, source_target_pairs={{0,8},{8,0},{16,24},{24,16},{1,9},{9,1},{17,25},{25,17},{2,10},{10... | collective-permute-start | bytes 2408456 | tf_op jit(solution)/shard_map/ppermute | solution.py:58
  6.6 1.5 %collective-permute-start.5 = (bf16[768,512]{1,0:T(8,128)(2,1)}, bf16[768,512]{1,0:T(8,128)(2,1)}, u32[]{:S(2)}, u32[]{:S(2)}) collective-permute-start(bf16[768,512]{1,0:T(8,128)(2,1)} %block.1), channel_id=1, source_target_pairs={{0,4},{2,6},{4,0},{6,2},{1,5},{3,7},{5,1},{7,3},{8,12},{10,14},{12... | collective-permute-start | bytes 2359304 | tf_op jit(solution)/shard_map/ppermute | solution.py:54
  8.9 1.6 %collective-permute-start.4 = (bf16[768,512]{1,0:T(8,128)(2,1)}, bf16[768,512]{1,0:T(8,128)(2,1)}, u32[]{:S(2)}, u32[]{:S(2)}) collective-permute-start(bf16[768,512]{1,0:T(8,128)(2,1)} %block.1), channel_id=1, source_target_pairs={{0,1},{1,0},{2,3},{3,2},{4,5},{5,4},{6,7},{7,6},{8,9},{9,8},{10,11... | collective-permute-start | bytes 2359304 | tf_op jit(solution)/shard_map/ppermute | solution.py:50
  10.4 14.1 %collective-permute-done.refs_0_ = bf16[784,512]{1,0:T(8,128)(2,1)S(1)} collective-permute-done((bf16[784,512]{1,0:T(8,128)(2,1)S(1)}, bf16[784,512]{1,0:T(8,128)(2,1)S(1)}, u32[]{:S(2)}, u32[]{:S(2)}) %collective-permute-start) | collective-permute-done | bytes 802848 | tf_op jit(solution)/shard_map/ppermute | solution.py:58
  26.1 1.9 %collective-permute-done.4.refs_0_.refs_4_ = bf16[768,512]{1,0:T(8,128)(2,1)} collective-permute-done((bf16[768,512]{1,0:T(8,128)(2,1)}, bf16[768,512]{1,0:T(8,128)(2,1)}, u32[]{:S(2)}, u32[]{:S(2)}) %collective-permute-start.4) | collective-permute-done | bytes 786464 | tf_op jit(solution)/shard_map/ppermute | solution.py:50
  28.0 4.1 %collective-permute-start.9 = (bf16[784,512]{1,0:T(8,128)(2,1)S(1)}, bf16[784,512]{1,0:T(8,128)(2,1)}, u32[]{:S(2)}, u32[]{:S(2)}) collective-permute-start(bf16[784,512]{1,0:T(8,128)(2,1)S(1)} %shard_map.66.refs_0_.refs_1_), channel_id=1, source_target_pairs={{0,8},{8,0},{16,24},{24,16},{1,9},{9,1},{17,25},{25,17},{2,10},{10... | collective-permute-start | bytes 2408456 | tf_op jit(solution)/shard_map/ppermute | solution.py:58
  32.1 1.5 %collective-permute-start.1 = (bf16[784,512]{1,0:T(8,128)(2,1)S(1)}, bf16[784,512]{1,0:T(8,128)(2,1)}, u32[]{:S(2)}, u32[]{:S(2)}) collective-permute-start(bf16[784,512]{1,0:T(8,128)(2,1)S(1)} %collective-permute-done.refs_0_), channel_id=1, source_target_pairs={{0,0},{8,16},{16,8},{24,24},{1,1},{9,17},{17,9},{25,25},{2,2},{10,... | collective-permute-start | bytes 2408456 | tf_op jit(solution)/shard_map/ppermute | solution.py:58
  34.3 1.5 %collective-permute-start.13 = (bf16[784,512]{1,0:T(8,128)(2,1)S(1)}, bf16[784,512]{1,0:T(8,128)(2,1)S(1)}, u32[]{:S(2)}, u32[]{:S(2)}) collective-permute-start(bf16[784,512]{1,0:T(8,128)(2,1)S(1)} %broadcast_select_fusion.2.refs_0_), channel_id=1, source_target_pairs={{0,1},{1,0},{2,3},{3,2},{4,5},{5,4},{6,7},{7,6},{8,9},{9,8},{10,11... | collective-permute-start | bytes 2408456 | tf_op jit(solution)/shard_map/ppermute | solution.py:50
  35.8 7.4 %shard_map.71.refs_0_.refs_5_ = f32[2,4,768,768]{3,2,1,0:T(8,128)S(1)} custom-call(f32[8,128]{1,0:T(8,128)S(1)} %shard_map.70.token.refs_9_, f32[1,512]{1,0:T(1,128)S(1)} %add_divide_fusion.3.weight, bf16[784,512]{1,0:T(8,128)(2,1)S(1)} %shard_map.64.refs_0_, bf16[768,512]{1,0:T(8,128)(2,1)} %collective-permute-done.7.refs_1_, ...), custom_call_target="tpu_custom_call" | custom-call | flops 57982058496 | tf_op jit(solution)/shard_map/pallas_call | solution.py:131
  43.3 5.1 %collective-permute-done.9 = bf16[784,512]{1,0:T(8,128)(2,1)} collective-permute-done((bf16[784,512]{1,0:T(8,128)(2,1)S(1)}, bf16[784,512]{1,0:T(8,128)(2,1)}, u32[]{:S(2)}, u32[]{:S(2)}) %collective-permute-start.9) | collective-permute-done | bytes 802848 | tf_op jit(solution)/shard_map/ppermute | solution.py:58
  50.1 2.7 %collective-permute-start.2 = (bf16[784,512]{1,0:T(8,128)(2,1)}, bf16[784,512]{1,0:T(8,128)(2,1)S(1)}, u32[]{:S(2)}, u32[]{:S(2)}) collective-permute-start(bf16[784,512]{1,0:T(8,128)(2,1)} %collective-permute-done.1.refs_0_), channel_id=1, source_target_pairs={{0,8},{8,0},{16,24},{24,16},{1,9},{9,1},{17,25},{25,17},{2,10},{10... | collective-permute-start | bytes 2408456 | tf_op jit(solution)/shard_map/ppermute | solution.py:58
  53.2 1.6 %collective-permute-start.19 = (bf16[784,512]{1,0:T(8,128)(2,1)S(1)}, bf16[784,512]{1,0:T(8,128)(2,1)S(1)}, u32[]{:S(2)}, u32[]{:S(2)}) collective-permute-start(bf16[784,512]{1,0:T(8,128)(2,1)S(1)} %broadcast_select_fusion.1.refs_0_), channel_id=1, source_target_pairs={{0,1},{1,0},{2,3},{3,2},{4,5},{5,4},{6,7},{7,6},{8,9},{9,8},{10,11... | collective-permute-start | bytes 2408456 | tf_op jit(solution)/shard_map/ppermute | solution.py:50
  55.4 5.7 %shard_map.75.refs_0_.refs_5_ = f32[2,4,768,768]{3,2,1,0:T(8,128)S(1)} custom-call(f32[8,128]{1,0:T(8,128)S(1)} %shard_map.73.token.refs_12_, f32[1,512]{1,0:T(1,128)S(1)} %add_divide_fusion.2.weight, bf16[784,512]{1,0:T(8,128)(2,1)S(1)} %broadcast_select_fusion.2.refs_0_, ...), custom_call_target="tpu_custom_call", output_to_operand_aliasing={{}: (7, {})} | custom-call | flops 4831838208 | tf_op jit(solution)/shard_map/pallas_call | solution.py:131
  61.1 7.5 %collective-permute-done.17.value = bf16[784,512]{1,0:T(8,128)(2,1)S(1)} collective-permute-done((bf16[784,512]{1,0:T(8,128)(2,1)S(1)}, bf16[784,512]{1,0:T(8,128)(2,1)S(1)}, u32[]{:S(2)}, u32[]{:S(2)}) %collective-permute-start.17) | collective-permute-done | bytes 802848 | tf_op jit(solution)/shard_map/ppermute | solution.py:54
  68.6 3.0 %collective-permute-done.2.refs_0_ = bf16[784,512]{1,0:T(8,128)(2,1)S(1)} collective-permute-done((bf16[784,512]{1,0:T(8,128)(2,1)}, bf16[784,512]{1,0:T(8,128)(2,1)S(1)}, u32[]{:S(2)}, u32[]{:S(2)}) %collective-permute-start.2) | collective-permute-done | bytes 802848 | tf_op jit(solution)/shard_map/ppermute | solution.py:58
  71.9 1.4 %collective-permute-start.20 = (bf16[384,512]{1,0:T(8,128)(2,1)S(1)}, bf16[384,512]{1,0:T(8,128)(2,1)S(1)}, u32[]{:S(2)}, u32[]{:S(2)}) collective-permute-start(bf16[384,512]{1,0:T(8,128)(2,1)S(1)} %get-tuple-element.35), channel_id=1, source_target_pairs={{0,4},{2,6},{4,0},{6,2},{1,5},{3,7},{5,1},{7,3},{8,12},{10,14},{12... | collective-permute-start | bytes 1179656 | tf_op jit(solution)/shard_map/ppermute | solution.py:54
  73.3 1.5 %collective-permute-start.15 = (bf16[384,512]{1,0:T(8,128)(2,1)S(1)}, bf16[384,512]{1,0:T(8,128)(2,1)S(1)}, u32[]{:S(2)}, u32[]{:S(2)}) collective-permute-start(bf16[384,512]{1,0:T(8,128)(2,1)S(1)} %get-tuple-element.35), channel_id=1, source_target_pairs={{0,1},{1,0},{2,3},{3,2},{4,5},{5,4},{6,7},{7,6},{8,9},{9,8},{10,11... | collective-permute-start | bytes 1179656 | tf_op jit(solution)/shard_map/ppermute | solution.py:50
  76.1 6.1 %shard_map.80.refs_4_.refs_0_ = f32[2,4,768,768]{3,2,1,0:T(8,128)S(1)} custom-call(f32[8,128]{1,0:T(8,128)S(1)} %shard_map.78.token.refs_15_, f32[1,512]{1,0:T(1,128)S(1)} %add_divide_fusion.weight, bf16[784,512]{1,0:T(8,128)(2,1)S(1)} %broadcast_select_fusion.1.refs_0_, ...), custom_call_target="tpu_custom_call", output_to_operand_aliasing={{}: (7, {})} | custom-call | flops 4831838208 | tf_op jit(solution)/shard_map/pallas_call | solution.py:131
  82.2 4.0 %shard_map.81 = (f32[2,4,768,768]{3,2,1,0:T(8,128)S(1)}, f32[4,768,1536]{2,1,0:T(8,128)}, bf16[2,768,512]{2,1,0:T(8,128)(2,1)S(1)}) custom-call(s32[5]{0:T(128)S(1)} %stack.30.refs_0_, f32[1,512]{1,0:T(1,128)S(1)} %add_divide_fusion.1.refs_1_, bf16[784,512]{1,0:T(8,128)(2,1)S(1)} %broadcast_select_fusion.refs_0_.refs_2_, ...), custom_call_target="tpu_custom_call", output_to_operand_aliasing={{0}: (4, {})} | custom-call | flops 1207959552 | bytes 4718592 | tf_op jit(solution)/shard_map/pallas_call | solution.py:203
  86.4 1.7 %collective-permute-done.21.refs_3_ = bf16[384,512]{1,0:T(8,128)(2,1)S(1)} collective-permute-done((bf16[384,512]{1,0:T(8,128)(2,1)S(1)}, bf16[384,512]{1,0:T(8,128)(2,1)S(1)}, u32[]{:S(2)}, u32[]{:S(2)}) %collective-permute-start.21) | collective-permute-done | bytes 393248 | tf_op jit(solution)/shard_map/ppermute | solution.py:67
  88.1 4.0 %shard_map.86 = (f32[2,4,768,768]{3,2,1,0:T(8,128)S(1)}, f32[4,768,1536]{2,1,0:T(8,128)}, bf16[2,768,512]{2,1,0:T(8,128)(2,1)S(1)}) custom-call(s32[5]{0:T(128)S(1)} %stack.30.refs_0_, f32[1,512]{1,0:T(1,128)S(1)} %add_divide_fusion.1.refs_1_, ...), custom_call_target="tpu_custom_call", output_to_operand_aliasing={{0}: (7, {}), {1}: (8, {}), {2}: (9, {})} | custom-call | flops 1509949440 | bytes 5898240 | tf_op jit(solution)/shard_map/pallas_call | solution.py:203
  93.0 3.9 %shard_map.91 = (f32[2,4,768,768]{3,2,1,0:T(8,128)S(1)}, f32[4,768,1536]{2,1,0:T(8,128)}, bf16[2,768,512]{2,1,0:T(8,128)(2,1)S(1)}) custom-call(s32[5]{0:T(128)S(1)} %stack.30.refs_0_, f32[1,512]{1,0:T(1,128)S(1)} %add_divide_fusion.1.refs_1_, ...), custom_call_target="tpu_custom_call", output_to_operand_aliasing={{0}: (8, {}), {1}: (9, {}), {2}: (10, {})} | custom-call | flops 1509949440 | bytes 5898240 | tf_op jit(solution)/shard_map/pallas_call | solution.py:203
  96.9 2.6 %shard_map.93 = (f32[2,4,768,768]{3,2,1,0:T(8,128)S(1)}, f32[4,768,1536]{2,1,0:T(8,128)}, bf16[2,768,512]{2,1,0:T(8,128)(2,1)S(1)}) custom-call(s32[5]{0:T(128)S(1)} %stack.30.refs_0_, f32[1,512]{1,0:T(1,128)S(1)} %add_divide_fusion.1.refs_1_, ...), custom_call_target="tpu_custom_call", output_to_operand_aliasing={{0}: (3, {}), {1}: (4, {}), {2}: (5, {})} | custom-call | flops 603979776 | bytes 2359296 | tf_op jit(solution)/shard_map/pallas_call | solution.py:203
  (76 shorter events, 9.8 us)
Async XLA Ops:
  3.5 21.0 %collective-permute-start = (bf16[784,512]{1,0:T(8,128)(2,1)S(1)}, bf16[784,512]{1,0:T(8,128)(2,1)S(1)}, u32[]{:S(2)}, u32[]{:S(2)}) collective-permute-start(bf16[784,512]{1,0:T(8,128)(2,1)S(1)} %shard_map.64.refs_0_), channel_id=1, source_target_pairs={{0,8},{8,0},{16,24},{24,16},{1,9},{9,1},{17,25},{25,17},{2,10},{10... | collective-permute-start | bytes 2408456 | tf_op jit(solution)/shard_map/ppermute | solution.py:58
  6.6 19.3 %collective-permute-start.5 = (bf16[768,512]{1,0:T(8,128)(2,1)}, bf16[768,512]{1,0:T(8,128)(2,1)}, u32[]{:S(2)}, u32[]{:S(2)}) collective-permute-start(bf16[768,512]{1,0:T(8,128)(2,1)} %block.1), channel_id=1, source_target_pairs={{0,4},{2,6},{4,0},{6,2},{1,5},{3,7},{5,1},{7,3},{8,12},{10,14},{12... | collective-permute-start | bytes 2359304 | tf_op jit(solution)/shard_map/ppermute | solution.py:54
  8.2 19.8 %collective-permute-start.3 = (bf16[784,512]{1,0:T(8,128)(2,1)S(1)}, bf16[784,512]{1,0:T(8,128)(2,1)S(1)}, u32[]{:S(2)}, u32[]{:S(2)}) collective-permute-start(bf16[784,512]{1,0:T(8,128)(2,1)S(1)} %shard_map.64.refs_0_), channel_id=1, source_target_pairs={{0,0},{8,16},{16,8},{24,24},{1,1},{9,17},{17,9},{25,25},{2,2},{10,... | collective-permute-start | bytes 2408456 | tf_op jit(solution)/shard_map/ppermute | solution.py:58
  8.9 19.1 %collective-permute-start.4 = (bf16[768,512]{1,0:T(8,128)(2,1)}, bf16[768,512]{1,0:T(8,128)(2,1)}, u32[]{:S(2)}, u32[]{:S(2)}) collective-permute-start(bf16[768,512]{1,0:T(8,128)(2,1)} %block.1), channel_id=1, source_target_pairs={{0,1},{1,0},{2,3},{3,2},{4,5},{5,4},{6,7},{7,6},{8,9},{9,8},{10,11... | collective-permute-start | bytes 2359304 | tf_op jit(solution)/shard_map/ppermute | solution.py:50
  24.5 9.1 %collective-permute-start.6 = (bf16[784,512]{1,0:T(8,128)(2,1)S(1)}, bf16[784,512]{1,0:T(8,128)(2,1)S(1)}, u32[]{:S(2)}, u32[]{:S(2)}) collective-permute-start(bf16[784,512]{1,0:T(8,128)(2,1)S(1)} %collective-permute-done.refs_0_), channel_id=1, source_target_pairs={{0,2},{2,0},{4,6},{6,4},{1,3},{3,1},{5,7},{7,5},{8,10},{10,8},{12,... | collective-permute-start | bytes 2408456 | tf_op jit(solution)/shard_map/ppermute | solution.py:67
  24.5 9.8 %collective-permute-start.7 = (bf16[768,512]{1,0:T(8,128)(2,1)}, bf16[768,512]{1,0:T(8,128)(2,1)}, u32[]{:S(2)}, u32[]{:S(2)}) collective-permute-start(bf16[768,512]{1,0:T(8,128)(2,1)} %block.1), channel_id=1, source_target_pairs={{0,2},{2,0},{4,6},{6,4},{1,3},{3,1},{5,7},{7,5},{8,10},{10,8},{12,... | collective-permute-start | bytes 2359304 | tf_op jit(solution)/shard_map/ppermute | solution.py:67
  26.0 9.9 %collective-permute-start.8 = (bf16[768,512]{1,0:T(8,128)(2,1)}, bf16[768,512]{1,0:T(8,128)(2,1)}, u32[]{:S(2)}, u32[]{:S(2)}) collective-permute-start(bf16[768,512]{1,0:T(8,128)(2,1)} %collective-permute-done.5.refs_1_.refs_2_), channel_id=1, source_target_pairs={{0,2},{2,0},{4,6},{6,4},{1,3},{3,1},{5,7},{7,5},{8,10},{10,8},{12,... | collective-permute-start | bytes 2359304 | tf_op jit(solution)/shard_map/ppermute | solution.py:67
  28.0 20.4 %collective-permute-start.9 = (bf16[784,512]{1,0:T(8,128)(2,1)S(1)}, bf16[784,512]{1,0:T(8,128)(2,1)}, u32[]{:S(2)}, u32[]{:S(2)}) collective-permute-start(bf16[784,512]{1,0:T(8,128)(2,1)S(1)} %shard_map.66.refs_0_.refs_1_), channel_id=1, source_target_pairs={{0,8},{8,0},{16,24},{24,16},{1,9},{9,1},{17,25},{25,17},{2,10},{10... | collective-permute-start | bytes 2408456 | tf_op jit(solution)/shard_map/ppermute | solution.py:58
  32.1 11.2 %collective-permute-start.1 = (bf16[784,512]{1,0:T(8,128)(2,1)S(1)}, bf16[784,512]{1,0:T(8,128)(2,1)}, u32[]{:S(2)}, u32[]{:S(2)}) collective-permute-start(bf16[784,512]{1,0:T(8,128)(2,1)S(1)} %collective-permute-done.refs_0_), channel_id=1, source_target_pairs={{0,0},{8,16},{16,8},{24,24},{1,1},{9,17},{17,9},{25,25},{2,2},{10,... | collective-permute-start | bytes 2408456 | tf_op jit(solution)/shard_map/ppermute | solution.py:58
  33.8 19.3 %collective-permute-start.11 = (bf16[784,512]{1,0:T(8,128)(2,1)S(1)}, bf16[784,512]{1,0:T(8,128)(2,1)S(1)}, u32[]{:S(2)}, u32[]{:S(2)}) collective-permute-start(bf16[784,512]{1,0:T(8,128)(2,1)S(1)} %broadcast_select_fusion.2.refs_0_), channel_id=1, source_target_pairs={{0,4},{2,6},{4,0},{6,2},{1,5},{3,7},{5,1},{7,3},{8,12},{10,14},{12... | collective-permute-start | bytes 2408456 | tf_op jit(solution)/shard_map/ppermute | solution.py:54
  34.3 18.8 %collective-permute-start.13 = (bf16[784,512]{1,0:T(8,128)(2,1)S(1)}, bf16[784,512]{1,0:T(8,128)(2,1)S(1)}, u32[]{:S(2)}, u32[]{:S(2)}) collective-permute-start(bf16[784,512]{1,0:T(8,128)(2,1)S(1)} %broadcast_select_fusion.2.refs_0_), channel_id=1, source_target_pairs={{0,1},{1,0},{2,3},{3,2},{4,5},{5,4},{6,7},{7,6},{8,9},{9,8},{10,11... | collective-permute-start | bytes 2408456 | tf_op jit(solution)/shard_map/ppermute | solution.py:50
  49.6 19.0 %collective-permute-start.17 = (bf16[784,512]{1,0:T(8,128)(2,1)S(1)}, bf16[784,512]{1,0:T(8,128)(2,1)S(1)}, u32[]{:S(2)}, u32[]{:S(2)}) collective-permute-start(bf16[784,512]{1,0:T(8,128)(2,1)S(1)} %broadcast_select_fusion.1.refs_0_), channel_id=1, source_target_pairs={{0,4},{2,6},{4,0},{6,2},{1,5},{3,7},{5,1},{7,3},{8,12},{10,14},{12... | collective-permute-start | bytes 2408456 | tf_op jit(solution)/shard_map/ppermute | solution.py:54
  50.1 18.5 %collective-permute-start.10 = (bf16[784,512]{1,0:T(8,128)(2,1)S(1)}, bf16[784,512]{1,0:T(8,128)(2,1)S(1)}, u32[]{:S(2)}, u32[]{:S(2)}) collective-permute-start(bf16[784,512]{1,0:T(8,128)(2,1)S(1)} %broadcast_select_fusion.1.refs_0_), channel_id=1, source_target_pairs={{0,2},{2,0},{4,6},{6,4},{1,3},{3,1},{5,7},{7,5},{8,10},{10,8},{12,... | collective-permute-start | bytes 2408456 | tf_op jit(solution)/shard_map/ppermute | solution.py:67
  50.1 21.5 %collective-permute-start.2 = (bf16[784,512]{1,0:T(8,128)(2,1)}, bf16[784,512]{1,0:T(8,128)(2,1)S(1)}, u32[]{:S(2)}, u32[]{:S(2)}) collective-permute-start(bf16[784,512]{1,0:T(8,128)(2,1)} %collective-permute-done.1.refs_0_), channel_id=1, source_target_pairs={{0,8},{8,0},{16,24},{24,16},{1,9},{9,1},{17,25},{25,17},{2,10},{10... | collective-permute-start | bytes 2408456 | tf_op jit(solution)/shard_map/ppermute | solution.py:58
  53.1 2.3 %collective-permute-start.12 = (bf16[784,512]{1,0:T(8,128)(2,1)S(1)}, bf16[784,512]{1,0:T(8,128)(2,1)S(1)}, u32[]{:S(2)}, u32[]{:S(2)}) collective-permute-start(bf16[784,512]{1,0:T(8,128)(2,1)S(1)} %shard_map.74.refs_2_), channel_id=1, source_target_pairs={{0,2},{2,0},{4,6},{6,4},{1,3},{3,1},{5,7},{7,5},{8,10},{10,8},{12,... | collective-permute-start | bytes 2408456 | tf_op jit(solution)/shard_map/ppermute | solution.py:67
  53.2 21.6 %collective-permute-start.19 = (bf16[784,512]{1,0:T(8,128)(2,1)S(1)}, bf16[784,512]{1,0:T(8,128)(2,1)S(1)}, u32[]{:S(2)}, u32[]{:S(2)}) collective-permute-start(bf16[784,512]{1,0:T(8,128)(2,1)S(1)} %broadcast_select_fusion.1.refs_0_), channel_id=1, source_target_pairs={{0,1},{1,0},{2,3},{3,2},{4,5},{5,4},{6,7},{7,6},{8,9},{9,8},{10,11... | collective-permute-start | bytes 2408456 | tf_op jit(solution)/shard_map/ppermute | solution.py:50
  68.6 6.8 %collective-permute-start.18 = (bf16[784,512]{1,0:T(8,128)(2,1)S(1)}, bf16[784,512]{1,0:T(8,128)(2,1)S(1)}, u32[]{:S(2)}, u32[]{:S(2)}) collective-permute-start(bf16[784,512]{1,0:T(8,128)(2,1)S(1)} %shard_map.79.refs_2_), channel_id=1, source_target_pairs={{0,2},{2,0},{4,6},{6,4},{1,3},{3,1},{5,7},{7,5},{8,10},{10,8},{12,... | collective-permute-start | bytes 2408456 | tf_op jit(solution)/shard_map/ppermute | solution.py:67
  71.7 10.5 %collective-permute-start.16 = (bf16[784,512]{1,0:T(8,128)(2,1)S(1)}, bf16[784,512]{1,0:T(8,128)(2,1)S(1)}, u32[]{:S(2)}, u32[]{:S(2)}) collective-permute-start(bf16[784,512]{1,0:T(8,128)(2,1)S(1)} %broadcast_select_fusion.refs_0_.refs_2_), channel_id=1, source_target_pairs={{0,2},{2,0},{4,6},{6,4},{1,3},{3,1},{5,7},{7,5},{8,10},{10,8},{12,... | collective-permute-start | bytes 2408456 | tf_op jit(solution)/shard_map/ppermute | solution.py:67
  71.9 14.4 %collective-permute-start.20 = (bf16[384,512]{1,0:T(8,128)(2,1)S(1)}, bf16[384,512]{1,0:T(8,128)(2,1)S(1)}, u32[]{:S(2)}, u32[]{:S(2)}) collective-permute-start(bf16[384,512]{1,0:T(8,128)(2,1)S(1)} %get-tuple-element.35), channel_id=1, source_target_pairs={{0,4},{2,6},{4,0},{6,2},{1,5},{3,7},{5,1},{7,3},{8,12},{10,14},{12... | collective-permute-start | bytes 1179656 | tf_op jit(solution)/shard_map/ppermute | solution.py:54
  73.3 13.1 %collective-permute-start.15 = (bf16[384,512]{1,0:T(8,128)(2,1)S(1)}, bf16[384,512]{1,0:T(8,128)(2,1)S(1)}, u32[]{:S(2)}, u32[]{:S(2)}) collective-permute-start(bf16[384,512]{1,0:T(8,128)(2,1)S(1)} %get-tuple-element.35), channel_id=1, source_target_pairs={{0,1},{1,0},{2,3},{3,2},{4,5},{5,4},{6,7},{7,6},{8,9},{9,8},{10,11... | collective-permute-start | bytes 1179656 | tf_op jit(solution)/shard_map/ppermute | solution.py:50
  74.8 18.1 %collective-permute-start.23 = (bf16[384,512]{1,0:T(8,128)(2,1)S(1)}, bf16[384,512]{1,0:T(8,128)(2,1)S(1)}, u32[]{:S(2)}, u32[]{:S(2)}) collective-permute-start(bf16[384,512]{1,0:T(8,128)(2,1)S(1)} %get-tuple-element.36), channel_id=1, source_target_pairs={{0,1},{1,0},{2,3},{3,2},{4,5},{5,4},{6,7},{7,6},{8,9},{9,8},{10,11... | collective-permute-start | bytes 1179656 | tf_op jit(solution)/shard_map/ppermute | solution.py:50
  75.4 16.6 %collective-permute-start.14 = (bf16[384,512]{1,0:T(8,128)(2,1)S(1)}, bf16[384,512]{1,0:T(8,128)(2,1)S(1)}, u32[]{:S(2)}, u32[]{:S(2)}) collective-permute-start(bf16[384,512]{1,0:T(8,128)(2,1)S(1)} %get-tuple-element.36), channel_id=1, source_target_pairs={{0,4},{2,6},{4,0},{6,2},{1,5},{3,7},{5,1},{7,3},{8,12},{10,14},{12... | collective-permute-start | bytes 1179656 | tf_op jit(solution)/shard_map/ppermute | solution.py:54
  86.3 1.8 %collective-permute-start.21 = (bf16[384,512]{1,0:T(8,128)(2,1)S(1)}, bf16[384,512]{1,0:T(8,128)(2,1)S(1)}, u32[]{:S(2)}, u32[]{:S(2)}) collective-permute-start(bf16[384,512]{1,0:T(8,128)(2,1)S(1)} %shard_map.84.refs_1_.refs_5_), channel_id=1, source_target_pairs={{0,2},{2,0},{4,6},{6,4},{1,3},{3,1},{5,7},{7,5},{8,10},{10,8},{12,... | collective-permute-start | bytes 1179656 | tf_op jit(solution)/shard_map/ppermute | solution.py:67
  92.1 4.8 %collective-permute-start.22 = (bf16[384,512]{1,0:T(8,128)(2,1)S(1)}, bf16[384,512]{1,0:T(8,128)(2,1)S(1)}, u32[]{:S(2)}, u32[]{:S(2)}) collective-permute-start(bf16[384,512]{1,0:T(8,128)(2,1)S(1)} %shard_map.88.refs_1_.refs_6_), channel_id=1, source_target_pairs={{0,2},{2,0},{4,6},{6,4},{1,3},{3,1},{5,7},{7,5},{8,10},{10,8},{12,... | collective-permute-start | bytes 1179656 | tf_op jit(solution)/shard_map/ppermute | solution.py:67
  (2 other events, 9.6 us)

commit v6 on v5

--- a/solution.py
+++ b/solution.py
@@ -77,8 +77,8 @@
 
 
 def look_up(table, index):
-    hit = index[:, None] == lax.broadcasted_iota(jnp.int32, (1, table.shape[0]), 1)
-    return jnp.sum(jnp.where(hit, table[None, :], 0.0), axis=1)
+    hit = index[None, :] == lax.broadcasted_iota(jnp.int32, (table.shape[0], 1), 0)
+    return jnp.sum(jnp.where(hit, table[:, None], 0.0), axis=0)
 
 
 def split_rows(value):
@@ -338,7 +338,7 @@
 
     got = lag((last, swap_2, added), LAGS[1], tokens)
     mine_3 = jnp.where(after(end, got), last, far_2)
-    cut = sub // 2
+    cut = sub * 2 // 3
     parts = [(mine_3[:cut], 0, cut), (mine_3[cut:sub], cut, sub - cut)]
     x[3] = [across_col(part) for part, _, _ in parts]
     y[3] = [across_row(part) for part, _, _ in parts]
@@ -371,12 +371,10 @@
         else:
             jobs = (("own", "x1"), ("swap", "x1"), ("y1", "own"), ("y1", "x0"))
             jobs += (("y1", "x1"), ("y0", "x1"), ("s0", "x1"))
-            acc, out, weighted = finish(
-                here, weight, rights, lefts, ("x1",), jobs, state
+            jobs += (("s1", "own"), ("s1", "x0"), ("s1", "x1"))
+            _, out, _ = finish(
+                here, weight, rights, lefts, ("x1",), jobs, state, tokens
             )
-            jobs = (("s1", "own"), ("s1", "x0"), ("s1", "x1"))
-            state = acc, weighted, out
-            _, out, _ = finish(place, weight, rights, lefts, (), jobs, state, tokens)
     return out.reshape(1, 4, 1, sub, 2 * sub)
 
 

time: 100 us -> 99.3 us (level)
  Pallas kernels: 35 us -> 33 us
  waiting for transfers between devices: 35.1 us -> 36.4 us
    pallas_call x4 -> x3, Pallas kernels: 14.5 us -> 12.5 us  [finish(): pl.pallas_call(functools.partial(finish_kernel, *where, fresh, jobs, n_in...]
  transfers between devices with their start and end apart: 24 -> 24, of which waited for: 10 -> 12; matrix products, arithmetic and copies ran while one was open for 2% -> 2% of each run, Pallas kernels for 31% -> 28%
where the time goes in v6:
time: 99.3 us; the launch traced here: 98.7 us
  waiting for transfers between devices  36.4 us (37%)
  Pallas kernels  33 us (33%)
  starting transfers between devices  24.4 us (25%)
  other arithmetic  3.57 us (4%)
  between operations  1.13 us (1%)
    ppermute x5, waiting for transfers between devices, along_line(): return lambda value: lax.ppermute(value, 'freq', hops)  22.2 us
    pallas_call x3, Pallas kernels, add_slot(): pl.pallas_call(functools.partial(slot_kernel, acc is None), out_shape=plt...  19.2 us
    pallas_call x3, Pallas kernels, finish(): pl.pallas_call(functools.partial(finish_kernel, *where, fresh, jobs, n_in...  12.5 us
    ppermute x5, starting transfers between devices, along_line(): return lambda value: lax.ppermute(value, 'freq', hops)  12.1 us
    ppermute x5, waiting for transfers between devices, across_row(): return lax.ppermute(value, 'row', [(i, (i + 2) % 4) for i in range(4)])  8.36 us
    ppermute x5, starting transfers between devices, across_col(): return lax.ppermute(value, 'col', [(0, 1), (1, 0)])  6.64 us
    ppermute x5, starting transfers between devices, across_row(): return lax.ppermute(value, 'row', [(i, (i + 2) % 4) for i in range(4)])  4.82 us
    ppermute x5, waiting for transfers between devices, across_col(): return lax.ppermute(value, 'col', [(0, 1), (1, 0)])  3.28 us
  transfers between devices with their start and end apart: 24, of which 12 were waited for; matrix products, arithmetic and copies ran while one was open for 2% of the time, Pallas kernels for 28%

profile of v6, /device:TPU:0, one launch (start us, length us, event | category | flops | bytes accessed | tf_op | source)
XLA Modules:
  0.0 98.7 jit_solution(12287567696374464413)
XLA Ops:
  2.1 1.3 %shard_map.64.refs_0_ = bf16[784,512]{1,0:T(8,128)(2,1)S(1)} custom-call(bf16[768,512]{1,0:T(8,128)(2,1)} %block.1, bf16[16,512]{1,0:T(8,128)(2,1)S(1)} %fusion.4.rows), custom_call_target="tpu_custom_call" | custom-call | tf_op jit(solution)/shard_map/pallas_call | solution.py:237
  3.4 3.1 %collective-permute-start = (bf16[784,512]{1,0:T(8,128)(2,1)S(1)}, bf16[784,512]{1,0:T(8,128)(2,1)S(1)}, u32[]{:S(2)}, u32[]{:S(2)}) collective-permute-start(bf16[784,512]{1,0:T(8,128)(2,1)S(1)} %shard_map.64.refs_0_), channel_id=1, source_target_pairs={{0,8},{8,0},{16,24},{24,16},{1,9},{9,1},{17,25},{25,17},{2,10},{10... | collective-permute-start | bytes 2408456 | tf_op jit(solution)/shard_map/ppermute | solution.py:58
  6.4 1.5 %collective-permute-start.5 = (bf16[768,512]{1,0:T(8,128)(2,1)}, bf16[768,512]{1,0:T(8,128)(2,1)}, u32[]{:S(2)}, u32[]{:S(2)}) collective-permute-start(bf16[768,512]{1,0:T(8,128)(2,1)} %block.1), channel_id=1, source_target_pairs={{0,4},{2,6},{4,0},{6,2},{1,5},{3,7},{5,1},{7,3},{8,12},{10,14},{12... | collective-permute-start | bytes 2359304 | tf_op jit(solution)/shard_map/ppermute | solution.py:54
  8.7 1.6 %collective-permute-start.4 = (bf16[768,512]{1,0:T(8,128)(2,1)}, bf16[768,512]{1,0:T(8,128)(2,1)}, u32[]{:S(2)}, u32[]{:S(2)}) collective-permute-start(bf16[768,512]{1,0:T(8,128)(2,1)} %block.1), channel_id=1, source_target_pairs={{0,1},{1,0},{2,3},{3,2},{4,5},{5,4},{6,7},{7,6},{8,9},{9,8},{10,11... | collective-permute-start | bytes 2359304 | tf_op jit(solution)/shard_map/ppermute | solution.py:50
  10.2 14.1 %collective-permute-done.refs_0_ = bf16[784,512]{1,0:T(8,128)(2,1)S(1)} collective-permute-done((bf16[784,512]{1,0:T(8,128)(2,1)S(1)}, bf16[784,512]{1,0:T(8,128)(2,1)S(1)}, u32[]{:S(2)}, u32[]{:S(2)}) %collective-permute-start) | collective-permute-done | bytes 802848 | tf_op jit(solution)/shard_map/ppermute | solution.py:58
  25.9 1.9 %collective-permute-done.4.refs_0_.refs_4_ = bf16[768,512]{1,0:T(8,128)(2,1)} collective-permute-done((bf16[768,512]{1,0:T(8,128)(2,1)}, bf16[768,512]{1,0:T(8,128)(2,1)}, u32[]{:S(2)}, u32[]{:S(2)}) %collective-permute-start.4) | collective-permute-done | bytes 786464 | tf_op jit(solution)/shard_map/ppermute | solution.py:50
  27.8 4.1 %collective-permute-start.9 = (bf16[784,512]{1,0:T(8,128)(2,1)S(1)}, bf16[784,512]{1,0:T(8,128)(2,1)}, u32[]{:S(2)}, u32[]{:S(2)}) collective-permute-start(bf16[784,512]{1,0:T(8,128)(2,1)S(1)} %shard_map.66.refs_0_.refs_1_), channel_id=1, source_target_pairs={{0,8},{8,0},{16,24},{24,16},{1,9},{9,1},{17,25},{25,17},{2,10},{10... | collective-permute-start | bytes 2408456 | tf_op jit(solution)/shard_map/ppermute | solution.py:58
  31.9 1.5 %collective-permute-start.1 = (bf16[784,512]{1,0:T(8,128)(2,1)S(1)}, bf16[784,512]{1,0:T(8,128)(2,1)}, u32[]{:S(2)}, u32[]{:S(2)}) collective-permute-start(bf16[784,512]{1,0:T(8,128)(2,1)S(1)} %collective-permute-done.refs_0_), channel_id=1, source_target_pairs={{0,0},{8,16},{16,8},{24,24},{1,1},{9,17},{17,9},{25,25},{2,2},{10,... | collective-permute-start | bytes 2408456 | tf_op jit(solution)/shard_map/ppermute | solution.py:58
  34.1 1.5 %collective-permute-start.13 = (bf16[784,512]{1,0:T(8,128)(2,1)S(1)}, bf16[784,512]{1,0:T(8,128)(2,1)S(1)}, u32[]{:S(2)}, u32[]{:S(2)}) collective-permute-start(bf16[784,512]{1,0:T(8,128)(2,1)S(1)} %broadcast_select_fusion.2.refs_0_), channel_id=1, source_target_pairs={{0,1},{1,0},{2,3},{3,2},{4,5},{5,4},{6,7},{7,6},{8,9},{9,8},{10,11... | collective-permute-start | bytes 2408456 | tf_op jit(solution)/shard_map/ppermute | solution.py:50
  35.6 7.4 %shard_map.71.refs_0_.refs_5_ = f32[2,4,768,768]{3,2,1,0:T(8,128)S(1)} custom-call(f32[8,128]{1,0:T(8,128)S(1)} %shard_map.70.token.refs_15_, f32[1,512]{1,0:T(1,128)S(1)} %add_divide_fusion.3.weight, bf16[784,512]{1,0:T(8,128)(2,1)S(1)} %shard_map.64.refs_0_, bf16[768,512]{1,0:T(8,128)(2,1)} %collective-permute-done.7.refs_1_, ...), custom_call_target="tpu_custom_call" | custom-call | flops 57982058496 | tf_op jit(solution)/shard_map/pallas_call | solution.py:131
  43.1 5.1 %collective-permute-done.9 = bf16[784,512]{1,0:T(8,128)(2,1)} collective-permute-done((bf16[784,512]{1,0:T(8,128)(2,1)S(1)}, bf16[784,512]{1,0:T(8,128)(2,1)}, u32[]{:S(2)}, u32[]{:S(2)}) %collective-permute-start.9) | collective-permute-done | bytes 802848 | tf_op jit(solution)/shard_map/ppermute | solution.py:58
  50.0 2.7 %collective-permute-start.2 = (bf16[784,512]{1,0:T(8,128)(2,1)}, bf16[784,512]{1,0:T(8,128)(2,1)S(1)}, u32[]{:S(2)}, u32[]{:S(2)}) collective-permute-start(bf16[784,512]{1,0:T(8,128)(2,1)} %collective-permute-done.1.refs_0_), channel_id=1, source_target_pairs={{0,8},{8,0},{16,24},{24,16},{1,9},{9,1},{17,25},{25,17},{2,10},{10... | collective-permute-start | bytes 2408456 | tf_op jit(solution)/shard_map/ppermute | solution.py:58
  53.0 1.6 %collective-permute-start.19 = (bf16[784,512]{1,0:T(8,128)(2,1)S(1)}, bf16[784,512]{1,0:T(8,128)(2,1)S(1)}, u32[]{:S(2)}, u32[]{:S(2)}) collective-permute-start(bf16[784,512]{1,0:T(8,128)(2,1)S(1)} %broadcast_select_fusion.1.refs_0_), channel_id=1, source_target_pairs={{0,1},{1,0},{2,3},{3,2},{4,5},{5,4},{6,7},{7,6},{8,9},{9,8},{10,11... | collective-permute-start | bytes 2408456 | tf_op jit(solution)/shard_map/ppermute | solution.py:50
  55.2 5.8 %shard_map.75.refs_0_.refs_5_ = f32[2,4,768,768]{3,2,1,0:T(8,128)S(1)} custom-call(f32[8,128]{1,0:T(8,128)S(1)} %shard_map.73.token.refs_18_, f32[1,512]{1,0:T(1,128)S(1)} %add_divide_fusion.2.weight, bf16[784,512]{1,0:T(8,128)(2,1)S(1)} %broadcast_select_fusion.2.refs_0_, ...), custom_call_target="tpu_custom_call", output_to_operand_aliasing={{}: (7, {})} | custom-call | flops 4831838208 | tf_op jit(solution)/shard_map/pallas_call | solution.py:131
  61.1 7.4 %collective-permute-done.17.value = bf16[784,512]{1,0:T(8,128)(2,1)S(1)} collective-permute-done((bf16[784,512]{1,0:T(8,128)(2,1)S(1)}, bf16[784,512]{1,0:T(8,128)(2,1)S(1)}, u32[]{:S(2)}, u32[]{:S(2)}) %collective-permute-start.17) | collective-permute-done | bytes 802848 | tf_op jit(solution)/shard_map/ppermute | solution.py:54
  68.4 3.0 %collective-permute-done.2.refs_0_ = bf16[784,512]{1,0:T(8,128)(2,1)S(1)} collective-permute-done((bf16[784,512]{1,0:T(8,128)(2,1)}, bf16[784,512]{1,0:T(8,128)(2,1)S(1)}, u32[]{:S(2)}, u32[]{:S(2)}) %collective-permute-start.2) | collective-permute-done | bytes 802848 | tf_op jit(solution)/shard_map/ppermute | solution.py:58
  71.7 1.4 %collective-permute-start.20 = (bf16[512,512]{1,0:T(8,128)(2,1)S(1)}, bf16[512,512]{1,0:T(8,128)(2,1)S(1)}, u32[]{:S(2)}, u32[]{:S(2)}) collective-permute-start(bf16[512,512]{1,0:T(8,128)(2,1)S(1)} %slice.89), channel_id=1, source_target_pairs={{0,4},{2,6},{4,0},{6,2},{1,5},{3,7},{5,1},{7,3},{8,12},{10,14},{12... | collective-permute-start | bytes 1572872 | tf_op jit(solution)/shard_map/ppermute | solution.py:54
  73.1 1.5 %collective-permute-start.15 = (bf16[512,512]{1,0:T(8,128)(2,1)S(1)}, bf16[512,512]{1,0:T(8,128)(2,1)S(1)}, u32[]{:S(2)}, u32[]{:S(2)}) collective-permute-start(bf16[512,512]{1,0:T(8,128)(2,1)S(1)} %slice.89), channel_id=1, source_target_pairs={{0,1},{1,0},{2,3},{3,2},{4,5},{5,4},{6,7},{7,6},{8,9},{9,8},{10,11... | collective-permute-start | bytes 1572872 | tf_op jit(solution)/shard_map/ppermute | solution.py:50
  75.9 5.9 %shard_map.80.refs_4_.refs_0_ = f32[2,4,768,768]{3,2,1,0:T(8,128)S(1)} custom-call(f32[8,128]{1,0:T(8,128)S(1)} %shard_map.78.token.refs_21_, f32[1,512]{1,0:T(1,128)S(1)} %add_divide_fusion.weight, bf16[784,512]{1,0:T(8,128)(2,1)S(1)} %broadcast_select_fusion.1.refs_0_, ...), custom_call_target="tpu_custom_call", output_to_operand_aliasing={{}: (7, {})} | custom-call | flops 4831838208 | tf_op jit(solution)/shard_map/pallas_call | solution.py:131
  81.9 4.0 %shard_map.81 = (f32[2,4,768,768]{3,2,1,0:T(8,128)S(1)}, f32[4,768,1536]{2,1,0:T(8,128)}, bf16[2,768,512]{2,1,0:T(8,128)(2,1)S(1)}) custom-call(s32[5]{0:T(128)S(1)} %stack.30.refs_0_, f32[1,512]{1,0:T(1,128)S(1)} %add_divide_fusion.1.refs_1_, bf16[784,512]{1,0:T(8,128)(2,1)S(1)} %broadcast_select_fusion.refs_0_.refs_2_, ...), custom_call_target="tpu_custom_call", output_to_operand_aliasing={{0}: (4, {})} | custom-call | flops 1207959552 | bytes 4718592 | tf_op jit(solution)/shard_map/pallas_call | solution.py:203
  86.5 1.4 %collective-permute-done.15.value = bf16[512,512]{1,0:T(8,128)(2,1)S(1)} collective-permute-done((bf16[512,512]{1,0:T(8,128)(2,1)S(1)}, bf16[512,512]{1,0:T(8,128)(2,1)S(1)}, u32[]{:S(2)}, u32[]{:S(2)}) %collective-permute-start.15) | collective-permute-done | bytes 524320 | tf_op jit(solution)/shard_map/ppermute | solution.py:50
  88.4 4.6 %shard_map.86 = (f32[2,4,768,768]{3,2,1,0:T(8,128)S(1)}, f32[4,768,1536]{2,1,0:T(8,128)}, bf16[2,768,512]{2,1,0:T(8,128)(2,1)S(1)}) custom-call(s32[5]{0:T(128)S(1)} %stack.30.refs_0_, f32[1,512]{1,0:T(1,128)S(1)} %add_divide_fusion.1.refs_1_, ...), custom_call_target="tpu_custom_call", output_to_operand_aliasing={{0}: (7, {}), {1}: (8, {}), {2}: (9, {})} | custom-call | flops 2147483648 | bytes 8388608 | tf_op jit(solution)/shard_map/pallas_call | solution.py:203
  93.3 1.4 %collective-permute-done.23.refs_4_ = bf16[256,512]{1,0:T(8,128)(2,1)S(1)} collective-permute-done((bf16[256,512]{1,0:T(8,128)(2,1)S(1)}, bf16[256,512]{1,0:T(8,128)(2,1)S(1)}, u32[]{:S(2)}, u32[]{:S(2)}) %collective-permute-start.23) | collective-permute-done | bytes 262176 | tf_op jit(solution)/shard_map/ppermute | solution.py:67
  94.7 3.9 %shard_map.92 = (f32[2,4,768,768]{3,2,1,0:T(8,128)S(1)}, f32[4,768,1536]{2,1,0:T(8,128)}, bf16[2,768,512]{2,1,0:T(8,128)(2,1)S(1)}) custom-call(s32[5]{0:T(128)S(1)} %stack.30.refs_0_, f32[1,512]{1,0:T(1,128)S(1)} %add_divide_fusion.1.refs_1_, ...), custom_call_target="tpu_custom_call", output_to_operand_aliasing={{0}: (9, {}), {1}: (10, {}), {2}: (11, {})} | custom-call | flops 1476395008 | bytes 5767168 | tf_op jit(solution)/shard_map/pallas_call | solution.py:203
  (76 shorter events, 9.9 us)
Async XLA Ops:
  3.4 21.0 %collective-permute-start = (bf16[784,512]{1,0:T(8,128)(2,1)S(1)}, bf16[784,512]{1,0:T(8,128)(2,1)S(1)}, u32[]{:S(2)}, u32[]{:S(2)}) collective-permute-start(bf16[784,512]{1,0:T(8,128)(2,1)S(1)} %shard_map.64.refs_0_), channel_id=1, source_target_pairs={{0,8},{8,0},{16,24},{24,16},{1,9},{9,1},{17,25},{25,17},{2,10},{10... | collective-permute-start | bytes 2408456 | tf_op jit(solution)/shard_map/ppermute | solution.py:58
  6.4 19.3 %collective-permute-start.5 = (bf16[768,512]{1,0:T(8,128)(2,1)}, bf16[768,512]{1,0:T(8,128)(2,1)}, u32[]{:S(2)}, u32[]{:S(2)}) collective-permute-start(bf16[768,512]{1,0:T(8,128)(2,1)} %block.1), channel_id=1, source_target_pairs={{0,4},{2,6},{4,0},{6,2},{1,5},{3,7},{5,1},{7,3},{8,12},{10,14},{12... | collective-permute-start | bytes 2359304 | tf_op jit(solution)/shard_map/ppermute | solution.py:54
  8.0 19.8 %collective-permute-start.3 = (bf16[784,512]{1,0:T(8,128)(2,1)S(1)}, bf16[784,512]{1,0:T(8,128)(2,1)S(1)}, u32[]{:S(2)}, u32[]{:S(2)}) collective-permute-start(bf16[784,512]{1,0:T(8,128)(2,1)S(1)} %shard_map.64.refs_0_), channel_id=1, source_target_pairs={{0,0},{8,16},{16,8},{24,24},{1,1},{9,17},{17,9},{25,25},{2,2},{10,... | collective-permute-start | bytes 2408456 | tf_op jit(solution)/shard_map/ppermute | solution.py:58
  8.7 19.1 %collective-permute-start.4 = (bf16[768,512]{1,0:T(8,128)(2,1)}, bf16[768,512]{1,0:T(8,128)(2,1)}, u32[]{:S(2)}, u32[]{:S(2)}) collective-permute-start(bf16[768,512]{1,0:T(8,128)(2,1)} %block.1), channel_id=1, source_target_pairs={{0,1},{1,0},{2,3},{3,2},{4,5},{5,4},{6,7},{7,6},{8,9},{9,8},{10,11... | collective-permute-start | bytes 2359304 | tf_op jit(solution)/shard_map/ppermute | solution.py:50
  24.3 9.1 %collective-permute-start.6 = (bf16[784,512]{1,0:T(8,128)(2,1)S(1)}, bf16[784,512]{1,0:T(8,128)(2,1)S(1)}, u32[]{:S(2)}, u32[]{:S(2)}) collective-permute-start(bf16[784,512]{1,0:T(8,128)(2,1)S(1)} %collective-permute-done.refs_0_), channel_id=1, source_target_pairs={{0,2},{2,0},{4,6},{6,4},{1,3},{3,1},{5,7},{7,5},{8,10},{10,8},{12,... | collective-permute-start | bytes 2408456 | tf_op jit(solution)/shard_map/ppermute | solution.py:67
  24.3 9.8 %collective-permute-start.7 = (bf16[768,512]{1,0:T(8,128)(2,1)}, bf16[768,512]{1,0:T(8,128)(2,1)}, u32[]{:S(2)}, u32[]{:S(2)}) collective-permute-start(bf16[768,512]{1,0:T(8,128)(2,1)} %block.1), channel_id=1, source_target_pairs={{0,2},{2,0},{4,6},{6,4},{1,3},{3,1},{5,7},{7,5},{8,10},{10,8},{12,... | collective-permute-start | bytes 2359304 | tf_op jit(solution)/shard_map/ppermute | solution.py:67
  25.8 9.9 %collective-permute-start.8 = (bf16[768,512]{1,0:T(8,128)(2,1)}, bf16[768,512]{1,0:T(8,128)(2,1)}, u32[]{:S(2)}, u32[]{:S(2)}) collective-permute-start(bf16[768,512]{1,0:T(8,128)(2,1)} %collective-permute-done.5.refs_1_.refs_2_), channel_id=1, source_target_pairs={{0,2},{2,0},{4,6},{6,4},{1,3},{3,1},{5,7},{7,5},{8,10},{10,8},{12,... | collective-permute-start | bytes 2359304 | tf_op jit(solution)/shard_map/ppermute | solution.py:67
  27.8 20.4 %collective-permute-start.9 = (bf16[784,512]{1,0:T(8,128)(2,1)S(1)}, bf16[784,512]{1,0:T(8,128)(2,1)}, u32[]{:S(2)}, u32[]{:S(2)}) collective-permute-start(bf16[784,512]{1,0:T(8,128)(2,1)S(1)} %shard_map.66.refs_0_.refs_1_), channel_id=1, source_target_pairs={{0,8},{8,0},{16,24},{24,16},{1,9},{9,1},{17,25},{25,17},{2,10},{10... | collective-permute-start | bytes 2408456 | tf_op jit(solution)/shard_map/ppermute | solution.py:58
  31.9 11.1 %collective-permute-start.1 = (bf16[784,512]{1,0:T(8,128)(2,1)S(1)}, bf16[784,512]{1,0:T(8,128)(2,1)}, u32[]{:S(2)}, u32[]{:S(2)}) collective-permute-start(bf16[784,512]{1,0:T(8,128)(2,1)S(1)} %collective-permute-done.refs_0_), channel_id=1, source_target_pairs={{0,0},{8,16},{16,8},{24,24},{1,1},{9,17},{17,9},{25,25},{2,2},{10,... | collective-permute-start | bytes 2408456 | tf_op jit(solution)/shard_map/ppermute | solution.py:58
  33.6 19.3 %collective-permute-start.11 = (bf16[784,512]{1,0:T(8,128)(2,1)S(1)}, bf16[784,512]{1,0:T(8,128)(2,1)S(1)}, u32[]{:S(2)}, u32[]{:S(2)}) collective-permute-start(bf16[784,512]{1,0:T(8,128)(2,1)S(1)} %broadcast_select_fusion.2.refs_0_), channel_id=1, source_target_pairs={{0,4},{2,6},{4,0},{6,2},{1,5},{3,7},{5,1},{7,3},{8,12},{10,14},{12... | collective-permute-start | bytes 2408456 | tf_op jit(solution)/shard_map/ppermute | solution.py:54
  34.1 18.8 %collective-permute-start.13 = (bf16[784,512]{1,0:T(8,128)(2,1)S(1)}, bf16[784,512]{1,0:T(8,128)(2,1)S(1)}, u32[]{:S(2)}, u32[]{:S(2)}) collective-permute-start(bf16[784,512]{1,0:T(8,128)(2,1)S(1)} %broadcast_select_fusion.2.refs_0_), channel_id=1, source_target_pairs={{0,1},{1,0},{2,3},{3,2},{4,5},{5,4},{6,7},{7,6},{8,9},{9,8},{10,11... | collective-permute-start | bytes 2408456 | tf_op jit(solution)/shard_map/ppermute | solution.py:50
  49.4 19.0 %collective-permute-start.17 = (bf16[784,512]{1,0:T(8,128)(2,1)S(1)}, bf16[784,512]{1,0:T(8,128)(2,1)S(1)}, u32[]{:S(2)}, u32[]{:S(2)}) collective-permute-start(bf16[784,512]{1,0:T(8,128)(2,1)S(1)} %broadcast_select_fusion.1.refs_0_), channel_id=1, source_target_pairs={{0,4},{2,6},{4,0},{6,2},{1,5},{3,7},{5,1},{7,3},{8,12},{10,14},{12... | collective-permute-start | bytes 2408456 | tf_op jit(solution)/shard_map/ppermute | solution.py:54
  50.0 18.5 %collective-permute-start.10 = (bf16[784,512]{1,0:T(8,128)(2,1)S(1)}, bf16[784,512]{1,0:T(8,128)(2,1)S(1)}, u32[]{:S(2)}, u32[]{:S(2)}) collective-permute-start(bf16[784,512]{1,0:T(8,128)(2,1)S(1)} %broadcast_select_fusion.1.refs_0_), channel_id=1, source_target_pairs={{0,2},{2,0},{4,6},{6,4},{1,3},{3,1},{5,7},{7,5},{8,10},{10,8},{12,... | collective-permute-start | bytes 2408456 | tf_op jit(solution)/shard_map/ppermute | solution.py:67
  50.0 21.5 %collective-permute-start.2 = (bf16[784,512]{1,0:T(8,128)(2,1)}, bf16[784,512]{1,0:T(8,128)(2,1)S(1)}, u32[]{:S(2)}, u32[]{:S(2)}) collective-permute-start(bf16[784,512]{1,0:T(8,128)(2,1)} %collective-permute-done.1.refs_0_), channel_id=1, source_target_pairs={{0,8},{8,0},{16,24},{24,16},{1,9},{9,1},{17,25},{25,17},{2,10},{10... | collective-permute-start | bytes 2408456 | tf_op jit(solution)/shard_map/ppermute | solution.py:58
  52.9 2.3 %collective-permute-start.12 = (bf16[784,512]{1,0:T(8,128)(2,1)S(1)}, bf16[784,512]{1,0:T(8,128)(2,1)S(1)}, u32[]{:S(2)}, u32[]{:S(2)}) collective-permute-start(bf16[784,512]{1,0:T(8,128)(2,1)S(1)} %shard_map.74.refs_2_), channel_id=1, source_target_pairs={{0,2},{2,0},{4,6},{6,4},{1,3},{3,1},{5,7},{7,5},{8,10},{10,8},{12,... | collective-permute-start | bytes 2408456 | tf_op jit(solution)/shard_map/ppermute | solution.py:67
  53.0 21.7 %collective-permute-start.19 = (bf16[784,512]{1,0:T(8,128)(2,1)S(1)}, bf16[784,512]{1,0:T(8,128)(2,1)S(1)}, u32[]{:S(2)}, u32[]{:S(2)}) collective-permute-start(bf16[784,512]{1,0:T(8,128)(2,1)S(1)} %broadcast_select_fusion.1.refs_0_), channel_id=1, source_target_pairs={{0,1},{1,0},{2,3},{3,2},{4,5},{5,4},{6,7},{7,6},{8,9},{9,8},{10,11... | collective-permute-start | bytes 2408456 | tf_op jit(solution)/shard_map/ppermute | solution.py:50
  68.4 7.0 %collective-permute-start.18 = (bf16[784,512]{1,0:T(8,128)(2,1)S(1)}, bf16[784,512]{1,0:T(8,128)(2,1)S(1)}, u32[]{:S(2)}, u32[]{:S(2)}) collective-permute-start(bf16[784,512]{1,0:T(8,128)(2,1)S(1)} %shard_map.79.refs_2_), channel_id=1, source_target_pairs={{0,2},{2,0},{4,6},{6,4},{1,3},{3,1},{5,7},{7,5},{8,10},{10,8},{12,... | collective-permute-start | bytes 2408456 | tf_op jit(solution)/shard_map/ppermute | solution.py:67
  71.5 10.4 %collective-permute-start.16 = (bf16[784,512]{1,0:T(8,128)(2,1)S(1)}, bf16[784,512]{1,0:T(8,128)(2,1)S(1)}, u32[]{:S(2)}, u32[]{:S(2)}) collective-permute-start(bf16[784,512]{1,0:T(8,128)(2,1)S(1)} %broadcast_select_fusion.refs_0_.refs_2_), channel_id=1, source_target_pairs={{0,2},{2,0},{4,6},{6,4},{1,3},{3,1},{5,7},{7,5},{8,10},{10,8},{12,... | collective-permute-start | bytes 2408456 | tf_op jit(solution)/shard_map/ppermute | solution.py:67
  71.7 14.8 %collective-permute-start.20 = (bf16[512,512]{1,0:T(8,128)(2,1)S(1)}, bf16[512,512]{1,0:T(8,128)(2,1)S(1)}, u32[]{:S(2)}, u32[]{:S(2)}) collective-permute-start(bf16[512,512]{1,0:T(8,128)(2,1)S(1)} %slice.89), channel_id=1, source_target_pairs={{0,4},{2,6},{4,0},{6,2},{1,5},{3,7},{5,1},{7,3},{8,12},{10,14},{12... | collective-permute-start | bytes 1572872 | tf_op jit(solution)/shard_map/ppermute | solution.py:54
  73.1 14.8 %collective-permute-start.15 = (bf16[512,512]{1,0:T(8,128)(2,1)S(1)}, bf16[512,512]{1,0:T(8,128)(2,1)S(1)}, u32[]{:S(2)}, u32[]{:S(2)}) collective-permute-start(bf16[512,512]{1,0:T(8,128)(2,1)S(1)} %slice.89), channel_id=1, source_target_pairs={{0,1},{1,0},{2,3},{3,2},{4,5},{5,4},{6,7},{7,6},{8,9},{9,8},{10,11... | collective-permute-start | bytes 1572872 | tf_op jit(solution)/shard_map/ppermute | solution.py:50
  74.6 18.4 %collective-permute-start.22 = (bf16[256,512]{1,0:T(8,128)(2,1)S(1)}, bf16[256,512]{1,0:T(8,128)(2,1)S(1)}, u32[]{:S(2)}, u32[]{:S(2)}) collective-permute-start(bf16[256,512]{1,0:T(8,128)(2,1)S(1)} %slice.88), channel_id=1, source_target_pairs={{0,4},{2,6},{4,0},{6,2},{1,5},{3,7},{5,1},{7,3},{8,12},{10,14},{12... | collective-permute-start | bytes 786440 | tf_op jit(solution)/shard_map/ppermute | solution.py:54
  75.4 17.9 %collective-permute-start.14 = (bf16[256,512]{1,0:T(8,128)(2,1)S(1)}, bf16[256,512]{1,0:T(8,128)(2,1)S(1)}, u32[]{:S(2)}, u32[]{:S(2)}) collective-permute-start(bf16[256,512]{1,0:T(8,128)(2,1)S(1)} %slice.88), channel_id=1, source_target_pairs={{0,1},{1,0},{2,3},{3,2},{4,5},{5,4},{6,7},{7,6},{8,9},{9,8},{10,11... | collective-permute-start | bytes 786440 | tf_op jit(solution)/shard_map/ppermute | solution.py:50
  86.5 1.9 %collective-permute-start.21 = (bf16[512,512]{1,0:T(8,128)(2,1)S(1)}, bf16[512,512]{1,0:T(8,128)(2,1)S(1)}, u32[]{:S(2)}, u32[]{:S(2)}) collective-permute-start(bf16[512,512]{1,0:T(8,128)(2,1)S(1)} %shard_map.84.refs_1_.refs_5_.refs_6_), channel_id=1, source_target_pairs={{0,2},{2,0},{4,6},{6,4},{1,3},{3,1},{5,7},{7,5},{8,10},{10,8},{12,... | collective-permute-start | bytes 1572872 | tf_op jit(solution)/shard_map/ppermute | solution.py:67
  93.1 1.6 %collective-permute-start.23 = (bf16[256,512]{1,0:T(8,128)(2,1)S(1)}, bf16[256,512]{1,0:T(8,128)(2,1)S(1)}, u32[]{:S(2)}, u32[]{:S(2)}) collective-permute-start(bf16[256,512]{1,0:T(8,128)(2,1)S(1)} %shard_map.89.refs_1_.refs_7_), channel_id=1, source_target_pairs={{0,2},{2,0},{4,6},{6,4},{1,3},{3,1},{5,7},{7,5},{8,10},{10,8},{12,... | collective-permute-start | bytes 786440 | tf_op jit(solution)/shard_map/ppermute | solution.py:67
  (2 other events, 7.1 us)

commit v7 on v6

--- a/solution.py
+++ b/solution.py
@@ -219,9 +219,9 @@
 
 
 def mark_kernel(block, rows, marked, sem):
-    part = block.shape[0] // 4
+    part = block.shape[0] // 8
     copies = []
-    for n in range(4):
+    for n in range(8):
         at = pl.ds(n * part, part)
         copies.append(pltpu.make_async_copy(block.at[at, :], marked.at[at, :], sem.at[n]))
     for copy in copies:
@@ -239,7 +239,7 @@
         out_shape=pltpu.VMEM(shape, block.dtype),
         in_specs=[pl.BlockSpec(memory_space=pltpu.HBM), near],
         out_specs=near,
-        scratch_shapes=[pltpu.SemaphoreType.DMA((4,))],
+        scratch_shapes=[pltpu.SemaphoreType.DMA((8,))],
         compiler_params=pltpu.CompilerParams(vmem_limit_bytes=4 * 1024 * 1024),
     )(block, rows)
 

time: 99.3 us -> 99.3 us (level)
  no operation moved by 1% of the time
where the time goes in v7:
time: 99.3 us; the launch traced here: 98.7 us
  waiting for transfers between devices  36.4 us (37%)
  Pallas kernels  33 us (33%)
  starting transfers between devices  24.4 us (25%)
  other arithmetic  3.57 us (4%)
  between operations  1.13 us (1%)
    ppermute x5, waiting for transfers between devices, along_line(): return lambda value: lax.ppermute(value, 'freq', hops)  22.2 us
    pallas_call x3, Pallas kernels, add_slot(): pl.pallas_call(functools.partial(slot_kernel, acc is None), out_shape=plt...  19.2 us
    pallas_call x3, Pallas kernels, finish(): pl.pallas_call(functools.partial(finish_kernel, *where, fresh, jobs, n_in...  12.5 us
    ppermute x5, starting transfers between devices, along_line(): return lambda value: lax.ppermute(value, 'freq', hops)  12.1 us
    ppermute x5, waiting for transfers between devices, across_row(): return lax.ppermute(value, 'row', [(i, (i + 2) % 4) for i in range(4)])  8.36 us
    ppermute x5, starting transfers between devices, across_col(): return lax.ppermute(value, 'col', [(0, 1), (1, 0)])  6.64 us
    ppermute x5, starting transfers between devices, across_row(): return lax.ppermute(value, 'row', [(i, (i + 2) % 4) for i in range(4)])  4.82 us
    ppermute x5, waiting for transfers between devices, across_col(): return lax.ppermute(value, 'col', [(0, 1), (1, 0)])  3.28 us
  transfers between devices with their start and end apart: 24, of which 12 were waited for; matrix products, arithmetic and copies ran while one was open for 2% of the time, Pallas kernels for 28%

profile of v7, /device:TPU:0, one launch (start us, length us, event | category | flops | bytes accessed | tf_op | source)
XLA Modules:
  0.0 98.7 jit_solution(9780428255893050271)
XLA Ops:
  2.1 1.3 %shard_map.64.refs_0_ = bf16[784,512]{1,0:T(8,128)(2,1)S(1)} custom-call(bf16[768,512]{1,0:T(8,128)(2,1)} %block.1, bf16[16,512]{1,0:T(8,128)(2,1)S(1)} %fusion.4.rows), custom_call_target="tpu_custom_call" | custom-call | tf_op jit(solution)/shard_map/pallas_call | solution.py:237
  3.4 3.1 %collective-permute-start = (bf16[784,512]{1,0:T(8,128)(2,1)S(1)}, bf16[784,512]{1,0:T(8,128)(2,1)S(1)}, u32[]{:S(2)}, u32[]{:S(2)}) collective-permute-start(bf16[784,512]{1,0:T(8,128)(2,1)S(1)} %shard_map.64.refs_0_), channel_id=1, source_target_pairs={{0,8},{8,0},{16,24},{24,16},{1,9},{9,1},{17,25},{25,17},{2,10},{10... | collective-permute-start | bytes 2408456 | tf_op jit(solution)/shard_map/ppermute | solution.py:58
  6.5 1.5 %collective-permute-start.5 = (bf16[768,512]{1,0:T(8,128)(2,1)}, bf16[768,512]{1,0:T(8,128)(2,1)}, u32[]{:S(2)}, u32[]{:S(2)}) collective-permute-start(bf16[768,512]{1,0:T(8,128)(2,1)} %block.1), channel_id=1, source_target_pairs={{0,4},{2,6},{4,0},{6,2},{1,5},{3,7},{5,1},{7,3},{8,12},{10,14},{12... | collective-permute-start | bytes 2359304 | tf_op jit(solution)/shard_map/ppermute | solution.py:54
  8.7 1.6 %collective-permute-start.4 = (bf16[768,512]{1,0:T(8,128)(2,1)}, bf16[768,512]{1,0:T(8,128)(2,1)}, u32[]{:S(2)}, u32[]{:S(2)}) collective-permute-start(bf16[768,512]{1,0:T(8,128)(2,1)} %block.1), channel_id=1, source_target_pairs={{0,1},{1,0},{2,3},{3,2},{4,5},{5,4},{6,7},{7,6},{8,9},{9,8},{10,11... | collective-permute-start | bytes 2359304 | tf_op jit(solution)/shard_map/ppermute | solution.py:50
  10.3 14.1 %collective-permute-done.refs_0_ = bf16[784,512]{1,0:T(8,128)(2,1)S(1)} collective-permute-done((bf16[784,512]{1,0:T(8,128)(2,1)S(1)}, bf16[784,512]{1,0:T(8,128)(2,1)S(1)}, u32[]{:S(2)}, u32[]{:S(2)}) %collective-permute-start) | collective-permute-done | bytes 802848 | tf_op jit(solution)/shard_map/ppermute | solution.py:58
  25.9 1.9 %collective-permute-done.4.refs_0_.refs_4_ = bf16[768,512]{1,0:T(8,128)(2,1)} collective-permute-done((bf16[768,512]{1,0:T(8,128)(2,1)}, bf16[768,512]{1,0:T(8,128)(2,1)}, u32[]{:S(2)}, u32[]{:S(2)}) %collective-permute-start.4) | collective-permute-done | bytes 786464 | tf_op jit(solution)/shard_map/ppermute | solution.py:50
  27.8 4.1 %collective-permute-start.9 = (bf16[784,512]{1,0:T(8,128)(2,1)S(1)}, bf16[784,512]{1,0:T(8,128)(2,1)}, u32[]{:S(2)}, u32[]{:S(2)}) collective-permute-start(bf16[784,512]{1,0:T(8,128)(2,1)S(1)} %shard_map.66.refs_0_.refs_1_), channel_id=1, source_target_pairs={{0,8},{8,0},{16,24},{24,16},{1,9},{9,1},{17,25},{25,17},{2,10},{10... | collective-permute-start | bytes 2408456 | tf_op jit(solution)/shard_map/ppermute | solution.py:58
  32.0 1.5 %collective-permute-start.1 = (bf16[784,512]{1,0:T(8,128)(2,1)S(1)}, bf16[784,512]{1,0:T(8,128)(2,1)}, u32[]{:S(2)}, u32[]{:S(2)}) collective-permute-start(bf16[784,512]{1,0:T(8,128)(2,1)S(1)} %collective-permute-done.refs_0_), channel_id=1, source_target_pairs={{0,0},{8,16},{16,8},{24,24},{1,1},{9,17},{17,9},{25,25},{2,2},{10,... | collective-permute-start | bytes 2408456 | tf_op jit(solution)/shard_map/ppermute | solution.py:58
  34.2 1.5 %collective-permute-start.13 = (bf16[784,512]{1,0:T(8,128)(2,1)S(1)}, bf16[784,512]{1,0:T(8,128)(2,1)S(1)}, u32[]{:S(2)}, u32[]{:S(2)}) collective-permute-start(bf16[784,512]{1,0:T(8,128)(2,1)S(1)} %broadcast_select_fusion.2.refs_0_), channel_id=1, source_target_pairs={{0,1},{1,0},{2,3},{3,2},{4,5},{5,4},{6,7},{7,6},{8,9},{9,8},{10,11... | collective-permute-start | bytes 2408456 | tf_op jit(solution)/shard_map/ppermute | solution.py:50
  35.7 7.4 %shard_map.71.refs_0_.refs_5_ = f32[2,4,768,768]{3,2,1,0:T(8,128)S(1)} custom-call(f32[8,128]{1,0:T(8,128)S(1)} %shard_map.70.token.refs_15_, f32[1,512]{1,0:T(1,128)S(1)} %add_divide_fusion.3.weight, bf16[784,512]{1,0:T(8,128)(2,1)S(1)} %shard_map.64.refs_0_, bf16[768,512]{1,0:T(8,128)(2,1)} %collective-permute-done.7.refs_1_, ...), custom_call_target="tpu_custom_call" | custom-call | flops 57982058496 | tf_op jit(solution)/shard_map/pallas_call | solution.py:131
  43.1 5.1 %collective-permute-done.9 = bf16[784,512]{1,0:T(8,128)(2,1)} collective-permute-done((bf16[784,512]{1,0:T(8,128)(2,1)S(1)}, bf16[784,512]{1,0:T(8,128)(2,1)}, u32[]{:S(2)}, u32[]{:S(2)}) %collective-permute-start.9) | collective-permute-done | bytes 802848 | tf_op jit(solution)/shard_map/ppermute | solution.py:58
  50.0 2.7 %collective-permute-start.2 = (bf16[784,512]{1,0:T(8,128)(2,1)}, bf16[784,512]{1,0:T(8,128)(2,1)S(1)}, u32[]{:S(2)}, u32[]{:S(2)}) collective-permute-start(bf16[784,512]{1,0:T(8,128)(2,1)} %collective-permute-done.1.refs_0_), channel_id=1, source_target_pairs={{0,8},{8,0},{16,24},{24,16},{1,9},{9,1},{17,25},{25,17},{2,10},{10... | collective-permute-start | bytes 2408456 | tf_op jit(solution)/shard_map/ppermute | solution.py:58
  53.0 1.6 %collective-permute-start.19 = (bf16[784,512]{1,0:T(8,128)(2,1)S(1)}, bf16[784,512]{1,0:T(8,128)(2,1)S(1)}, u32[]{:S(2)}, u32[]{:S(2)}) collective-permute-start(bf16[784,512]{1,0:T(8,128)(2,1)S(1)} %broadcast_select_fusion.1.refs_0_), channel_id=1, source_target_pairs={{0,1},{1,0},{2,3},{3,2},{4,5},{5,4},{6,7},{7,6},{8,9},{9,8},{10,11... | collective-permute-start | bytes 2408456 | tf_op jit(solution)/shard_map/ppermute | solution.py:50
  55.2 5.8 %shard_map.75.refs_0_.refs_5_ = f32[2,4,768,768]{3,2,1,0:T(8,128)S(1)} custom-call(f32[8,128]{1,0:T(8,128)S(1)} %shard_map.73.token.refs_18_, f32[1,512]{1,0:T(1,128)S(1)} %add_divide_fusion.2.weight, bf16[784,512]{1,0:T(8,128)(2,1)S(1)} %broadcast_select_fusion.2.refs_0_, ...), custom_call_target="tpu_custom_call", output_to_operand_aliasing={{}: (7, {})} | custom-call | flops 4831838208 | tf_op jit(solution)/shard_map/pallas_call | solution.py:131
  61.1 7.4 %collective-permute-done.17.value = bf16[784,512]{1,0:T(8,128)(2,1)S(1)} collective-permute-done((bf16[784,512]{1,0:T(8,128)(2,1)S(1)}, bf16[784,512]{1,0:T(8,128)(2,1)S(1)}, u32[]{:S(2)}, u32[]{:S(2)}) %collective-permute-start.17) | collective-permute-done | bytes 802848 | tf_op jit(solution)/shard_map/ppermute | solution.py:54
  68.5 3.0 %collective-permute-done.2.refs_0_ = bf16[784,512]{1,0:T(8,128)(2,1)S(1)} collective-permute-done((bf16[784,512]{1,0:T(8,128)(2,1)}, bf16[784,512]{1,0:T(8,128)(2,1)S(1)}, u32[]{:S(2)}, u32[]{:S(2)}) %collective-permute-start.2) | collective-permute-done | bytes 802848 | tf_op jit(solution)/shard_map/ppermute | solution.py:58
  71.7 1.4 %collective-permute-start.20 = (bf16[512,512]{1,0:T(8,128)(2,1)S(1)}, bf16[512,512]{1,0:T(8,128)(2,1)S(1)}, u32[]{:S(2)}, u32[]{:S(2)}) collective-permute-start(bf16[512,512]{1,0:T(8,128)(2,1)S(1)} %slice.89), channel_id=1, source_target_pairs={{0,4},{2,6},{4,0},{6,2},{1,5},{3,7},{5,1},{7,3},{8,12},{10,14},{12... | collective-permute-start | bytes 1572872 | tf_op jit(solution)/shard_map/ppermute | solution.py:54
  73.1 1.5 %collective-permute-start.15 = (bf16[512,512]{1,0:T(8,128)(2,1)S(1)}, bf16[512,512]{1,0:T(8,128)(2,1)S(1)}, u32[]{:S(2)}, u32[]{:S(2)}) collective-permute-start(bf16[512,512]{1,0:T(8,128)(2,1)S(1)} %slice.89), channel_id=1, source_target_pairs={{0,1},{1,0},{2,3},{3,2},{4,5},{5,4},{6,7},{7,6},{8,9},{9,8},{10,11... | collective-permute-start | bytes 1572872 | tf_op jit(solution)/shard_map/ppermute | solution.py:50
  76.0 5.9 %shard_map.80.refs_4_.refs_0_ = f32[2,4,768,768]{3,2,1,0:T(8,128)S(1)} custom-call(f32[8,128]{1,0:T(8,128)S(1)} %shard_map.78.token.refs_21_, f32[1,512]{1,0:T(1,128)S(1)} %add_divide_fusion.weight, bf16[784,512]{1,0:T(8,128)(2,1)S(1)} %broadcast_select_fusion.1.refs_0_, ...), custom_call_target="tpu_custom_call", output_to_operand_aliasing={{}: (7, {})} | custom-call | flops 4831838208 | tf_op jit(solution)/shard_map/pallas_call | solution.py:131
  81.9 4.0 %shard_map.81 = (f32[2,4,768,768]{3,2,1,0:T(8,128)S(1)}, f32[4,768,1536]{2,1,0:T(8,128)}, bf16[2,768,512]{2,1,0:T(8,128)(2,1)S(1)}) custom-call(s32[5]{0:T(128)S(1)} %stack.30.refs_0_, f32[1,512]{1,0:T(1,128)S(1)} %add_divide_fusion.1.refs_1_, bf16[784,512]{1,0:T(8,128)(2,1)S(1)} %broadcast_select_fusion.refs_0_.refs_2_, ...), custom_call_target="tpu_custom_call", output_to_operand_aliasing={{0}: (4, {})} | custom-call | flops 1207959552 | bytes 4718592 | tf_op jit(solution)/shard_map/pallas_call | solution.py:203
  86.5 1.4 %collective-permute-done.15.value = bf16[512,512]{1,0:T(8,128)(2,1)S(1)} collective-permute-done((bf16[512,512]{1,0:T(8,128)(2,1)S(1)}, bf16[512,512]{1,0:T(8,128)(2,1)S(1)}, u32[]{:S(2)}, u32[]{:S(2)}) %collective-permute-start.15) | collective-permute-done | bytes 524320 | tf_op jit(solution)/shard_map/ppermute | solution.py:50
  88.4 4.6 %shard_map.86 = (f32[2,4,768,768]{3,2,1,0:T(8,128)S(1)}, f32[4,768,1536]{2,1,0:T(8,128)}, bf16[2,768,512]{2,1,0:T(8,128)(2,1)S(1)}) custom-call(s32[5]{0:T(128)S(1)} %stack.30.refs_0_, f32[1,512]{1,0:T(1,128)S(1)} %add_divide_fusion.1.refs_1_, ...), custom_call_target="tpu_custom_call", output_to_operand_aliasing={{0}: (7, {}), {1}: (8, {}), {2}: (9, {})} | custom-call | flops 2147483648 | bytes 8388608 | tf_op jit(solution)/shard_map/pallas_call | solution.py:203
  93.3 1.4 %collective-permute-done.23.refs_4_ = bf16[256,512]{1,0:T(8,128)(2,1)S(1)} collective-permute-done((bf16[256,512]{1,0:T(8,128)(2,1)S(1)}, bf16[256,512]{1,0:T(8,128)(2,1)S(1)}, u32[]{:S(2)}, u32[]{:S(2)}) %collective-permute-start.23) | collective-permute-done | bytes 262176 | tf_op jit(solution)/shard_map/ppermute | solution.py:67
  94.7 3.9 %shard_map.92 = (f32[2,4,768,768]{3,2,1,0:T(8,128)S(1)}, f32[4,768,1536]{2,1,0:T(8,128)}, bf16[2,768,512]{2,1,0:T(8,128)(2,1)S(1)}) custom-call(s32[5]{0:T(128)S(1)} %stack.30.refs_0_, f32[1,512]{1,0:T(1,128)S(1)} %add_divide_fusion.1.refs_1_, ...), custom_call_target="tpu_custom_call", output_to_operand_aliasing={{0}: (9, {}), {1}: (10, {}), {2}: (11, {})} | custom-call | flops 1476395008 | bytes 5767168 | tf_op jit(solution)/shard_map/pallas_call | solution.py:203
  (76 shorter events, 9.9 us)
Async XLA Ops:
  3.4 21.0 %collective-permute-start = (bf16[784,512]{1,0:T(8,128)(2,1)S(1)}, bf16[784,512]{1,0:T(8,128)(2,1)S(1)}, u32[]{:S(2)}, u32[]{:S(2)}) collective-permute-start(bf16[784,512]{1,0:T(8,128)(2,1)S(1)} %shard_map.64.refs_0_), channel_id=1, source_target_pairs={{0,8},{8,0},{16,24},{24,16},{1,9},{9,1},{17,25},{25,17},{2,10},{10... | collective-permute-start | bytes 2408456 | tf_op jit(solution)/shard_map/ppermute | solution.py:58
  6.5 19.3 %collective-permute-start.5 = (bf16[768,512]{1,0:T(8,128)(2,1)}, bf16[768,512]{1,0:T(8,128)(2,1)}, u32[]{:S(2)}, u32[]{:S(2)}) collective-permute-start(bf16[768,512]{1,0:T(8,128)(2,1)} %block.1), channel_id=1, source_target_pairs={{0,4},{2,6},{4,0},{6,2},{1,5},{3,7},{5,1},{7,3},{8,12},{10,14},{12... | collective-permute-start | bytes 2359304 | tf_op jit(solution)/shard_map/ppermute | solution.py:54
  8.0 19.8 %collective-permute-start.3 = (bf16[784,512]{1,0:T(8,128)(2,1)S(1)}, bf16[784,512]{1,0:T(8,128)(2,1)S(1)}, u32[]{:S(2)}, u32[]{:S(2)}) collective-permute-start(bf16[784,512]{1,0:T(8,128)(2,1)S(1)} %shard_map.64.refs_0_), channel_id=1, source_target_pairs={{0,0},{8,16},{16,8},{24,24},{1,1},{9,17},{17,9},{25,25},{2,2},{10,... | collective-permute-start | bytes 2408456 | tf_op jit(solution)/shard_map/ppermute | solution.py:58
  8.7 19.1 %collective-permute-start.4 = (bf16[768,512]{1,0:T(8,128)(2,1)}, bf16[768,512]{1,0:T(8,128)(2,1)}, u32[]{:S(2)}, u32[]{:S(2)}) collective-permute-start(bf16[768,512]{1,0:T(8,128)(2,1)} %block.1), channel_id=1, source_target_pairs={{0,1},{1,0},{2,3},{3,2},{4,5},{5,4},{6,7},{7,6},{8,9},{9,8},{10,11... | collective-permute-start | bytes 2359304 | tf_op jit(solution)/shard_map/ppermute | solution.py:50
  24.4 9.1 %collective-permute-start.6 = (bf16[784,512]{1,0:T(8,128)(2,1)S(1)}, bf16[784,512]{1,0:T(8,128)(2,1)S(1)}, u32[]{:S(2)}, u32[]{:S(2)}) collective-permute-start(bf16[784,512]{1,0:T(8,128)(2,1)S(1)} %collective-permute-done.refs_0_), channel_id=1, source_target_pairs={{0,2},{2,0},{4,6},{6,4},{1,3},{3,1},{5,7},{7,5},{8,10},{10,8},{12,... | collective-permute-start | bytes 2408456 | tf_op jit(solution)/shard_map/ppermute | solution.py:67
  24.4 9.8 %collective-permute-start.7 = (bf16[768,512]{1,0:T(8,128)(2,1)}, bf16[768,512]{1,0:T(8,128)(2,1)}, u32[]{:S(2)}, u32[]{:S(2)}) collective-permute-start(bf16[768,512]{1,0:T(8,128)(2,1)} %block.1), channel_id=1, source_target_pairs={{0,2},{2,0},{4,6},{6,4},{1,3},{3,1},{5,7},{7,5},{8,10},{10,8},{12,... | collective-permute-start | bytes 2359304 | tf_op jit(solution)/shard_map/ppermute | solution.py:67
  25.8 9.9 %collective-permute-start.8 = (bf16[768,512]{1,0:T(8,128)(2,1)}, bf16[768,512]{1,0:T(8,128)(2,1)}, u32[]{:S(2)}, u32[]{:S(2)}) collective-permute-start(bf16[768,512]{1,0:T(8,128)(2,1)} %collective-permute-done.5.refs_1_.refs_2_), channel_id=1, source_target_pairs={{0,2},{2,0},{4,6},{6,4},{1,3},{3,1},{5,7},{7,5},{8,10},{10,8},{12,... | collective-permute-start | bytes 2359304 | tf_op jit(solution)/shard_map/ppermute | solution.py:67
  27.8 20.4 %collective-permute-start.9 = (bf16[784,512]{1,0:T(8,128)(2,1)S(1)}, bf16[784,512]{1,0:T(8,128)(2,1)}, u32[]{:S(2)}, u32[]{:S(2)}) collective-permute-start(bf16[784,512]{1,0:T(8,128)(2,1)S(1)} %shard_map.66.refs_0_.refs_1_), channel_id=1, source_target_pairs={{0,8},{8,0},{16,24},{24,16},{1,9},{9,1},{17,25},{25,17},{2,10},{10... | collective-permute-start | bytes 2408456 | tf_op jit(solution)/shard_map/ppermute | solution.py:58
  32.0 11.1 %collective-permute-start.1 = (bf16[784,512]{1,0:T(8,128)(2,1)S(1)}, bf16[784,512]{1,0:T(8,128)(2,1)}, u32[]{:S(2)}, u32[]{:S(2)}) collective-permute-start(bf16[784,512]{1,0:T(8,128)(2,1)S(1)} %collective-permute-done.refs_0_), channel_id=1, source_target_pairs={{0,0},{8,16},{16,8},{24,24},{1,1},{9,17},{17,9},{25,25},{2,2},{10,... | collective-permute-start | bytes 2408456 | tf_op jit(solution)/shard_map/ppermute | solution.py:58
  33.6 19.3 %collective-permute-start.11 = (bf16[784,512]{1,0:T(8,128)(2,1)S(1)}, bf16[784,512]{1,0:T(8,128)(2,1)S(1)}, u32[]{:S(2)}, u32[]{:S(2)}) collective-permute-start(bf16[784,512]{1,0:T(8,128)(2,1)S(1)} %broadcast_select_fusion.2.refs_0_), channel_id=1, source_target_pairs={{0,4},{2,6},{4,0},{6,2},{1,5},{3,7},{5,1},{7,3},{8,12},{10,14},{12... | collective-permute-start | bytes 2408456 | tf_op jit(solution)/shard_map/ppermute | solution.py:54
  34.2 18.8 %collective-permute-start.13 = (bf16[784,512]{1,0:T(8,128)(2,1)S(1)}, bf16[784,512]{1,0:T(8,128)(2,1)S(1)}, u32[]{:S(2)}, u32[]{:S(2)}) collective-permute-start(bf16[784,512]{1,0:T(8,128)(2,1)S(1)} %broadcast_select_fusion.2.refs_0_), channel_id=1, source_target_pairs={{0,1},{1,0},{2,3},{3,2},{4,5},{5,4},{6,7},{7,6},{8,9},{9,8},{10,11... | collective-permute-start | bytes 2408456 | tf_op jit(solution)/shard_map/ppermute | solution.py:50
  49.4 19.0 %collective-permute-start.17 = (bf16[784,512]{1,0:T(8,128)(2,1)S(1)}, bf16[784,512]{1,0:T(8,128)(2,1)S(1)}, u32[]{:S(2)}, u32[]{:S(2)}) collective-permute-start(bf16[784,512]{1,0:T(8,128)(2,1)S(1)} %broadcast_select_fusion.1.refs_0_), channel_id=1, source_target_pairs={{0,4},{2,6},{4,0},{6,2},{1,5},{3,7},{5,1},{7,3},{8,12},{10,14},{12... | collective-permute-start | bytes 2408456 | tf_op jit(solution)/shard_map/ppermute | solution.py:54
  50.0 18.5 %collective-permute-start.10 = (bf16[784,512]{1,0:T(8,128)(2,1)S(1)}, bf16[784,512]{1,0:T(8,128)(2,1)S(1)}, u32[]{:S(2)}, u32[]{:S(2)}) collective-permute-start(bf16[784,512]{1,0:T(8,128)(2,1)S(1)} %broadcast_select_fusion.1.refs_0_), channel_id=1, source_target_pairs={{0,2},{2,0},{4,6},{6,4},{1,3},{3,1},{5,7},{7,5},{8,10},{10,8},{12,... | collective-permute-start | bytes 2408456 | tf_op jit(solution)/shard_map/ppermute | solution.py:67
  50.0 21.5 %collective-permute-start.2 = (bf16[784,512]{1,0:T(8,128)(2,1)}, bf16[784,512]{1,0:T(8,128)(2,1)S(1)}, u32[]{:S(2)}, u32[]{:S(2)}) collective-permute-start(bf16[784,512]{1,0:T(8,128)(2,1)} %collective-permute-done.1.refs_0_), channel_id=1, source_target_pairs={{0,8},{8,0},{16,24},{24,16},{1,9},{9,1},{17,25},{25,17},{2,10},{10... | collective-permute-start | bytes 2408456 | tf_op jit(solution)/shard_map/ppermute | solution.py:58
  52.9 2.3 %collective-permute-start.12 = (bf16[784,512]{1,0:T(8,128)(2,1)S(1)}, bf16[784,512]{1,0:T(8,128)(2,1)S(1)}, u32[]{:S(2)}, u32[]{:S(2)}) collective-permute-start(bf16[784,512]{1,0:T(8,128)(2,1)S(1)} %shard_map.74.refs_2_), channel_id=1, source_target_pairs={{0,2},{2,0},{4,6},{6,4},{1,3},{3,1},{5,7},{7,5},{8,10},{10,8},{12,... | collective-permute-start | bytes 2408456 | tf_op jit(solution)/shard_map/ppermute | solution.py:67
  53.0 21.7 %collective-permute-start.19 = (bf16[784,512]{1,0:T(8,128)(2,1)S(1)}, bf16[784,512]{1,0:T(8,128)(2,1)S(1)}, u32[]{:S(2)}, u32[]{:S(2)}) collective-permute-start(bf16[784,512]{1,0:T(8,128)(2,1)S(1)} %broadcast_select_fusion.1.refs_0_), channel_id=1, source_target_pairs={{0,1},{1,0},{2,3},{3,2},{4,5},{5,4},{6,7},{7,6},{8,9},{9,8},{10,11... | collective-permute-start | bytes 2408456 | tf_op jit(solution)/shard_map/ppermute | solution.py:50
  68.4 7.0 %collective-permute-start.18 = (bf16[784,512]{1,0:T(8,128)(2,1)S(1)}, bf16[784,512]{1,0:T(8,128)(2,1)S(1)}, u32[]{:S(2)}, u32[]{:S(2)}) collective-permute-start(bf16[784,512]{1,0:T(8,128)(2,1)S(1)} %shard_map.79.refs_2_), channel_id=1, source_target_pairs={{0,2},{2,0},{4,6},{6,4},{1,3},{3,1},{5,7},{7,5},{8,10},{10,8},{12,... | collective-permute-start | bytes 2408456 | tf_op jit(solution)/shard_map/ppermute | solution.py:67
  71.6 10.4 %collective-permute-start.16 = (bf16[784,512]{1,0:T(8,128)(2,1)S(1)}, bf16[784,512]{1,0:T(8,128)(2,1)S(1)}, u32[]{:S(2)}, u32[]{:S(2)}) collective-permute-start(bf16[784,512]{1,0:T(8,128)(2,1)S(1)} %broadcast_select_fusion.refs_0_.refs_2_), channel_id=1, source_target_pairs={{0,2},{2,0},{4,6},{6,4},{1,3},{3,1},{5,7},{7,5},{8,10},{10,8},{12,... | collective-permute-start | bytes 2408456 | tf_op jit(solution)/shard_map/ppermute | solution.py:67
  71.7 14.8 %collective-permute-start.20 = (bf16[512,512]{1,0:T(8,128)(2,1)S(1)}, bf16[512,512]{1,0:T(8,128)(2,1)S(1)}, u32[]{:S(2)}, u32[]{:S(2)}) collective-permute-start(bf16[512,512]{1,0:T(8,128)(2,1)S(1)} %slice.89), channel_id=1, source_target_pairs={{0,4},{2,6},{4,0},{6,2},{1,5},{3,7},{5,1},{7,3},{8,12},{10,14},{12... | collective-permute-start | bytes 1572872 | tf_op jit(solution)/shard_map/ppermute | solution.py:54
  73.1 14.8 %collective-permute-start.15 = (bf16[512,512]{1,0:T(8,128)(2,1)S(1)}, bf16[512,512]{1,0:T(8,128)(2,1)S(1)}, u32[]{:S(2)}, u32[]{:S(2)}) collective-permute-start(bf16[512,512]{1,0:T(8,128)(2,1)S(1)} %slice.89), channel_id=1, source_target_pairs={{0,1},{1,0},{2,3},{3,2},{4,5},{5,4},{6,7},{7,6},{8,9},{9,8},{10,11... | collective-permute-start | bytes 1572872 | tf_op jit(solution)/shard_map/ppermute | solution.py:50
  74.7 18.4 %collective-permute-start.22 = (bf16[256,512]{1,0:T(8,128)(2,1)S(1)}, bf16[256,512]{1,0:T(8,128)(2,1)S(1)}, u32[]{:S(2)}, u32[]{:S(2)}) collective-permute-start(bf16[256,512]{1,0:T(8,128)(2,1)S(1)} %slice.88), channel_id=1, source_target_pairs={{0,4},{2,6},{4,0},{6,2},{1,5},{3,7},{5,1},{7,3},{8,12},{10,14},{12... | collective-permute-start | bytes 786440 | tf_op jit(solution)/shard_map/ppermute | solution.py:54
  75.4 17.9 %collective-permute-start.14 = (bf16[256,512]{1,0:T(8,128)(2,1)S(1)}, bf16[256,512]{1,0:T(8,128)(2,1)S(1)}, u32[]{:S(2)}, u32[]{:S(2)}) collective-permute-start(bf16[256,512]{1,0:T(8,128)(2,1)S(1)} %slice.88), channel_id=1, source_target_pairs={{0,1},{1,0},{2,3},{3,2},{4,5},{5,4},{6,7},{7,6},{8,9},{9,8},{10,11... | collective-permute-start | bytes 786440 | tf_op jit(solution)/shard_map/ppermute | solution.py:50
  86.5 1.9 %collective-permute-start.21 = (bf16[512,512]{1,0:T(8,128)(2,1)S(1)}, bf16[512,512]{1,0:T(8,128)(2,1)S(1)}, u32[]{:S(2)}, u32[]{:S(2)}) collective-permute-start(bf16[512,512]{1,0:T(8,128)(2,1)S(1)} %shard_map.84.refs_1_.refs_5_.refs_6_), channel_id=1, source_target_pairs={{0,2},{2,0},{4,6},{6,4},{1,3},{3,1},{5,7},{7,5},{8,10},{10,8},{12,... | collective-permute-start | bytes 1572872 | tf_op jit(solution)/shard_map/ppermute | solution.py:67
  93.1 1.6 %collective-permute-start.23 = (bf16[256,512]{1,0:T(8,128)(2,1)S(1)}, bf16[256,512]{1,0:T(8,128)(2,1)S(1)}, u32[]{:S(2)}, u32[]{:S(2)}) collective-permute-start(bf16[256,512]{1,0:T(8,128)(2,1)S(1)} %shard_map.89.refs_1_.refs_7_), channel_id=1, source_target_pairs={{0,2},{2,0},{4,6},{6,4},{1,3},{3,1},{5,7},{7,5},{8,10},{10,8},{12,... | collective-permute-start | bytes 786440 | tf_op jit(solution)/shard_map/ppermute | solution.py:67
  (2 other events, 7.1 us)
